TPU v7x, 256 devices: a whole 4x4x8 slice. The times are simulated.
256 devices in a mesh: gx: 16 (over y, z_hi), gz: 16 (over x, z_lo, core).
Axes of the slice: x: 4, y: 4, z: 8 (z_hi: 4, z_lo: 2; z = z_hi * 2 + z_lo), core: 2. Of those that a mesh axis runs over, the one named last changes fastest.
Arguments:
- stored: bfloat16 [19, 256, 128, 256], P(None, 'gx', 'gz'), may hold values from 0 to 1, as said below
- adjoint_in: float32 [19, 256, 128, 256], P(None, 'gx', 'gz'), may hold values from -6 to 6
- marker_cell: int32 [524288], P(('gx', 'gz')), may hold values from 0 to 32767, as said below
- marker_weight: float32 [9, 524288], P(None, ('gx', 'gz')), may hold values from 0 to 1
- marker_panel: int32 [524288], P(('gx', 'gz')), may hold values from 0 to 127
- marker_count: int32 [256], P(('gx', 'gz')), may hold values from 256 to 2048, as said below
Outputs:
- adjoint_out: float32 [19, 256, 128, 256], P(None, 'gx', 'gz')
- marker_grad: float32 [3, 524288], P(None, ('gx', 'gz'))
- panel_grad: float32 [3, 128], replicated
Inputs may be any that keep to these rules, and one draw needn't show every extreme that they name: marker_cell is an index within the owner tile; the base cell never lies on the grid's first or last streamwise or vertical layer. `marker_count`: some tile has all 2048 slots live in every draw. stored populations are positive.
All inputs are finite; a program needn't handle non-finite values.
Results may differ from a plain program's by a relative error of at most 0.0003.
Values sent between devices are 32-bit elements; how exact they have to be, the bound alone decides.
No kernel may reach another device: no remote copies, remote signals or barrier semaphores. Data moves between devices by JAX's collectives and lax.ppermute only.
A program may use at most 128 MiB of HBM per device.

v0:
```python
import jax
import jax.numpy as jnp
import numpy as np
from jax import lax
from jax.sharding import PartitionSpec as P

PANELS = 128


STENCIL = [
    (0, 0, 0),
    (1, 0, 0),
    (-1, 0, 0),
    (0, 1, 0),
    (0, -1, 0),
    (0, 0, 1),
    (0, 0, -1),
    (1, 1, 0),
    (-1, 1, 0),
    (1, -1, 0),
    (-1, -1, 0),
    (1, 0, 1),
    (-1, 0, 1),
    (1, 0, -1),
    (-1, 0, -1),
    (0, 1, 1),
    (0, -1, 1),
    (0, 1, -1),
    (0, -1, -1),
]
LATTICE_WEIGHTS = [1.0 / 3.0] + [1.0 / 18.0] * 6 + [1.0 / 36.0] * 12
RELAXATION = 1.6


def with_halo(cells, sides, width):
    for axis, dim in sides:
        count = lax.axis_size(axis)
        ends = count - 1
        head = lax.slice_in_dim(cells, 0, width, axis=dim)
        tail = lax.slice_in_dim(cells, cells.shape[dim] - width, cells.shape[dim], axis=dim)
        cells = jnp.concatenate(
            [
                lax.ppermute(tail, axis, [(i, (i + 1) % count) for i in range(ends)]),
                cells,
                lax.ppermute(head, axis, [((i + 1) % count, i) for i in range(ends)]),
            ],
            axis=dim,
        )
    return cells


def signed_sum(pieces, factors):
    result = None
    for piece, factor in zip(pieces, factors):
        if factor == 0:
            continue
        term = piece * factor
        result = term if result is None else result + term
    return result


def collide_list(pops):
    density = pops[0]
    for piece in pops[1:]:
        density = density + piece
    velocity = []
    for comp in range(3):
        velocity.append(signed_sum(pops, [float(entry[comp]) for entry in STENCIL]) / density)
    speed = velocity[0] * velocity[0] + velocity[1] * velocity[1] + velocity[2] * velocity[2]
    result = []
    for popid in range(19):
        along = signed_sum(velocity, [float(entry) for entry in STENCIL[popid]])
        if along is None:
            along = jnp.zeros_like(density)
        equilibrium = (
            LATTICE_WEIGHTS[popid]
            * density
            * (1.0 + 3.0 * along + 4.5 * along * along - 1.5 * speed)
        )
        result.append(pops[popid] - RELAXATION * (pops[popid] - equilibrium))
    return result


def sense(density, pulled):
    parts = []
    for comp in range(3):
        parts.append(
            3.0
            * density
            * signed_sum(
                pulled,
                [LATTICE_WEIGHTS[popid] * float(STENCIL[popid][comp]) for popid in range(19)],
            )
        )
    return jnp.stack(parts)


def transpose_collision(stored, pulled):
    pops = [stored[popid].astype(jnp.float32) for popid in range(19)]
    unused, backward = jax.vjp(collide_list, pops)
    result = backward(pulled)[0]
    density = pops[0]
    for piece in pops[1:]:
        density = density + piece
    return (jnp.stack(result), density)


def pull(extended, width, border, extent_x, extent_z):
    pieces = []
    for popid in range(19):
        step_x, step_y, step_z = STENCIL[popid]
        low_x = width - border + step_x
        low_z = width - border + step_z
        piece = extended[
            popid, low_x : low_x + extent_x + 2 * border, low_z : low_z + extent_z + 2 * border, :
        ]
        if step_y != 0:
            piece = jnp.roll(piece, -step_y, axis=-1)
        pieces.append(piece)
    return pieces


def local(stored, adjoint_in, marker_cell, marker_weight, marker_panel, marker_count):
    extent_x = stored.shape[1]
    extent_z = stored.shape[2]
    span_cells = stored.shape[3]
    extended = with_halo(adjoint_in, (("gx", 1), ("gz", 2)), 1)
    pulled = pull(extended, 1, 0, extent_x, extent_z)
    adjoint_out, density = transpose_collision(stored, pulled)
    sensing = sense(density, pulled)
    sens_ext = with_halo(sensing, (("gx", 1), ("gz", 2)), 1)
    slots = marker_cell.shape[0]
    rows = jnp.arange(slots, dtype=jnp.int32)
    live = rows < marker_count[0]
    weight = jnp.where(live[None, :], marker_weight, 0.0)
    base_x = marker_cell // (extent_z * span_cells)
    base_z = marker_cell // span_cells % extent_z
    span = marker_cell % span_cells
    flat = sens_ext.reshape(3, -1)
    offsets = []
    for shift_x in (-1, 0, 1):
        for shift_z in (-1, 0, 1):
            offsets.append((1 + shift_x) * (extent_z + 2) * span_cells + (1 + shift_z) * span_cells)
    offset_table = jnp.asarray(np.array(offsets, dtype=np.int32))[:, None]
    start = (base_x * (extent_z + 2) + base_z) * span_cells + span
    address = (start[None, :] + offset_table).reshape(-1)
    picked = jnp.take(flat, address, axis=1).reshape(3, 9, slots)
    total = jnp.sum(weight[None, :, :] * picked, axis=1)
    onehot = (marker_panel[:, None] == jnp.arange(PANELS, dtype=jnp.int32)[None, :]).astype(
        jnp.float32
    )
    partial_sums = jnp.dot(total, onehot, precision=lax.Precision.HIGHEST)
    panel = lax.psum(partial_sums, ("gx", "gz"))
    return (adjoint_out, total, panel)


def solution(mesh):
    return jax.shard_map(
        local,
        mesh=mesh,
        in_specs=(
            P(None, "gx", "gz", None),
            P(None, "gx", "gz", None),
            P(("gx", "gz")),
            P(None, ("gx", "gz")),
            P(("gx", "gz")),
            P(("gx", "gz")),
        ),
        out_specs=(P(None, "gx", "gz", None), P(None, ("gx", "gz")), P()),
        check_vma=False,
    )
```

profile of v0, /device:TPU:1, one launch (start us, length us, event | category | flops | bytes accessed | tf_op | source)
XLA Modules:
  0.0 253.3 jit_solution(13228933084501921300)
XLA Ops:
  0.6 1.0 fusion.168
  1.7 5.7 %collective-permute-start = (f32[19,1,8,256]{3,2,1,0:T(8,128)S(1)}, f32[19,1,8,256]{3,2,1,0:T(8,128)S(1)}, u32[]{:S(2)}, u32[]{:S(2)}) collective-permute-start(f32[19,1,8,256]{3,2,1,0:T(8,128)S(1)} %get-tuple-element.61), channel_id=1, source_target_pairs={{0,16},{16,32},{32,48},{48,64},{64,80},{80,96},{96,112},{112,128},... | collective-permute-start | bytes 466952 | tf_op jit(solution)/shard_map/ppermute | solution.py:43
  7.4 1.3 collective-permute-start.1
  16.7 2.2 constant_dynamic-update-slice_fusion.1
  19.0 1.9 collective-permute-done.1
  20.9 1.7 fusion.167
  22.6 2.5 collective-permute-start.2
  25.1 1.9 collective-permute-start.3
  31.6 1.5 slice.300
  36.5 1.5 slice.307
  39.7 1.7 slice_bitcast_fusion.2
  52.6 2.2 add_multiply_fusion.3
  55.4 1.1 copy-done
  56.5 3.4 %add_dynamic-update-slice_fusion.18 = (f32[19,16,8,256]{3,2,1,0:T(8,128)S(1)}, f32[1,16,8,256]{3,2,1,0:T(8,128)S(1)}, f32[1,16,8,256]{3,2,1,0:T(8,128)S(1)}, f32...) fusion(f32[19,16,8,256]{3,2,1,0:T(8,128)} %param.8, f32[1,16,8,256]{3,2,1,0:T(8,128)S(1)} %get-tuple-element.24, ...), kind=kLoop, calls=%fused_computation.263 | loop fusion | flops 17235968 | bytes 4456448
  62.6 1.3 collective-permute-start.5
  63.9 6.8 %collective-permute-start.4 = (f32[3,1,8,256]{3,2,1,0:T(8,128)S(1)}, f32[3,1,8,256]{3,2,1,0:T(8,128)S(1)}, u32[]{:S(2)}, u32[]{:S(2)}) collective-permute-start(f32[3,1,8,256]{3,2,1,0:T(8,128)S(1)} %get-tuple-element.65), channel_id=1, source_target_pairs={{0,16},{16,32},{32,48},{48,64},{64,80},{80,96},{96,112},{112,128},... | collective-permute-start | bytes 73736 | tf_op jit(solution)/shard_map/ppermute | solution.py:43
  71.7 1.9 collective-permute-start.7
  73.6 4.5 %collective-permute-start.6 = (f32[3,18,1,256]{3,2,1,0:T(1,128)S(1)}, f32[3,18,1,256]{3,2,1,0:T(1,128)S(1)}, u32[]{:S(2)}, u32[]{:S(2)}) collective-permute-start(f32[3,18,1,256]{3,2,1,0:T(1,128)S(1)} %get-tuple-element.63), channel_id=1, source_target_pairs={{0,1},{1,2},{2,3},{3,4},{4,5},{5,6},{6,7},{7,8},{8,9},{9,10},{10,1... | collective-permute-start | bytes 165896 | tf_op jit(solution)/shard_map/ppermute | solution.py:43
  78.2 1.1 collective-permute-done.6
  79.8 11.5 %copy.242 = f32[3,18,10,256]{0,3,2,1:T(8,128)} copy(f32[3,18,10,256]{3,2,1,0:T(8,128)S(1)} %pad_maximum_fusion) | data formatting | bytes 1105920 | tf_op jit(solution)/shard_map/concatenate | solution.py:41
  91.3 69.0 %gather_fusion = f32[18432,3]{1,0:T(8,128)} fusion(f32[3,46080]{0,1:T(8,128)} %bitcast.63, s32[18432]{0:T(1024)S(1)} %copy-done.11), kind=kCustom, calls=%fused_computation | custom fusion | bytes 516096 | tf_op jit(solution)/shard_map/jit(_take)/gather | solution.py:147
  160.4 7.6 %multiply_reduce_fusion = f32[3,2048]{0,1:T(8,128)S(1)} fusion(f32[3,9,2048]{0,2,1:T(8,128)} %bitcast.64, f32[9,2048]{1,0:T(8,128)S(1)} %copy-done.10, pred[9,2048]{1,0:T(8,128)(4,1)S(1)} %fusion.140), kind=kLoop, calls=%fused_computation.1 | loop fusion | flops 159744 | bytes 337920 | tf_op jit(solution)/shard_map/reduce_sum | solution.py:148
  168.9 1.2 fusion
  170.1 83.2 %psum.7 = f32[3,128]{1,0:T(4,128)} all-reduce(f32[3,128]{1,0:T(4,128)S(1)} %fusion), channel_id=1, replica_groups=mesh['gx'=16,'gz'=16] {'gx','gz'}, use_global_device_ids=true, to_apply=%region_1.2 | all-reduce | flops 384 | bytes 3072 | tf_op jit(solution)/shard_map/psum | solution.py:153
  (115 shorter events, 33.7 us)
Async XLA Ops:
  0.6 14.7 %copy-start.17 = (f32[9,2048]{1,0:T(8,128)S(1)}, f32[9,2048]{1,0:T(8,128)}, u32[]{:S(2)}) copy-start(f32[9,2048]{1,0:T(8,128)} %param.10) | copy-start | bytes 221188
  1.7 15.0 %collective-permute-start = (f32[19,1,8,256]{3,2,1,0:T(8,128)S(1)}, f32[19,1,8,256]{3,2,1,0:T(8,128)S(1)}, u32[]{:S(2)}, u32[]{:S(2)}) collective-permute-start(f32[19,1,8,256]{3,2,1,0:T(8,128)S(1)} %get-tuple-element.61), channel_id=1, source_target_pairs={{0,16},{16,32},{32,48},{48,64},{64,80},{80,96},{96,112},{112,128},... | collective-permute-start | bytes 466952 | tf_op jit(solution)/shard_map/ppermute | solution.py:43
  7.4 13.4 %collective-permute-start.1 = (f32[19,1,8,256]{3,2,1,0:T(8,128)S(1)}, f32[19,1,8,256]{3,2,1,0:T(8,128)S(1)}, u32[]{:S(2)}, u32[]{:S(2)}) collective-permute-start(f32[19,1,8,256]{3,2,1,0:T(8,128)S(1)} %get-tuple-element.62), channel_id=1, source_target_pairs={{16,0},{32,16},{48,32},{64,48},{80,64},{96,80},{112,96},{128,112},... | collective-permute-start | bytes 466952 | tf_op jit(solution)/shard_map/ppermute | solution.py:45
  19.0 10.3 %copy-start.16 = (f32[19,17,8,256]{3,2,1,0:T(8,128)}, f32[19,17,8,256]{3,2,1,0:T(8,128)S(1)}, u32[]{:S(2)}) copy-start(f32[19,17,8,256]{3,2,1,0:T(8,128)S(1)} %get-tuple-element.60) | copy-start | bytes 7938052
  20.9 6.9 %copy-start.1 = (f32[19,17,8,256]{3,2,1,0:T(8,128)}, f32[19,17,8,256]{3,2,1,0:T(8,128)S(1)}, u32[]{:S(2)}) copy-start(f32[19,17,8,256]{3,2,1,0:T(8,128)S(1)} %get-tuple-element.68) | copy-start | bytes 7938052
  22.6 18.8 %collective-permute-start.2 = (f32[19,18,1,256]{3,2,1,0:T(1,128)}, f32[19,18,1,256]{3,2,1,0:T(1,128)S(1)}, u32[]{:S(2)}, u32[]{:S(2)}) collective-permute-start(f32[19,18,1,256]{3,2,1,0:T(1,128)} %get-tuple-element.51), channel_id=1, source_target_pairs={{0,1},{1,2},{2,3},{3,4},{4,5},{5,6},{6,7},{7,8},{8,9},{9,10},{10,1... | collective-permute-start | bytes 1050632 | tf_op jit(solution)/shard_map/ppermute | solution.py:43
  25.1 16.4 %collective-permute-start.3 = (f32[19,18,1,256]{3,2,1,0:T(1,128)}, f32[19,18,1,256]{3,2,1,0:T(1,128)S(1)}, u32[]{:S(2)}, u32[]{:S(2)}) collective-permute-start(f32[19,18,1,256]{3,2,1,0:T(1,128)} %get-tuple-element.50), channel_id=1, source_target_pairs={{1,0},{2,1},{3,2},{4,3},{5,4},{6,5},{7,6},{8,7},{9,8},{10,9},{11,1... | collective-permute-start | bytes 1050632 | tf_op jit(solution)/shard_map/ppermute | solution.py:45
  52.6 2.3 copy-start.4
  52.6 2.3 copy-start.5
  52.6 2.3 copy-start.6
  52.6 2.3 copy-start.7
  52.6 2.3 copy-start.8
  52.6 2.3 copy-start.9
  52.6 2.3 copy-start.12
  52.6 2.3 copy-start.13
  52.6 2.3 copy-start.14
  52.6 2.3 copy-start.15
  62.6 8.1 %collective-permute-start.5 = (f32[3,1,8,256]{3,2,1,0:T(8,128)S(1)}, f32[3,1,8,256]{3,2,1,0:T(8,128)S(1)}, u32[]{:S(2)}, u32[]{:S(2)}) collective-permute-start(f32[3,1,8,256]{3,2,1,0:T(8,128)S(1)} %get-tuple-element.66), channel_id=1, source_target_pairs={{16,0},{32,16},{48,32},{64,48},{80,64},{96,80},{112,96},{128,112},... | collective-permute-start | bytes 73736 | tf_op jit(solution)/shard_map/ppermute | solution.py:45
  63.9 7.7 %collective-permute-start.4 = (f32[3,1,8,256]{3,2,1,0:T(8,128)S(1)}, f32[3,1,8,256]{3,2,1,0:T(8,128)S(1)}, u32[]{:S(2)}, u32[]{:S(2)}) collective-permute-start(f32[3,1,8,256]{3,2,1,0:T(8,128)S(1)} %get-tuple-element.65), channel_id=1, source_target_pairs={{0,16},{16,32},{32,48},{48,64},{64,80},{80,96},{96,112},{112,128},... | collective-permute-start | bytes 73736 | tf_op jit(solution)/shard_map/ppermute | solution.py:43
  71.7 6.5 %collective-permute-start.7 = (f32[3,18,1,256]{3,2,1,0:T(1,128)S(1)}, f32[3,18,1,256]{3,2,1,0:T(1,128)S(1)}, u32[]{:S(2)}, u32[]{:S(2)}) collective-permute-start(f32[3,18,1,256]{3,2,1,0:T(1,128)S(1)} %get-tuple-element.64), channel_id=1, source_target_pairs={{1,0},{2,1},{3,2},{4,3},{5,4},{6,5},{7,6},{8,7},{9,8},{10,9},{11,1... | collective-permute-start | bytes 165896 | tf_op jit(solution)/shard_map/ppermute | solution.py:45
  73.6 5.7 %collective-permute-start.6 = (f32[3,18,1,256]{3,2,1,0:T(1,128)S(1)}, f32[3,18,1,256]{3,2,1,0:T(1,128)S(1)}, u32[]{:S(2)}, u32[]{:S(2)}) collective-permute-start(f32[3,18,1,256]{3,2,1,0:T(1,128)S(1)} %get-tuple-element.63), channel_id=1, source_target_pairs={{0,1},{1,2},{2,3},{3,4},{4,5},{5,6},{6,7},{7,8},{8,9},{9,10},{10,1... | collective-permute-start | bytes 165896 | tf_op jit(solution)/shard_map/ppermute | solution.py:43
  79.8 11.5 %copy-start.11 = (s32[18432]{0:T(1024)S(1)}, s32[18432]{0:T(1024)}, u32[]{:S(2)}) copy-start(s32[18432]{0:T(1024)} %broadcast_clamp_fusion) | copy-start | bytes 221188
  91.3 69.1 %copy-start.10 = (f32[9,2048]{1,0:T(8,128)S(1)}, f32[9,2048]{1,0:T(8,128)}, u32[]{:S(2)}) copy-start(f32[9,2048]{1,0:T(8,128)} %broadcast_select_fusion) | copy-start | bytes 221188
  160.4 8.5 %copy-start.18 = (s32[2048]{0:T(1024)S(1)}, s32[2048]{0:T(1024)}, u32[]{:S(2)}) copy-start(s32[2048]{0:T(1024)} %param.11) | copy-start | bytes 24580
  (4 other events, 7.3 us)
where the time goes:
time: 254 us; the launch traced here: 253 us
  local copies, waits for them, and re-layouts  117 us (46%)
  blocking collectives  83.2 us (33%)
  starting transfers between devices  25.9 us (10%)
  other arithmetic  20.3 us (8%)
  waiting for transfers between devices  3.94 us (2%)
    psum x1, blocking collectives, local(): panel = lax.psum(partial_sums, ('gx', 'gz'))  83.2 us
    gather x1, local copies, waits for them, and re-layouts, local(): picked = jnp.take(flat, address, axis=1).reshape(3, 9, slots)  69 us
    ppermute x4, starting transfers between devices, with_halo(): lax.ppermute(tail, axis, [(i, (i + 1) % count) for i in range(ends)])  19.5 us
    slice x20, local copies, waits for them, and re-layouts, pull(): piece = jnp.roll(piece, -step_y, axis=-1)  15 us
    concatenate x15, local copies, waits for them, and re-layouts, pull(): piece = jnp.roll(piece, -step_y, axis=-1)  12.3 us
    concatenate x2, local copies, waits for them, and re-layouts, with_halo(): jnp.concatenate([lax.ppermute(tail, axis, [(i, (i + 1) % count) for i in...  11.5 us
    reduce_sum x1, other arithmetic, local(): total = jnp.sum(weight[None, :, :] * picked, axis=1)  7.57 us
    unnamed x19, other arithmetic  6.82 us
  transfers between devices with their start and end apart: 8, of which 3 were waited for; matrix products, arithmetic and copies ran while one was open for 9% of the time, Pallas kernels for 0%

commit v1 on v0

v1 whole, which is shorter than its diff:
```python
import functools

import jax
import jax.numpy as jnp
from jax import lax
from jax.experimental import pallas as pl
from jax.experimental.pallas import tpu as pltpu
from jax.sharding import PartitionSpec as P

PANELS = 128
STENCIL = [
    (0, 0, 0),
    (1, 0, 0),
    (-1, 0, 0),
    (0, 1, 0),
    (0, -1, 0),
    (0, 0, 1),
    (0, 0, -1),
    (1, 1, 0),
    (-1, 1, 0),
    (1, -1, 0),
    (-1, -1, 0),
    (1, 0, 1),
    (-1, 0, 1),
    (1, 0, -1),
    (-1, 0, -1),
    (0, 1, 1),
    (0, -1, 1),
    (0, 1, -1),
    (0, -1, -1),
]
W0, W1, W2 = 1.0 / 3.0, 1.0 / 18.0, 1.0 / 36.0
WEIGHTS = [W0] + [W1] * 6 + [W2] * 12
OMEGA = 1.6

X, Z, Y = 16, 8, 256
X_UP = [q for q in range(19) if STENCIL[q][0] == 1]
X_DOWN = [q for q in range(19) if STENCIL[q][0] == -1]
Z_UP = [q for q in range(19) if STENCIL[q][2] == 1]
Z_DOWN = [q for q in range(19) if STENCIL[q][2] == -1]

ZROWS, Z_RHO, Z_MOM, Z_SPILL = 152, 80, 96, 144
XROWS, X_MOM, X_RHO, X_EDGE, X_FAR = 88, 40, 64, 72, 80

SROWS, S_LOW, S_HIGH = 192, 144, 168
CHUNK = 256


def roll_y(tile, q):
    step = STENCIL[q][1]
    if step == 0:
        return tile
    return pltpu.roll(tile, (-step) % Y, tile.ndim - 1)


def first_moments(g):
    def total(terms):
        out = None
        for q, sign in terms:
            if g[q] is None:
                continue
            if out is None:
                out = g[q] if sign > 0 else -g[q]
            else:
                out = out + g[q] if sign > 0 else out - g[q]
        return out

    parts = []
    for d in range(3):
        axis = total([(q, STENCIL[q][d]) for q in range(1, 7) if STENCIL[q][d]])
        diag = total([(q, STENCIL[q][d]) for q in range(7, 19) if STENCIL[q][d]])
        if axis is None and diag is None:
            parts.append(None)
        elif axis is None:
            parts.append(W2 * diag)
        elif diag is None:
            parts.append(W1 * axis)
        else:
            parts.append(W1 * axis + W2 * diag)
    return parts


def z_shift(tile, q, low, high):
    step = STENCIL[q][2]
    if step == 0:
        return tile
    rows = lax.broadcasted_iota(jnp.int32, tile.shape, 0)
    halo, edge = (high, Z - 1) if step > 0 else (low, 0)
    if halo is None:
        halo = jnp.zeros_like(tile)
    return jnp.where(rows == edge, halo, pltpu.roll(tile, (-step) % Z, 0))


def pulled_own(adj, q, x):
    return roll_y(z_shift(adj[q, x], q, None, None), q)


def row(ref, index):
    return ref[pl.ds(index, 1), :]


def pulled_z(adj, q, x, low, high, plane, low_on, high_on):
    step = STENCIL[q][2]
    lo = hi = None
    if step < 0:
        lo = row(low, Z_DOWN.index(q) * X + x) * low_on
    if step > 0:
        hi = row(high, Z_UP.index(q) * X + x) * high_on
    return roll_y(z_shift(adj[q, plane], q, lo, hi), q)


def ends():
    gz = lax.axis_index("gz")
    gx = lax.axis_index("gx")
    gz_n, gx_n = lax.axis_size("gz"), lax.axis_size("gx")
    flag = lambda c: jnp.where(c, 1.0, 0.0).astype(jnp.float32)
    return flag(gz > 0), flag(gz < gz_n - 1), flag(gx > 0), flag(gx < gx_n - 1)


def pack_z(stored, adj, to_low, to_high):
    def density(x):
        rho = stored[0, x].astype(jnp.float32)
        for q in range(1, 19):
            rho = rho + stored[q, x].astype(jnp.float32)
        return rho

    def column(x):
        g = [None] * 19
        for q in range(1, 19):
            at = x + STENCIL[q][0]
            if isinstance(at, int) and not 0 <= at < X:
                continue
            g[q] = pulled_own(adj, q, at)
        return first_moments(g)

    def inside(x):
        rho = density(x)
        to_low[pl.ds(Z_RHO + x, 1), :] = rho[0:1]
        to_high[pl.ds(Z_RHO + x, 1), :] = rho[Z - 1 : Z]
        for n in range(5):
            to_low[pl.ds(n * X + x, 1), :] = adj[Z_UP[n], x, 0:1, :]
            to_high[pl.ds(n * X + x, 1), :] = adj[Z_DOWN[n], x, Z - 1 : Z, :]
        for d, mom in enumerate(column(x)):
            to_low[pl.ds(Z_MOM + d * X + x, 1), :] = mom[0:1]
            to_high[pl.ds(Z_MOM + d * X + x, 1), :] = mom[Z - 1 : Z]

    inside(0)
    inside(X - 1)

    def body(x, carry):
        inside(x)
        return carry

    lax.fori_loop(1, X - 1, body, 0)
    spill = [column(-1), column(X)]
    zero = jnp.zeros((1, Y), jnp.float32)
    low_rows, high_rows = [], []
    for d in range(3):
        for side in range(2):
            mom = spill[side][d]
            low_rows.append(zero if mom is None else mom[0:1])
            high_rows.append(zero if mom is None else mom[Z - 1 : Z])
    to_low[Z_SPILL:, :] = jnp.concatenate(low_rows + [zero, zero])
    to_high[Z_SPILL:, :] = jnp.concatenate(high_rows + [zero, zero])


def shift_rows(tile, step):
    if step == 0:
        return tile
    rows = lax.broadcasted_iota(jnp.int32, tile.shape, 0)
    edge = X - 1 if step > 0 else 0
    return jnp.where(rows == edge, 0.0, pltpu.roll(tile, (-step) % X, 0))


def edge_moments(sent, pops):
    tiles, before, after = [None] * 19, [None] * 19, [None] * 19
    for n, q in enumerate(pops):
        tile = roll_y(sent[n * X : (n + 1) * X, :], q)
        step = STENCIL[q][0]
        tiles[q] = shift_rows(tile, step)
        if step > 0:
            before[q] = tile[0:1]
        if step < 0:
            after[q] = tile[X - 1 : X]
    return first_moments(tiles), first_moments(before), first_moments(after)


def plus(a, b):
    return a if b is None else a + b


def pack_x(
    stored_a, stored_b, adj_a, adj_b, sent_low, sent_high, low, high, to_left, to_right
):
    low_on, high_on, _, _ = ends()
    edge_low, edge_high = edge_moments(sent_low, Z_UP), edge_moments(sent_high, Z_DOWN)

    def side(out, adj, stored, x, plane, inner, away, skip):
        for n, q in enumerate(away):
            out[n * Z : (n + 1) * Z, :] = pulled_z(
                adj, q, x, low, high, plane, low_on, high_on
            )
        g = [None] * 19
        for q in range(1, 19):
            step = STENCIL[q][0]
            if step == 0:
                g[q] = pulled_z(adj, q, x, low, high, plane, low_on, high_on)
            elif step != skip:
                g[q] = pulled_z(adj, q, x + step, low, high, inner, low_on, high_on)
        for d, mom in enumerate(first_moments(g)):
            out[X_MOM + d * Z : X_MOM + (d + 1) * Z, :] = mom
        rho = stored[0, plane].astype(jnp.float32)
        for q in range(1, 19):
            rho = rho + stored[q, plane].astype(jnp.float32)
        out[X_RHO : X_RHO + Z, :] = rho
        beyond = 1 if x > 0 else 0
        edge, far = [], []
        for ref, own, on in ((low, edge_low, low_on), (high, edge_high, high_on)):
            for d in range(3):
                here = row(ref, Z_MOM + d * X + x) * on
                edge.append(here + own[0][d][x : x + 1])
                there = row(ref, Z_SPILL + 2 * d + beyond) * on
                far.append(plus(there, own[1 + beyond][d]))
        for ref, on in ((low, low_on), (high, high_on)):
            edge.append(row(ref, Z_RHO + x) * on)
        out[X_EDGE : X_EDGE + 8, :] = jnp.concatenate(edge)
        far = far + [jnp.zeros((1, Y), jnp.float32)] * 2
        out[X_FAR : X_FAR + 8, :] = jnp.concatenate(far)

    side(to_left, adj_a, stored_a, 0, 0, 1, X_UP, -1)
    side(to_right, adj_b, stored_b, X - 1, 1, 0, X_DOWN, 1)


def collide_transpose(f, g, emit):
    rho = f[0]
    for q in range(1, 19):
        rho = rho + f[q]
    jx = (f[1] - f[2]) + (f[7] - f[8]) + (f[9] - f[10]) + (f[11] - f[12]) + (f[13] - f[14])
    jy = (f[3] - f[4]) + (f[7] - f[9]) + (f[8] - f[10]) + (f[15] - f[16]) + (f[17] - f[18])
    jz = (f[5] - f[6]) + (f[11] - f[13]) + (f[12] - f[14]) + (f[15] - f[17]) + (f[16] - f[18])
    inv = 1.0 / rho
    ux, uy, uz = jx * inv, jy * inv, jz * inv

    sx, sy, sz = W1 * (g[1] + g[2]), W1 * (g[3] + g[4]), W1 * (g[5] + g[6])
    dx, dy, dz = W1 * (g[1] - g[2]), W1 * (g[3] - g[4]), W1 * (g[5] - g[6])

    def plane(a, b, c, d):
        p, m = g[a] + g[d], g[b] + g[c]
        r, s = g[a] - g[d], g[b] - g[c]
        return W2 * (p + m), W2 * (p - m), W2 * (r - s), W2 * (r + s)

    s_xy, c_xy, xy_x, xy_y = plane(7, 8, 9, 10)
    s_xz, c_xz, xz_x, xz_z = plane(11, 12, 13, 14)
    s_yz, c_yz, yz_y, yz_z = plane(15, 16, 17, 18)
    m_x = dx + xy_x + xz_x
    m_y = dy + xy_y + yz_y
    m_z = dz + xz_z + yz_z
    g_xx = sx + s_xy + s_xz
    g_yy = sy + s_xy + s_yz
    g_zz = sz + s_xz + s_yz
    g0 = W0 * g[0] + (sx + sy + sz) + (s_xy + s_xz + s_yz)
    vx = g_xx * ux + c_xy * uy + c_xz * uz
    vy = c_xy * ux + g_yy * uy + c_yz * uz
    vz = c_xz * ux + c_yz * uy + g_zz * uz
    uv = ux * vx + uy * vy + uz * vz
    uu = ux * ux + uy * uy + uz * uz
    base = OMEGA * (g0 - 4.5 * uv + 1.5 * uu * g0)
    bx = OMEGA * (3.0 * m_x + 9.0 * vx - 3.0 * ux * g0)
    by = OMEGA * (3.0 * m_y + 9.0 * vy - 3.0 * uy * g0)
    bz = OMEGA * (3.0 * m_z + 9.0 * vz - 3.0 * uz * g0)
    xp, xm = base + bx, base - bx
    yp, ym = base + by, base - by
    along = {
        (0, 0, 0): base,
        (1, 0, 0): xp,
        (-1, 0, 0): xm,
        (0, 1, 0): yp,
        (0, -1, 0): ym,
        (0, 0, 1): base + bz,
        (0, 0, -1): base - bz,
        (1, 1, 0): xp + by,
        (-1, 1, 0): xm + by,
        (1, -1, 0): xp - by,
        (-1, -1, 0): xm - by,
        (1, 0, 1): xp + bz,
        (-1, 0, 1): xm + bz,
        (1, 0, -1): xp - bz,
        (-1, 0, -1): xm - bz,
        (0, 1, 1): yp + bz,
        (0, -1, 1): ym + bz,
        (0, 1, -1): yp - bz,
        (0, -1, -1): ym - bz,
    }
    for q in range(19):
        emit(q, along[STENCIL[q]] + (1.0 - OMEGA) * g[q])
    scale = 3.0 * rho
    return scale * m_x, scale * m_y, scale * m_z


def interior(stored, adj, low, high, out, sens):
    low_on, high_on, _, _ = ends()

    def body(x, carry):
        f = [stored[q, x].astype(jnp.float32) for q in range(19)]
        g = []
        for q in range(19):
            at = x + STENCIL[q][0]
            g.append(pulled_z(adj, q, at, low, high, at, low_on, high_on))

        def emit(q, value):
            out[q, x] = value

        for d, tile in enumerate(collide_transpose(f, g, emit)):
            sens[d, pl.ds(pl.multiple_of(x * Z, Z), Z), :] = tile
        return carry

    lax.fori_loop(1, X - 1, body, 0)
    zero = jnp.zeros((Z, Y), jnp.float32)
    for q in range(19):
        out[q, 0] = zero
        out[q, X - 1] = zero
    for d in range(3):
        sens[d, 0:Z, :] = zero
        sens[d, (X - 1) * Z :, :] = zero


def finish(
    count,
    stored_a,
    stored_b,
    adj_a,
    adj_b,
    sent_low,
    sent_high,
    low,
    high,
    sent_left,
    sent_right,
    left,
    right,
    sens_in,
    cell,
    panel,
    weight,
    out_in,
    out,
    grad,
    partial,
    planes,
    sens,
    split,
    sems,
):
    del out_in
    low_on, high_on, left_on, right_on = ends()

    copies = []
    for x, adj, stored, plane, inner, taken, ref, on in (
        (0, adj_a, stored_a, 0, 1, X_DOWN, left, left_on),
        (X - 1, adj_b, stored_b, 1, 0, X_UP, right, right_on),
    ):
        f = [stored[q, plane].astype(jnp.float32) for q in range(19)]
        g = []
        for q in range(19):
            step = STENCIL[q][0]
            if q in taken:
                n = taken.index(q)
                g.append(ref[n * Z : (n + 1) * Z, :] * on)
            else:
                at = plane if step == 0 else inner
                g.append(pulled_z(adj, q, x + step, low, high, at, low_on, high_on))

        def emit(q, value, plane=plane):
            planes[plane, q] = value

        for d, tile in enumerate(collide_transpose(f, g, emit)):
            sens[pl.ds(d * SROWS + x * Z, Z), :] = tile
        copy = pltpu.make_async_copy(planes.at[plane], out.at[:, x], sems.at[plane])
        copy.start()
        copies.append(copy)

    for d in range(3):
        sens[d * SROWS + Z : d * SROWS + (X - 1) * Z, :] = sens_in[d, Z : (X - 1) * Z, :]

    for slot, sent, ref, pops in (
        (X, sent_left, left, X_UP),
        (X + 1, sent_right, right, X_DOWN),
    ):
        g = [None] * 19
        for n, q in enumerate(pops):
            g[q] = sent[n * Z : (n + 1) * Z, :]
        scale = 3.0 * ref[X_RHO : X_RHO + Z, :]
        for d, mom in enumerate(first_moments(g)):
            tile = scale * (ref[X_MOM + d * Z : X_MOM + (d + 1) * Z, :] + mom)
            sens[d * SROWS + slot * Z : d * SROWS + (slot + 1) * Z, :] = tile

    for k, (own, pops, ref, on, start) in enumerate(
        (
            (sent_low, Z_UP, low, low_on, S_LOW),
            (sent_high, Z_DOWN, high, high_on, S_HIGH),
        )
    ):
        moments, _, _ = edge_moments(own, pops)
        rows = lax.broadcasted_iota(jnp.int32, (X, Y), 0)
        scale = 3.0 * ref[Z_RHO : Z_RHO + X, :] * on
        for d in range(3):
            far_left = left[X_FAR + 3 * k + d : X_FAR + 3 * k + d + 1, :] * left_on
            far_right = right[X_FAR + 3 * k + d : X_FAR + 3 * k + d + 1, :] * right_on
            mom = moments[d] + ref[Z_MOM + d * X : Z_MOM + (d + 1) * X, :]
            mom = mom + jnp.where(rows == 0, far_left, 0.0)
            mom = mom + jnp.where(rows == X - 1, far_right, 0.0)
            sens[d * SROWS + start : d * SROWS + start + X, :] = scale * mom
            ends_rows = []
            for mine, theirs in ((sent_left, left), (sent_right, right)):
                rho = theirs[X_EDGE + 6 + k : X_EDGE + 7 + k, :]
                at = X_EDGE + 3 * k + d
                far = X_FAR + 3 * k + d
                ends_rows.append(3.0 * rho * (theirs[at : at + 1, :] + mine[far : far + 1, :]))
            ends_rows.append(jnp.zeros((6, Y), jnp.float32))
            sens[d * SROWS + start + X : d * SROWS + start + X + 8, :] = jnp.concatenate(
                ends_rows
            )

    value = sens[...]
    head = value.astype(jnp.bfloat16)
    split[:, 0:Y] = head
    split[:, Y : 2 * Y] = (value - head.astype(jnp.float32)).astype(jnp.bfloat16)

    sub = lax.broadcasted_iota(jnp.int32, (8, CHUNK), 0)
    edge_x = [sub, sub + 8, jnp.where(sub == 0, -1, jnp.where(sub == 1, X, -9))]
    lanes = lax.broadcasted_iota(jnp.int32, (1, CHUNK), 1)

    def chunk(c, acc):
        start = pl.multiple_of(c * CHUNK, CHUNK)
        where = pl.ds(start, CHUNK)
        cells = cell[:, where]
        base_x = cells >> 11
        base_z = (cells >> 8) & 7
        live = (lanes + start) < count[0]
        w = [jnp.where(live, weight[s : s + 1, where], 0.0) for s in range(9)]

        y_of = jnp.broadcast_to(cells & 255, (Y, CHUNK))
        hot = jnp.where(lax.broadcasted_iota(jnp.int32, (Y, CHUNK), 0) == y_of, 1.0, 0.0)
        hot = hot.astype(jnp.bfloat16)
        hot = jnp.concatenate([hot, hot])

        bx = jnp.broadcast_to(base_x, (8, CHUNK))
        bz = jnp.broadcast_to(base_z, (8, CHUNK))
        dz = sub - bz
        inner, lower, upper = [], [], []
        for a in range(3):
            wa = [jnp.broadcast_to(w[3 * a + b], (8, CHUNK)) for b in range(3)]
            inner.append(
                jnp.where(
                    dz == -1, wa[0], jnp.where(dz == 0, wa[1], jnp.where(dz == 1, wa[2], 0.0))
                )
            )
            lower.append(jnp.where(bz == 0, wa[0], 0.0))
            upper.append(jnp.where(bz == Z - 1, wa[2], 0.0))

        def pick(at, three):
            dx = at - bx
            return jnp.where(
                dx == -1, three[0], jnp.where(dx == 0, three[1], jnp.where(dx == 1, three[2], 0.0))
            )

        factors = [pick(x, inner) for x in list(range(X)) + [-1, X]]
        factors += [pick(at, lower) for at in edge_x]
        factors += [pick(at, upper) for at in edge_x]
        totals = []
        for d in range(3):
            picked = jnp.dot(
                split[d * SROWS : (d + 1) * SROWS, :], hot, preferred_element_type=jnp.float32
            )
            summed = factors[0] * picked[0:8]
            for t in range(1, SROWS // 8):
                summed = summed + factors[t] * picked[8 * t : 8 * t + 8]
            totals.append(jnp.sum(summed, axis=0, keepdims=True))
            grad[d : d + 1, where] = totals[d]
        rows = jnp.concatenate(totals + [jnp.zeros((5, CHUNK), jnp.float32)])
        top = rows.astype(jnp.bfloat16)
        rest = (rows - top.astype(jnp.float32)).astype(jnp.bfloat16)
        panels = jnp.broadcast_to(panel[:, where], (PANELS, CHUNK))
        which = lax.broadcasted_iota(jnp.int32, (PANELS, CHUNK), 0) == panels
        which = jnp.where(which, 1.0, 0.0).astype(jnp.bfloat16)
        both = jnp.concatenate([top, rest])
        return acc + lax.dot_general(
            both, which, (((1,), (1,)), ((), ())), preferred_element_type=jnp.float32
        )

    acc = lax.fori_loop(
        0, cell.shape[1] // CHUNK, chunk, jnp.zeros((16, PANELS), jnp.float32)
    )
    result = acc[0:3] + acc[8:11]
    for n in range(partial.shape[0]):
        partial[n] = result
    for copy in copies:
        copy.wait()


def ring(axis, step):
    count = lax.axis_size(axis)
    return [(i, (i + step) % count) for i in range(count)]


PARAMS = pltpu.CompilerParams(vmem_limit_bytes=48 * 1024 * 1024)


def cost(flops, moved):
    return pl.CostEstimate(flops=flops, bytes_accessed=moved, transcendentals=0)


def shape(*dims):
    return jax.ShapeDtypeStruct(dims, jnp.float32)


def pair(low):
    index = 0 if low else X // 2 - 1
    return pl.BlockSpec((19, 2, Z, Y), lambda i: (0, index, 0, 0))


def local(stored, adjoint_in, marker_cell, marker_weight, marker_panel, marker_count):
    slots = marker_cell.shape[0]
    whole = pl.BlockSpec(memory_space=pltpu.VMEM)
    to_low, to_high = pl.pallas_call(
        pack_z,
        out_shape=(shape(ZROWS, Y), shape(ZROWS, Y)),
        compiler_params=PARAMS,
        cost_estimate=cost(5_000_000, 4_000_000),
    )(stored, adjoint_in)
    low = lax.ppermute(to_high, "gz", ring("gz", 1))
    high = lax.ppermute(to_low, "gz", ring("gz", -1))
    to_left, to_right = pl.pallas_call(
        pack_x,
        grid=(1,),
        out_shape=(shape(XROWS, Y), shape(XROWS, Y)),
        in_specs=[pair(True), pair(False), pair(True), pair(False)] + [whole] * 4,
        compiler_params=PARAMS,
        cost_estimate=cost(1_000_000, 2_000_000),
    )(stored, stored, adjoint_in, adjoint_in, to_low, to_high, low, high)
    left = lax.ppermute(to_right, "gx", ring("gx", 1))
    right = lax.ppermute(to_left, "gx", ring("gx", -1))
    out, sens = pl.pallas_call(
        interior,
        out_shape=(shape(19, X, Z, Y), shape(3, X * Z, Y)),
        compiler_params=PARAMS,
        cost_estimate=cost(10_000_000, 7_000_000),
    )(stored, adjoint_in, low, high)
    any_space = pl.BlockSpec(memory_space=pl.ANY)
    out, grad, partial = pl.pallas_call(
        finish,
        grid=(1,),
        out_shape=(
            shape(19, X, Z, Y),
            shape(3, slots),
            shape(lax.axis_size("gz"), 3, PANELS),
        ),
        in_specs=[pl.BlockSpec(memory_space=pltpu.SMEM)]
        + [pair(True), pair(False), pair(True), pair(False)]
        + [whole] * 12
        + [any_space],
        out_specs=(any_space, whole, whole),
        scratch_shapes=[
            pltpu.VMEM((2, 19, Z, Y), jnp.float32),
            pltpu.VMEM((3 * SROWS, Y), jnp.float32),
            pltpu.VMEM((3 * SROWS, 2 * Y), jnp.bfloat16),
            pltpu.SemaphoreType.DMA((2,)),
        ],
        input_output_aliases={17: 0},
        compiler_params=PARAMS,
        cost_estimate=cost(1_000_000_000, 4_000_000),
    )(
        marker_count,
        stored,
        stored,
        adjoint_in,
        adjoint_in,
        to_low,
        to_high,
        low,
        high,
        to_left,
        to_right,
        left,
        right,
        sens,
        marker_cell.reshape(1, slots),
        marker_panel.reshape(1, slots),
        marker_weight,
        out,
    )
    total = jnp.sum(lax.all_to_all(partial, "gz", 0, 0), axis=0)
    copies = jnp.broadcast_to(total[None], (lax.axis_size("gx"),) + total.shape)
    total = jnp.sum(lax.all_to_all(copies, "gx", 0, 0), axis=0)
    return (out, grad, total)


def solution(mesh):
    return jax.shard_map(
        local,
        mesh=mesh,
        in_specs=(
            P(None, "gx", "gz", None),
            P(None, "gx", "gz", None),
            P(("gx", "gz")),
            P(None, ("gx", "gz")),
            P(("gx", "gz")),
            P(("gx", "gz")),
        ),
        out_specs=(P(None, "gx", "gz", None), P(None, ("gx", "gz")), P()),
        check_vma=False,
    )
```

time: 254 us -> 60 us (0.24)
  local copies, waits for them, and re-layouts: 117 us -> 3.02 us
  blocking collectives: 83.2 us -> 26.3 us
  other arithmetic: 20.3 us -> 0.63 us
  starting transfers between devices: 25.9 us -> 11.7 us
  Pallas kernels: 0 us -> 9.64 us
  waiting for transfers between devices: 3.94 us -> 7.1 us
    psum x1 -> x0, blocking collectives: 83.2 us -> none  [local(): panel = lax.psum(partial_sums, ('gx', 'gz'))]
    gather x1 -> x0, local copies, waits for them, and re-layouts: 69 us -> none  [local(): picked = jnp.take(flat, address, axis=1).reshape(3, 9, slots)]
    all_to_all x0 -> x2, blocking collectives: none -> 26.3 us  [the longest x1 14.9 us: local(): total = jnp.sum(lax.all_to_all(partial, 'gz', 0, 0), axis=0)]
    concatenate x17 -> x0, local copies, waits for them, and re-layouts: 23.8 us -> none  [the longest x15 12.3 us: pull(): piece = jnp.roll(piece, -step_y, axis=-1)]
    slice x22 -> x0, local copies, waits for them, and re-layouts: 17.7 us -> none  [the longest x20 15 us: pull(): piece = jnp.roll(piece, -step_y, axis=-1)]
    ppermute x8 -> x4, starting transfers between devices: 25.9 us -> 11.7 us  [the longest x1 8.37 us: local(): right = lax.ppermute(to_left, 'gx', ring('gx', -1))]
    pallas_call x0 -> x4, Pallas kernels: none -> 9.64 us  [the longest x1 4.72 us: local(): pl.pallas_call(finish, grid=(1,), out_shape=(shape(19, X, Z, Y), shape(3,...]
    reduce_sum x1 -> x2, other arithmetic: 7.57 us -> 0.63 us  [the longest x1 0.6 us: local(): total = jnp.sum(lax.all_to_all(copies, 'gx', 0, 0), axis=0)]
  transfers between devices with their start and end apart: 8 -> 4, of which waited for: 3 -> 2; matrix products, arithmetic and copies ran while one was open for 9% -> 0% of each run, Pallas kernels for 0% -> 5%
where the time goes in v1:
time: 60 us; the launch traced here: 59.8 us
  blocking collectives  26.3 us (44%)
  starting transfers between devices  11.7 us (20%)
  Pallas kernels  9.64 us (16%)
  waiting for transfers between devices  7.1 us (12%)
  local copies, waits for them, and re-layouts  3.02 us (5%)
  between operations  1.35 us (2%)
  other arithmetic  0.63 us (1%)
    all_to_all x1, blocking collectives, local(): total = jnp.sum(lax.all_to_all(partial, 'gz', 0, 0), axis=0)  14.9 us
    all_to_all x1, blocking collectives, local(): total = jnp.sum(lax.all_to_all(copies, 'gx', 0, 0), axis=0)  11.5 us
    ppermute x1, starting transfers between devices, local(): right = lax.ppermute(to_left, 'gx', ring('gx', -1))  8.37 us
    pallas_call x1, Pallas kernels, local(): pl.pallas_call(finish, grid=(1,), out_shape=(shape(19, X, Z, Y), shape(3,...  4.72 us
    ppermute x1, waiting for transfers between devices, local(): left = lax.ppermute(to_right, 'gx', ring('gx', 1))  4.4 us
    ppermute x1, starting transfers between devices, local(): high = lax.ppermute(to_low, 'gz', ring('gz', -1))  3.32 us
    pallas_call x1, Pallas kernels, local(): pl.pallas_call(interior, out_shape=(shape(19, X, Z, Y), shape(3, X * Z, Y...  3.22 us
    unnamed x10, local copies, waits for them, and re-layouts  3.01 us
  transfers between devices with their start and end apart: 4, of which 2 were waited for; matrix products, arithmetic and copies ran while one was open for 0% of the time, Pallas kernels for 5%

profile of v1, /device:TPU:1, one launch (start us, length us, event | category | flops | bytes accessed | tf_op | source)
XLA Modules:
  0.0 59.8 jit_solution(3336294019681513166)
XLA Ops:
  0.6 0.0 copy-start
  0.6 1.7 %copy-done = f32[19,16,8,256]{3,2,1,0:T(8,128)S(1)} copy-done((f32[19,16,8,256]{3,2,1,0:T(8,128)S(1)}, f32[19,16,8,256]{3,2,1,0:T(8,128)}, u32[]{:S(2)}) %copy-start) | copy-done | bytes 2490392
  2.3 1.3 %copy-done.1 = bf16[19,16,8,256]{3,2,1,0:T(8,128)(2,1)S(1)} copy-done((bf16[19,16,8,256]{3,2,1,0:T(8,128)(2,1)S(1)}, bf16[19,16,8,256]{3,2,1,0:T(8,128)(2,1)}, u32[]{:S(2)}) %copy-start.1) | copy-done | bytes 1245208
  3.6 1.6 %shard_map.85 = (f32[152,256]{1,0:T(8,128)S(1)}, f32[152,256]{1,0:T(8,128)S(1)}) custom-call(bf16[19,16,8,256]{3,2,1,0:T(8,128)(2,1)S(1)} %copy-done.1, f32[19,16,8,256]{3,2,1,0:T(8,128)S(1)} %copy-done), custom_call_target="tpu_custom_call" | custom-call | flops 5000000 | bytes 4000000 | tf_op jit(solution)/shard_map/pallas_call | solution.py:525
  5.2 3.3 %collective-permute-start.1 = (f32[152,256]{1,0:T(8,128)S(1)}, f32[152,256]{1,0:T(8,128)S(1)}, u32[]{:S(2)}, u32[]{:S(2)}) collective-permute-start(f32[152,256]{1,0:T(8,128)S(1)} %get-tuple-element.12.sent_low), channel_id=1, source_target_pairs={{0,15},{1,0},{2,1},{3,2},{4,3},{5,4},{6,5},{7,6},{8,7},{9,8},{10,9... | collective-permute-start | bytes 466952 | tf_op jit(solution)/shard_map/ppermute | solution.py:532
  8.5 0.0 collective-permute-start
  8.5 2.7 %collective-permute-done.1.high = f32[152,256]{1,0:T(8,128)S(1)} collective-permute-done((f32[152,256]{1,0:T(8,128)S(1)}, f32[152,256]{1,0:T(8,128)S(1)}, u32[]{:S(2)}, u32[]{:S(2)}) %collective-permute-start.1) | collective-permute-done | bytes 155680 | tf_op jit(solution)/shard_map/ppermute | solution.py:532
  11.2 0.0 collective-permute-done.low
  11.2 0.1 shard_map.86
  11.4 0.0 copy-start.2
  11.4 0.0 copy-start.3
  11.4 0.0 copy-start.4
  11.4 8.4 %collective-permute-start.3 = (f32[88,256]{1,0:T(8,128)S(1)}, f32[88,256]{1,0:T(8,128)S(1)}, u32[]{:S(2)}, u32[]{:S(2)}) collective-permute-start(f32[88,256]{1,0:T(8,128)S(1)} %get-tuple-element.14.sent_left), channel_id=1, source_target_pairs={{0,240},{16,0},{32,16},{48,32},{64,48},{80,64},{96,80},{112,96},{1... | collective-permute-start | bytes 270344 | tf_op jit(solution)/shard_map/ppermute | solution.py:542
  19.8 0.0 collective-permute-start.2
  20.4 3.2 %shard_map.87 = (f32[19,16,8,256]{3,2,1,0:T(8,128)}, f32[3,128,256]{2,1,0:T(8,128)S(1)}) custom-call(bf16[19,16,8,256]{3,2,1,0:T(8,128)(2,1)S(1)} %copy-done.1, f32[19,16,8,256]{3,2,1,0:T(8,128)S(1)} %copy-done, f32[152,256]{1,0:T(8,128)S(1)} %collective-permute-done.low, f32[152,256]{1,0:T(8,128)S(1)} %collective-permute-done.1.high), custom_call_target="tpu_custom_call" | custom-call | flops 10000000 | bytes 7000000 | tf_op jit(solution)/shard_map/pallas_call | solution.py:543
  23.6 0.0 collective-permute-done.3.right
  23.7 4.4 %collective-permute-done.2.left = f32[88,256]{1,0:T(8,128)S(1)} collective-permute-done((f32[88,256]{1,0:T(8,128)S(1)}, f32[88,256]{1,0:T(8,128)S(1)}, u32[]{:S(2)}, u32[]{:S(2)}) %collective-permute-start.2) | collective-permute-done | bytes 90144 | tf_op jit(solution)/shard_map/ppermute | solution.py:541
  28.1 0.0 copy-done.2
  28.1 0.0 copy-done.3
  28.1 0.0 copy-done.4
  28.1 4.7 %shard_map.88 = (f32[19,16,8,256]{3,2,1,0:T(8,128)}, f32[3,2048]{1,0:T(4,128)}, f32[16,3,128]{2,1,0:T(4,128)S(1)}) custom-call(s32[1]{0:T(128)S(6)} %copy.13.count, bf16[19,16,8,256]{3,2,1,0:T(8,128)(2,1)S(1)} %copy-done.1, bf16[19,16,8,256]{3,2,1,0:T(8,128)(2,1)S(1)} %copy-done.1, f32[19,16,8,256]{3,2,1,0:T(8,128)S(1)} %copy-done, ...), custom_call_target="tpu_custom_call", output_to_operand_aliasing={{0}: (17, {})} | custom-call | flops 1000000000 | bytes 4000000 | tf_op jit(solution)/shard_map/pallas_call | solution.py:550
  32.8 14.9 %all_to_all.10 = f32[16,3,128]{2,1,0:T(4,128)S(1)} all-to-all(f32[16,3,128]{2,1,0:T(4,128)S(1)} %get-tuple-element.20), channel_id=1, replica_groups=mesh['gx'=16,'gz'=16] {'gz'}, dimensions={0} | all-to-all | bytes 49152 | tf_op jit(solution)/shard_map/all_to_all | solution.py:592
  47.7 11.5 %all_to_all.11 = f32[16,3,128]{2,1,0:T(4,128)S(1)} all-to-all(f32[16,3,128]{2,1,0:T(4,128)S(1)} %broadcast_in_dim.2), channel_id=1, replica_groups=mesh['gx'=16,'gz'=16] {'gx'}, dimensions={0} | all-to-all | bytes 49152 | tf_op jit(solution)/shard_map/all_to_all | solution.py:594
  59.2 0.6 %reduce_sum.19 = f32[3,128]{1,0:T(4,128)} reduce(f32[16,3,128]{2,1,0:T(4,128)S(1)} %all_to_all.11, f32[]{:T(128)} %constant.0.clone.1), dimensions={0}, to_apply=%region_1.0 | reduce | flops 5760 | bytes 26116 | tf_op jit(solution)/shard_map/reduce_sum | solution.py:594
  (3 shorter events, 0.0 us)
Async XLA Ops:
  0.6 1.7 %copy-start = (f32[19,16,8,256]{3,2,1,0:T(8,128)S(1)}, f32[19,16,8,256]{3,2,1,0:T(8,128)}, u32[]{:S(2)}) copy-start(f32[19,16,8,256]{3,2,1,0:T(8,128)} %adj_b.3) | copy-start | bytes 7471108
  2.3 1.3 %copy-start.1 = (bf16[19,16,8,256]{3,2,1,0:T(8,128)(2,1)S(1)}, bf16[19,16,8,256]{3,2,1,0:T(8,128)(2,1)}, u32[]{:S(2)}) copy-start(bf16[19,16,8,256]{3,2,1,0:T(8,128)(2,1)} %stored_b.3) | copy-start | bytes 3735556
  5.2 6.0 %collective-permute-start.1 = (f32[152,256]{1,0:T(8,128)S(1)}, f32[152,256]{1,0:T(8,128)S(1)}, u32[]{:S(2)}, u32[]{:S(2)}) collective-permute-start(f32[152,256]{1,0:T(8,128)S(1)} %get-tuple-element.12.sent_low), channel_id=1, source_target_pairs={{0,15},{1,0},{2,1},{3,2},{4,3},{5,4},{6,5},{7,6},{8,7},{9,8},{10,9... | collective-permute-start | bytes 466952 | tf_op jit(solution)/shard_map/ppermute | solution.py:532
  8.5 2.7 %collective-permute-start = (f32[152,256]{1,0:T(8,128)S(1)}, f32[152,256]{1,0:T(8,128)S(1)}, u32[]{:S(2)}, u32[]{:S(2)}) collective-permute-start(f32[152,256]{1,0:T(8,128)S(1)} %get-tuple-element.13.sent_high), channel_id=1, source_target_pairs={{0,1},{1,2},{2,3},{3,4},{4,5},{5,6},{6,7},{7,8},{8,9},{9,10},{10,1... | collective-permute-start | bytes 466952 | tf_op jit(solution)/shard_map/ppermute | solution.py:531
  11.4 16.7 %copy-start.2 = (f32[9,2048]{1,0:T(8,128)S(1)}, f32[9,2048]{1,0:T(8,128)}, u32[]{:S(2)}) copy-start(f32[9,2048]{1,0:T(8,128)} %weight.1) | copy-start | bytes 221188
  11.4 16.7 %copy-start.3 = (s32[2048]{0:T(1024)S(1)}, s32[2048]{0:T(1024)}, u32[]{:S(2)}) copy-start(s32[2048]{0:T(1024)} %param.8) | copy-start | bytes 24580
  11.4 16.7 %copy-start.4 = (s32[2048]{0:T(1024)S(1)}, s32[2048]{0:T(1024)}, u32[]{:S(2)}) copy-start(s32[2048]{0:T(1024)} %param.10) | copy-start | bytes 24580
  11.4 12.3 %collective-permute-start.3 = (f32[88,256]{1,0:T(8,128)S(1)}, f32[88,256]{1,0:T(8,128)S(1)}, u32[]{:S(2)}, u32[]{:S(2)}) collective-permute-start(f32[88,256]{1,0:T(8,128)S(1)} %get-tuple-element.14.sent_left), channel_id=1, source_target_pairs={{0,240},{16,0},{32,16},{48,32},{64,48},{80,64},{96,80},{112,96},{1... | collective-permute-start | bytes 270344 | tf_op jit(solution)/shard_map/ppermute | solution.py:542
  19.8 8.3 %collective-permute-start.2 = (f32[88,256]{1,0:T(8,128)S(1)}, f32[88,256]{1,0:T(8,128)S(1)}, u32[]{:S(2)}, u32[]{:S(2)}) collective-permute-start(f32[88,256]{1,0:T(8,128)S(1)} %get-tuple-element.15.sent_right), channel_id=1, source_target_pairs={{0,16},{16,32},{32,48},{48,64},{64,80},{80,96},{96,112},{112,128},... | collective-permute-start | bytes 270344 | tf_op jit(solution)/shard_map/ppermute | solution.py:541

commit v2 on v1

--- a/solution.py
+++ b/solution.py
@@ -42,8 +42,10 @@
 ZROWS, Z_RHO, Z_MOM, Z_SPILL = 152, 80, 96, 144
 XROWS, X_MOM, X_RHO, X_EDGE, X_FAR = 88, 40, 64, 72, 80
 
-SROWS, S_LOW, S_HIGH = 192, 144, 168
 CHUNK = 256
+UNROLL_C = 8
+GROUPS = 4
+STEP = X // GROUPS
 
 
 def roll_y(tile, q):
@@ -117,12 +119,14 @@
     return flag(gz > 0), flag(gz < gz_n - 1), flag(gx > 0), flag(gx < gx_n - 1)
 
 
-def pack_z(stored, adj, to_low, to_high):
-    def density(x):
-        rho = stored[0, x].astype(jnp.float32)
-        for q in range(1, 19):
-            rho = rho + stored[q, x].astype(jnp.float32)
-        return rho
+def pack_z(stored_in, adj_in, to_low, to_high, mom_out, rho_out, stored, adj, sems):
+    copies = []
+    for n in range(GROUPS):
+        part = pl.ds(n * STEP, STEP)
+        for k, (src, dst) in enumerate(((adj_in, adj), (stored_in, stored))):
+            copy = pltpu.make_async_copy(src.at[:, part], dst.at[:, part], sems.at[k, n])
+            copy.start()
+            copies.append(copy)
 
     def column(x):
         g = [None] * 19
@@ -133,25 +137,31 @@
             g[q] = pulled_own(adj, q, at)
         return first_moments(g)
 
-    def inside(x):
-        rho = density(x)
+    def density(x):
+        rho = stored[0, x].astype(jnp.float32)
+        for q in range(1, 19):
+            rho = rho + stored[q, x].astype(jnp.float32)
+        rho_out[pl.ds(x * Z, Z), :] = rho
         to_low[pl.ds(Z_RHO + x, 1), :] = rho[0:1]
         to_high[pl.ds(Z_RHO + x, 1), :] = rho[Z - 1 : Z]
         for n in range(5):
             to_low[pl.ds(n * X + x, 1), :] = adj[Z_UP[n], x, 0:1, :]
             to_high[pl.ds(n * X + x, 1), :] = adj[Z_DOWN[n], x, Z - 1 : Z, :]
+
+    def moments(x):
         for d, mom in enumerate(column(x)):
+            mom_out[d, pl.ds(x * Z, Z), :] = mom
             to_low[pl.ds(Z_MOM + d * X + x, 1), :] = mom[0:1]
             to_high[pl.ds(Z_MOM + d * X + x, 1), :] = mom[Z - 1 : Z]
 
-    inside(0)
-    inside(X - 1)
-
-    def body(x, carry):
-        inside(x)
-        return carry
-
-    lax.fori_loop(1, X - 1, body, 0)
+    for n in range(GROUPS):
+        copies[2 * n].wait()
+        copies[2 * n + 1].wait()
+        first, last = n * STEP, (n + 1) * STEP
+        for x in range(first, last):
+            density(x)
+        for x in range(max(first - 1, 0), last if n == GROUPS - 1 else last - 1):
+            moments(x)
     spill = [column(-1), column(X)]
     zero = jnp.zeros((1, Y), jnp.float32)
     low_rows, high_rows = [], []
@@ -190,8 +200,19 @@
 
 
 def pack_x(
-    stored_a, stored_b, adj_a, adj_b, sent_low, sent_high, low, high, to_left, to_right
+    stored_a,
+    stored_b,
+    adj_a,
+    adj_b,
+    sent_low,
+    sent_high,
+    low,
+    high,
+    after,
+    to_left,
+    to_right,
 ):
+    del after
     low_on, high_on, _, _ = ends()
     edge_low, edge_high = edge_moments(sent_low, Z_UP), edge_moments(sent_high, Z_DOWN)
 
@@ -293,11 +314,9 @@
     }
     for q in range(19):
         emit(q, along[STENCIL[q]] + (1.0 - OMEGA) * g[q])
-    scale = 3.0 * rho
-    return scale * m_x, scale * m_y, scale * m_z
-
-
-def interior(stored, adj, low, high, out, sens):
+
+
+def interior(stored, adj, low, high, out):
     low_on, high_on, _, _ = ends()
 
     def body(x, carry):
@@ -310,8 +329,7 @@
         def emit(q, value):
             out[q, x] = value
 
-        for d, tile in enumerate(collide_transpose(f, g, emit)):
-            sens[d, pl.ds(pl.multiple_of(x * Z, Z), Z), :] = tile
+        collide_transpose(f, g, emit)
         return carry
 
     lax.fori_loop(1, X - 1, body, 0)
@@ -319,41 +337,11 @@
     for q in range(19):
         out[q, 0] = zero
         out[q, X - 1] = zero
-    for d in range(3):
-        sens[d, 0:Z, :] = zero
-        sens[d, (X - 1) * Z :, :] = zero
-
-
-def finish(
-    count,
-    stored_a,
-    stored_b,
-    adj_a,
-    adj_b,
-    sent_low,
-    sent_high,
-    low,
-    high,
-    sent_left,
-    sent_right,
-    left,
-    right,
-    sens_in,
-    cell,
-    panel,
-    weight,
-    out_in,
-    out,
-    grad,
-    partial,
-    planes,
-    sens,
-    split,
-    sems,
-):
+
+
+def borders(stored_a, stored_b, adj_a, adj_b, low, high, left, right, out_in, out, planes, sems):
     del out_in
     low_on, high_on, left_on, right_on = ends()
-
     copies = []
     for x, adj, stored, plane, inner, taken, ref, on in (
         (0, adj_a, stored_a, 0, 1, X_DOWN, left, left_on),
@@ -373,129 +361,225 @@
         def emit(q, value, plane=plane):
             planes[plane, q] = value
 
-        for d, tile in enumerate(collide_transpose(f, g, emit)):
-            sens[pl.ds(d * SROWS + x * Z, Z), :] = tile
+        collide_transpose(f, g, emit)
         copy = pltpu.make_async_copy(planes.at[plane], out.at[:, x], sems.at[plane])
         copy.start()
         copies.append(copy)
-
+    for copy in copies:
+        copy.wait()
+
+
+def put(split, at, tile):
+    head = tile.astype(jnp.bfloat16)
+    split[pl.ds(at, tile.shape[0]), :] = head
+    rest = (tile - head.astype(jnp.float32)).astype(jnp.bfloat16)
+    split[pl.ds(split.shape[0] // 2 + at, tile.shape[0]), :] = rest
+
+
+def bases(cell, where):
+    cells = cell[:, where]
+    bx = jnp.broadcast_to(cells >> 11, (8, CHUNK))
+    bz = jnp.broadcast_to((cells >> 8) & 7, (8, CHUNK))
+    return bx, bz
+
+
+def pick(dx, three):
+    return jnp.where(
+        dx == -1, three[0], jnp.where(dx == 0, three[1], jnp.where(dx == 1, three[2], 0.0))
+    )
+
+
+def gathered(split, rows, hot, factors):
+    picked = jnp.dot(split[...], hot, preferred_element_type=jnp.float32)
+    half = split.shape[0] // 2
+    out = []
     for d in range(3):
-        sens[d * SROWS + Z : d * SROWS + (X - 1) * Z, :] = sens_in[d, Z : (X - 1) * Z, :]
-
-    for slot, sent, ref, pops in (
-        (X, sent_left, left, X_UP),
-        (X + 1, sent_right, right, X_DOWN),
-    ):
-        g = [None] * 19
-        for n, q in enumerate(pops):
-            g[q] = sent[n * Z : (n + 1) * Z, :]
-        scale = 3.0 * ref[X_RHO : X_RHO + Z, :]
-        for d, mom in enumerate(first_moments(g)):
-            tile = scale * (ref[X_MOM + d * Z : X_MOM + (d + 1) * Z, :] + mom)
-            sens[d * SROWS + slot * Z : d * SROWS + (slot + 1) * Z, :] = tile
-
-    for k, (own, pops, ref, on, start) in enumerate(
+        summed = None
+        for t, factor in enumerate(factors):
+            at = d * rows + 8 * t
+            term = factor * (picked[at : at + 8] + picked[half + at : half + at + 8])
+            summed = term if summed is None else summed + term
+        out.append(summed)
+    return out
+
+
+def sublanes():
+    return lax.broadcasted_iota(jnp.int32, (8, CHUNK), 0)
+
+
+def chunk_of(c):
+    return pl.ds(pl.multiple_of(c * CHUNK, CHUNK), CHUNK)
+
+
+def weights_of(weight, where):
+    return [jnp.broadcast_to(weight[s : s + 1, where], (8, CHUNK)) for s in range(9)]
+
+
+def stage_a(count, mom, rho, cell, weight, live_weight, hot, acc, split):
+    rows = X * Z
+    for x in range(0, X, 2):
+        scale = 3.0 * rho[x * Z : (x + 2) * Z, :]
+        for d in range(3):
+            put(split, d * rows + x * Z, scale * mom[d, x * Z : (x + 2) * Z, :])
+    lanes = lax.broadcasted_iota(jnp.int32, (9, CHUNK), 1)
+
+    def chunk(c, carry):
+        where = chunk_of(c)
+        live = (lanes + c * CHUNK) < count[0]
+        live_weight[:, where] = jnp.where(live, weight[:, where], 0.0)
+        w = weights_of(live_weight, where)
+        y_of = jnp.broadcast_to(cell[:, where] & (Y - 1), (Y, CHUNK))
+        one = jnp.where(lax.broadcasted_iota(jnp.int32, (Y, CHUNK), 0) == y_of, 1.0, 0.0)
+        one = one.astype(jnp.bfloat16)
+        hot[:, where] = one
+        bx, bz = bases(cell, where)
+        dz = sublanes() - bz
+        three = [pick(dz, w[3 * a : 3 * a + 3]) for a in range(3)]
+        factors = [pick(x - bx, three) for x in range(X)]
+        for d, tile in enumerate(gathered(split, rows, one, factors)):
+            acc[d, :, where] = tile
+        return carry
+
+    lax.fori_loop(0, cell.shape[1] // CHUNK, chunk, 0)
+
+
+def stage_b(
+    sent_low, sent_high, low, high, cell, panel, weight, hot, acc_in, acc, which, split
+):
+    low_on, high_on, _, _ = ends()
+    rows = 4 * X
+    for k, (sent, up, back, ref, on) in enumerate(
         (
-            (sent_low, Z_UP, low, low_on, S_LOW),
-            (sent_high, Z_DOWN, high, high_on, S_HIGH),
+            (sent_low, Z_UP, Z_DOWN, low, low_on),
+            (sent_high, Z_DOWN, Z_UP, high, high_on),
         )
     ):
-        moments, _, _ = edge_moments(own, pops)
-        rows = lax.broadcasted_iota(jnp.int32, (X, Y), 0)
-        scale = 3.0 * ref[Z_RHO : Z_RHO + X, :] * on
+        beyond, _, _ = edge_moments(sent, up)
+        added, _, _ = edge_moments(ref, back)
+        here = 3.0 * sent[Z_RHO : Z_RHO + X, :] * on
+        there = 3.0 * ref[Z_RHO : Z_RHO + X, :]
         for d in range(3):
-            far_left = left[X_FAR + 3 * k + d : X_FAR + 3 * k + d + 1, :] * left_on
-            far_right = right[X_FAR + 3 * k + d : X_FAR + 3 * k + d + 1, :] * right_on
-            mom = moments[d] + ref[Z_MOM + d * X : Z_MOM + (d + 1) * X, :]
-            mom = mom + jnp.where(rows == 0, far_left, 0.0)
-            mom = mom + jnp.where(rows == X - 1, far_right, 0.0)
-            sens[d * SROWS + start : d * SROWS + start + X, :] = scale * mom
-            ends_rows = []
+            put(split, d * rows + k * X, here * added[d])
+            mom = beyond[d] + ref[Z_MOM + d * X : Z_MOM + (d + 1) * X, :]
+            put(split, d * rows + (2 + k) * X, there * mom)
+
+    def chunk(c, carry):
+        where = chunk_of(c)
+        w = weights_of(weight, where)
+        bx, bz = bases(cell, where)
+        sub = sublanes()
+        dx = [sub - bx, sub + 8 - bx]
+        first, last, under, over = [], [], [], []
+        for a in range(3):
+            wa = w[3 * a : 3 * a + 3]
+            first.append(jnp.where(bz == 0, wa[1], jnp.where(bz == 1, wa[0], 0.0)))
+            last.append(jnp.where(bz == Z - 1, wa[1], jnp.where(bz == Z - 2, wa[2], 0.0)))
+            under.append(jnp.where(bz == 0, wa[0], 0.0))
+            over.append(jnp.where(bz == Z - 1, wa[2], 0.0))
+        factors = [pick(at, three) for three in (first, last, under, over) for at in dx]
+        for d, tile in enumerate(gathered(split, rows, hot[:, where], factors)):
+            acc[d, :, where] = acc_in[d, :, where] + tile
+        panels = jnp.broadcast_to(panel[:, where], (PANELS, CHUNK))
+        match = lax.broadcasted_iota(jnp.int32, (PANELS, CHUNK), 0) == panels
+        which[:, where] = jnp.where(match, 1.0, 0.0).astype(jnp.bfloat16)
+        return carry
+
+    lax.fori_loop(0, cell.shape[1] // CHUNK, chunk, 0)
+
+
+def stage_c(
+    rho,
+    sent_left,
+    sent_right,
+    low,
+    high,
+    left,
+    right,
+    cell,
+    weight,
+    hot,
+    which,
+    acc_in,
+    grad,
+    partial,
+    split,
+    totals,
+):
+    low_on, high_on, left_on, right_on = ends()
+    rows = 48
+    zero = jnp.zeros((8, Y), jnp.float32)
+    beyond, added = [], []
+    for sent, ref, on, pops, back, x in (
+        (sent_left, left, left_on, X_UP, X_DOWN, 0),
+        (sent_right, right, right_on, X_DOWN, X_UP, X - 1),
+    ):
+        g, h = [None] * 19, [None] * 19
+        for n in range(5):
+            g[pops[n]] = sent[n * Z : (n + 1) * Z, :]
+            h[back[n]] = ref[n * Z : (n + 1) * Z, :]
+        there = 3.0 * ref[X_RHO : X_RHO + Z, :]
+        here = 3.0 * on * rho[x * Z : (x + 1) * Z, :]
+        beyond.append(
+            [
+                there * (ref[X_MOM + d * Z : X_MOM + (d + 1) * Z, :] + mom)
+                for d, mom in enumerate(first_moments(g))
+            ]
+        )
+        added.append([here * mom for mom in first_moments(h)])
+    for d in range(3):
+        corner = []
+        for k, (ref, on) in enumerate(((low, low_on), (high, high_on))):
+            at, far = X_EDGE + 3 * k + d, X_FAR + 3 * k + d
             for mine, theirs in ((sent_left, left), (sent_right, right)):
-                rho = theirs[X_EDGE + 6 + k : X_EDGE + 7 + k, :]
-                at = X_EDGE + 3 * k + d
-                far = X_FAR + 3 * k + d
-                ends_rows.append(3.0 * rho * (theirs[at : at + 1, :] + mine[far : far + 1, :]))
-            ends_rows.append(jnp.zeros((6, Y), jnp.float32))
-            sens[d * SROWS + start + X : d * SROWS + start + X + 8, :] = jnp.concatenate(
-                ends_rows
-            )
-
-    value = sens[...]
-    head = value.astype(jnp.bfloat16)
-    split[:, 0:Y] = head
-    split[:, Y : 2 * Y] = (value - head.astype(jnp.float32)).astype(jnp.bfloat16)
-
-    sub = lax.broadcasted_iota(jnp.int32, (8, CHUNK), 0)
-    edge_x = [sub, sub + 8, jnp.where(sub == 0, -1, jnp.where(sub == 1, X, -9))]
-    lanes = lax.broadcasted_iota(jnp.int32, (1, CHUNK), 1)
-
-    def chunk(c, acc):
-        start = pl.multiple_of(c * CHUNK, CHUNK)
-        where = pl.ds(start, CHUNK)
-        cells = cell[:, where]
-        base_x = cells >> 11
-        base_z = (cells >> 8) & 7
-        live = (lanes + start) < count[0]
-        w = [jnp.where(live, weight[s : s + 1, where], 0.0) for s in range(9)]
-
-        y_of = jnp.broadcast_to(cells & 255, (Y, CHUNK))
-        hot = jnp.where(lax.broadcasted_iota(jnp.int32, (Y, CHUNK), 0) == y_of, 1.0, 0.0)
-        hot = hot.astype(jnp.bfloat16)
-        hot = jnp.concatenate([hot, hot])
-
-        bx = jnp.broadcast_to(base_x, (8, CHUNK))
-        bz = jnp.broadcast_to(base_z, (8, CHUNK))
+                scale = 3.0 * theirs[X_EDGE + 6 + k : X_EDGE + 7 + k, :]
+                corner.append(scale * (theirs[at : at + 1, :] + mine[far : far + 1, :]))
+            for theirs, x, side_on in ((left, 0, left_on), (right, X - 1, right_on)):
+                scale = 3.0 * on * side_on * row(ref, Z_RHO + x)
+                corner.append(scale * theirs[far : far + 1, :])
+        tiles = [beyond[0][d], beyond[1][d], added[0][d], added[1][d], jnp.concatenate(corner), zero]
+        for t in range(0, 6, 2):
+            put(split, d * rows + t * 8, jnp.concatenate(tiles[t : t + 2]))
+
+    sub = sublanes()
+    kind = sub & 3
+    corner_x = jnp.where(kind == 0, -1, jnp.where(kind == 1, X, jnp.where(kind == 2, 0, X - 1)))
+    bottom = sub < 4
+
+    def chunk(c, carry):
+        where = chunk_of(c)
+        w = weights_of(weight, where)
+        bx, bz = bases(cell, where)
         dz = sub - bz
-        inner, lower, upper = [], [], []
+        at_low, at_high = bottom & (bz == 0), (sub >= 4) & (bz == Z - 1)
+        inner, corner = [], []
         for a in range(3):
-            wa = [jnp.broadcast_to(w[3 * a + b], (8, CHUNK)) for b in range(3)]
-            inner.append(
-                jnp.where(
-                    dz == -1, wa[0], jnp.where(dz == 0, wa[1], jnp.where(dz == 1, wa[2], 0.0))
-                )
-            )
-            lower.append(jnp.where(bz == 0, wa[0], 0.0))
-            upper.append(jnp.where(bz == Z - 1, wa[2], 0.0))
-
-        def pick(at, three):
-            dx = at - bx
-            return jnp.where(
-                dx == -1, three[0], jnp.where(dx == 0, three[1], jnp.where(dx == 1, three[2], 0.0))
-            )
-
-        factors = [pick(x, inner) for x in list(range(X)) + [-1, X]]
-        factors += [pick(at, lower) for at in edge_x]
-        factors += [pick(at, upper) for at in edge_x]
-        totals = []
-        for d in range(3):
-            picked = jnp.dot(
-                split[d * SROWS : (d + 1) * SROWS, :], hot, preferred_element_type=jnp.float32
-            )
-            summed = factors[0] * picked[0:8]
-            for t in range(1, SROWS // 8):
-                summed = summed + factors[t] * picked[8 * t : 8 * t + 8]
-            totals.append(jnp.sum(summed, axis=0, keepdims=True))
-            grad[d : d + 1, where] = totals[d]
-        rows = jnp.concatenate(totals + [jnp.zeros((5, CHUNK), jnp.float32)])
-        top = rows.astype(jnp.bfloat16)
-        rest = (rows - top.astype(jnp.float32)).astype(jnp.bfloat16)
-        panels = jnp.broadcast_to(panel[:, where], (PANELS, CHUNK))
-        which = lax.broadcasted_iota(jnp.int32, (PANELS, CHUNK), 0) == panels
-        which = jnp.where(which, 1.0, 0.0).astype(jnp.bfloat16)
-        both = jnp.concatenate([top, rest])
-        return acc + lax.dot_general(
-            both, which, (((1,), (1,)), ((), ())), preferred_element_type=jnp.float32
-        )
-
-    acc = lax.fori_loop(
-        0, cell.shape[1] // CHUNK, chunk, jnp.zeros((16, PANELS), jnp.float32)
+            wa = w[3 * a : 3 * a + 3]
+            inner.append(pick(dz, wa))
+            corner.append(jnp.where(at_low, wa[0], jnp.where(at_high, wa[2], 0.0)))
+        factors = [
+            jnp.where(bx == 0, inner[0], 0.0),
+            jnp.where(bx == X - 1, inner[2], 0.0),
+            jnp.where(bx == 0, inner[1], jnp.where(bx == 1, inner[0], 0.0)),
+            jnp.where(bx == X - 1, inner[1], jnp.where(bx == X - 2, inner[2], 0.0)),
+            pick(corner_x - bx, corner),
+        ]
+        sums = []
+        for d, tile in enumerate(gathered(split, rows, hot[:, where], factors)):
+            sums.append(jnp.sum(acc_in[d, :, where] + tile, axis=0, keepdims=True))
+            grad[d : d + 1, where] = sums[d]
+        sums = jnp.concatenate(sums + [jnp.zeros((5, CHUNK), jnp.float32)])
+        top = sums.astype(jnp.bfloat16)
+        rest = (sums - top.astype(jnp.float32)).astype(jnp.bfloat16)
+        totals[:, where] = jnp.concatenate([top, rest])
+        return carry
+
+    lax.fori_loop(0, cell.shape[1] // CHUNK, chunk, 0, unroll=UNROLL_C)
+    total = lax.dot_general(
+        totals[...], which[...], (((1,), (1,)), ((), ())), preferred_element_type=jnp.float32
     )
-    result = acc[0:3] + acc[8:11]
+    result = total[0:3] + total[8:11]
     for n in range(partial.shape[0]):
         partial[n] = result
-    for copy in copies:
-        copy.wait()
 
 
 def ring(axis, step):
@@ -519,76 +603,91 @@
     return pl.BlockSpec((19, 2, Z, Y), lambda i: (0, index, 0, 0))
 
 
-def local(stored, adjoint_in, marker_cell, marker_weight, marker_panel, marker_count):
+def local(stored, adj, marker_cell, marker_weight, marker_panel, marker_count):
     slots = marker_cell.shape[0]
     whole = pl.BlockSpec(memory_space=pltpu.VMEM)
-    to_low, to_high = pl.pallas_call(
+    hbm = pl.BlockSpec(memory_space=pltpu.HBM)
+    any_space = pl.BlockSpec(memory_space=pl.ANY)
+    cell, panel = marker_cell.reshape(1, slots), marker_panel.reshape(1, slots)
+    to_low, to_high, mom, rho = pl.pallas_call(
         pack_z,
-        out_shape=(shape(ZROWS, Y), shape(ZROWS, Y)),
-        compiler_params=PARAMS,
+        out_shape=(
+            shape(ZROWS, Y),
+            shape(ZROWS, Y),
+            shape(3, X * Z, Y),
+            shape(X * Z, Y),
+        ),
+        in_specs=[hbm, hbm],
+        out_specs=(whole,) * 4,
+        scratch_shapes=[
+            pltpu.VMEM(stored.shape, stored.dtype),
+            pltpu.VMEM(adj.shape, adj.dtype),
+            pltpu.SemaphoreType.DMA((2, GROUPS)),
+        ],
+        compiler_params=pltpu.CompilerParams(vmem_limit_bytes=52 * 1024 * 1024),
         cost_estimate=cost(5_000_000, 4_000_000),
-    )(stored, adjoint_in)
+    )(stored, adj)
     low = lax.ppermute(to_high, "gz", ring("gz", 1))
     high = lax.ppermute(to_low, "gz", ring("gz", -1))
+    weight, hot, acc = pl.pallas_call(
+        stage_a,
+        out_shape=(
+            shape(9, slots),
+            jax.ShapeDtypeStruct((Y, slots), jnp.bfloat16),
+            shape(3, 8, slots),
+        ),
+        in_specs=[pl.BlockSpec(memory_space=pltpu.SMEM)] + [whole] * 4,
+        scratch_shapes=[pltpu.VMEM((6 * X * Z, Y), jnp.bfloat16)],
+        compiler_params=PARAMS,
+        cost_estimate=cost(800_000_000, 2_000_000),
+    )(marker_count, mom, rho, cell, marker_weight)
     to_left, to_right = pl.pallas_call(
         pack_x,
         grid=(1,),
         out_shape=(shape(XROWS, Y), shape(XROWS, Y)),
-        in_specs=[pair(True), pair(False), pair(True), pair(False)] + [whole] * 4,
+        in_specs=[pair(True), pair(False), pair(True), pair(False)] + [whole] * 4 + [any_space],
         compiler_params=PARAMS,
         cost_estimate=cost(1_000_000, 2_000_000),
-    )(stored, stored, adjoint_in, adjoint_in, to_low, to_high, low, high)
+    )(stored, stored, adj, adj, to_low, to_high, low, high, acc)
     left = lax.ppermute(to_right, "gx", ring("gx", 1))
     right = lax.ppermute(to_left, "gx", ring("gx", -1))
-    out, sens = pl.pallas_call(
+    acc, which = pl.pallas_call(
+        stage_b,
+        out_shape=(shape(3, 8, slots), jax.ShapeDtypeStruct((PANELS, slots), jnp.bfloat16)),
+        scratch_shapes=[pltpu.VMEM((24 * X, Y), jnp.bfloat16)],
+        compiler_params=PARAMS,
+        cost_estimate=cost(400_000_000, 2_000_000),
+    )(to_low, to_high, low, high, cell, panel, weight, hot, acc)
+    out = pl.pallas_call(
         interior,
-        out_shape=(shape(19, X, Z, Y), shape(3, X * Z, Y)),
+        out_shape=shape(19, X, Z, Y),
         compiler_params=PARAMS,
         cost_estimate=cost(10_000_000, 7_000_000),
-    )(stored, adjoint_in, low, high)
-    any_space = pl.BlockSpec(memory_space=pl.ANY)
-    out, grad, partial = pl.pallas_call(
-        finish,
+    )(stored, adj, low, high)
+    grad, partial = pl.pallas_call(
+        stage_c,
+        out_shape=(shape(3, slots), shape(lax.axis_size("gz"), 3, PANELS)),
+        scratch_shapes=[
+            pltpu.VMEM((6 * 48, Y), jnp.bfloat16),
+            pltpu.VMEM((16, slots), jnp.bfloat16),
+        ],
+        compiler_params=PARAMS,
+        cost_estimate=cost(300_000_000, 2_000_000),
+    )(rho, to_left, to_right, low, high, left, right, cell, weight, hot, which, acc)
+    out = pl.pallas_call(
+        borders,
         grid=(1,),
-        out_shape=(
-            shape(19, X, Z, Y),
-            shape(3, slots),
-            shape(lax.axis_size("gz"), 3, PANELS),
-        ),
-        in_specs=[pl.BlockSpec(memory_space=pltpu.SMEM)]
-        + [pair(True), pair(False), pair(True), pair(False)]
-        + [whole] * 12
-        + [any_space],
-        out_specs=(any_space, whole, whole),
+        out_shape=shape(19, X, Z, Y),
+        in_specs=[pair(True), pair(False), pair(True), pair(False)] + [whole] * 4 + [any_space],
+        out_specs=any_space,
         scratch_shapes=[
             pltpu.VMEM((2, 19, Z, Y), jnp.float32),
-            pltpu.VMEM((3 * SROWS, Y), jnp.float32),
-            pltpu.VMEM((3 * SROWS, 2 * Y), jnp.bfloat16),
             pltpu.SemaphoreType.DMA((2,)),
         ],
-        input_output_aliases={17: 0},
+        input_output_aliases={8: 0},
         compiler_params=PARAMS,
-        cost_estimate=cost(1_000_000_000, 4_000_000),
-    )(
-        marker_count,
-        stored,
-        stored,
-        adjoint_in,
-        adjoint_in,
-        to_low,
-        to_high,
-        low,
-        high,
-        to_left,
-        to_right,
-        left,
-        right,
-        sens,
-        marker_cell.reshape(1, slots),
-        marker_panel.reshape(1, slots),
-        marker_weight,
-        out,
-    )
+        cost_estimate=cost(1_000_000, 2_000_000),
+    )(stored, stored, adj, adj, low, high, left, right, out)
     total = jnp.sum(lax.all_to_all(partial, "gz", 0, 0), axis=0)
     copies = jnp.broadcast_to(total[None], (lax.axis_size("gx"),) + total.shape)
     total = jnp.sum(lax.all_to_all(copies, "gx", 0, 0), axis=0)

time: 60 us -> 53.7 us (0.90)
  blocking collectives: 26.3 us -> 10.7 us
  starting transfers between devices: 11.7 us -> 19.4 us
  Pallas kernels: 9.64 us -> 12.2 us
  waiting for transfers between devices: 7.1 us -> 6.21 us
    all_to_all x1 -> x0, blocking collectives: 11.5 us -> none  [local(): total = jnp.sum(lax.all_to_all(copies, 'gx', 0, 0), axis=0)]
    all_to_all x0 -> x1, starting transfers between devices: none -> 7.65 us  [local(): total = jnp.sum(lax.all_to_all(copies, 'gx', 0, 0), axis=0)]
    ppermute x1, waiting for transfers between devices: 4.4 us -> 0.01 us  [local(): left = lax.ppermute(to_right, 'gx', ring('gx', 1))]
    all_to_all x1, blocking collectives: 14.9 us -> 10.7 us  [local(): total = jnp.sum(lax.all_to_all(partial, 'gz', 0, 0), axis=0)]
    all_to_all x0 -> x1, waiting for transfers between devices: none -> 3.51 us  [local(): total = jnp.sum(lax.all_to_all(copies, 'gx', 0, 0), axis=0)]
    ppermute x1, starting transfers between devices: 0.01 us -> 3.1 us  [local(): low = lax.ppermute(to_high, 'gz', ring('gz', 1))]
    ppermute x1, starting transfers between devices: 3.32 us -> 0.3 us  [local(): high = lax.ppermute(to_low, 'gz', ring('gz', -1))]
    ppermute x1, starting transfers between devices: 8.37 us -> 5.59 us  [local(): right = lax.ppermute(to_left, 'gx', ring('gx', -1))]
  transfers between devices with their start and end apart: 4 -> 5, of which waited for: 2 -> 3; matrix products, arithmetic and copies ran while one was open for 0% -> 0% of each run, Pallas kernels for 5% -> 16%
where the time goes in v2:
time: 53.7 us; the launch traced here: 53.4 us
  starting transfers between devices  19.4 us (36%)
  Pallas kernels  12.2 us (23%)
  blocking collectives  10.7 us (20%)
  waiting for transfers between devices  6.21 us (12%)
  local copies, waits for them, and re-layouts  2.81 us (5%)
  between operations  1.4 us (3%)
  other arithmetic  0.63 us (1%)
    all_to_all x1, blocking collectives, local(): total = jnp.sum(lax.all_to_all(partial, 'gz', 0, 0), axis=0)  10.7 us
    all_to_all x1, starting transfers between devices, local(): total = jnp.sum(lax.all_to_all(copies, 'gx', 0, 0), axis=0)  7.65 us
    ppermute x1, starting transfers between devices, local(): right = lax.ppermute(to_left, 'gx', ring('gx', -1))  5.59 us
    all_to_all x1, waiting for transfers between devices, local(): total = jnp.sum(lax.all_to_all(copies, 'gx', 0, 0), axis=0)  3.51 us
    pallas_call x1, Pallas kernels, local(): pl.pallas_call(interior, out_shape=shape(19, X, Z, Y), compiler_params=PA...  3.18 us
    ppermute x1, starting transfers between devices, local(): low = lax.ppermute(to_high, 'gz', ring('gz', 1))  3.1 us
    ppermute x1, starting transfers between devices, local(): left = lax.ppermute(to_right, 'gx', ring('gx', 1))  2.77 us
    pallas_call x1, Pallas kernels, local(): pl.pallas_call(pack_z, out_shape=(shape(ZROWS, Y), shape(ZROWS, Y), shape...  2.46 us
  transfers between devices with their start and end apart: 5, of which 3 were waited for; matrix products, arithmetic and copies ran while one was open for 0% of the time, Pallas kernels for 16%

profile of v2, /device:TPU:1, one launch (start us, length us, event | category | flops | bytes accessed | tf_op | source)
XLA Modules:
  0.0 53.4 jit_solution(8932733936933244154)
XLA Ops:
  0.6 0.0 copy-start.1
  0.7 2.5 %shard_map.85 = (f32[152,256]{1,0:T(8,128)S(1)}, f32[152,256]{1,0:T(8,128)S(1)}, f32[3,128,256]{2,1,0:T(8,128)S(1)}, f32[128,256]{1,0:T(8,128)S(1)}) custom-call(bf16[19,16,8,256]{3,2,1,0:T(8,128)(2,1)} %stored_b.3, f32[19,16,8,256]{3,2,1,0:T(8,128)} %adj_b.3), custom_call_target="tpu_custom_call" | custom-call | flops 5000000 | bytes 4000000 | tf_op jit(solution)/shard_map/pallas_call | solution.py:612
  3.1 3.1 %collective-permute-start = (f32[152,256]{1,0:T(8,128)S(1)}, f32[152,256]{1,0:T(8,128)S(1)}, u32[]{:S(2)}, u32[]{:S(2)}) collective-permute-start(f32[152,256]{1,0:T(8,128)S(1)} %get-tuple-element.16.sent_high), channel_id=1, source_target_pairs={{0,1},{1,2},{2,3},{3,4},{4,5},{5,6},{6,7},{7,8},{8,9},{9,10},{10,1... | collective-permute-start | bytes 466952 | tf_op jit(solution)/shard_map/ppermute | solution.py:630
  6.2 0.3 collective-permute-start.1
  7.2 0.0 copy-start.5
  7.2 0.9 %copy-done.5 = f32[9,2048]{1,0:T(8,128)S(1)} copy-done((f32[9,2048]{1,0:T(8,128)S(1)}, f32[9,2048]{1,0:T(8,128)}, u32[]{:S(2)}) %copy-start.5) | copy-done | bytes 73752
  8.1 2.3 %shard_map.86 = (f32[9,2048]{1,0:T(8,128)S(1)}, bf16[256,2048]{1,0:T(8,128)(2,1)S(1)}, f32[3,8,2048]{2,1,0:T(8,128)S(1)}) custom-call(s32[1]{0:T(128)S(6)} %copy.13.count, f32[3,128,256]{2,1,0:T(8,128)S(1)} %get-tuple-element.18.mom, f32[128,256]{1,0:T(8,128)S(1)} %get-tuple-element.19.rho, s32[1,2048]{1,0:T(1,128)S(1)} %bitcast.2, f32[9,2048]{1,0:T(8,128)S(1)} %copy-done.5), custom_call_target="tpu_custom_call" | custom-call | flops 800000000 | bytes 2000000 | tf_op jit(solution)/shard_map/pallas_call | solution.py:632
  10.4 0.0 collective-permute-done.low
  10.4 1.2 %collective-permute-done.1.high = f32[152,256]{1,0:T(8,128)S(1)} collective-permute-done((f32[152,256]{1,0:T(8,128)S(1)}, f32[152,256]{1,0:T(8,128)S(1)}, u32[]{:S(2)}, u32[]{:S(2)}) %collective-permute-start.1) | collective-permute-done | bytes 155680 | tf_op jit(solution)/shard_map/ppermute | solution.py:631
  11.6 0.1 shard_map.87
  11.7 2.8 %collective-permute-start.2 = (f32[88,256]{1,0:T(8,128)S(1)}, f32[88,256]{1,0:T(8,128)S(1)}, u32[]{:S(2)}, u32[]{:S(2)}) collective-permute-start(f32[88,256]{1,0:T(8,128)S(1)} %get-tuple-element.21.sent_right), channel_id=1, source_target_pairs={{0,16},{16,32},{32,48},{48,64},{64,80},{80,96},{96,112},{112,128},... | collective-permute-start | bytes 270344 | tf_op jit(solution)/shard_map/ppermute | solution.py:652
  14.5 5.6 %collective-permute-start.3 = (f32[88,256]{1,0:T(8,128)S(1)}, f32[88,256]{1,0:T(8,128)S(1)}, u32[]{:S(2)}, u32[]{:S(2)}) collective-permute-start(f32[88,256]{1,0:T(8,128)S(1)} %get-tuple-element.22.sent_left), channel_id=1, source_target_pairs={{0,240},{16,0},{32,16},{48,32},{64,48},{80,64},{96,80},{112,96},{1... | collective-permute-start | bytes 270344 | tf_op jit(solution)/shard_map/ppermute | solution.py:653
  20.1 2.0 %shard_map.90 = (f32[3,8,2048]{2,1,0:T(8,128)S(1)}, bf16[128,2048]{1,0:T(8,128)(2,1)S(1)}) custom-call(f32[152,256]{1,0:T(8,128)S(1)} %get-tuple-element.17.sent_low, f32[152,256]{1,0:T(8,128)S(1)} %get-tuple-element.16.sent_high, f32[152,256]{1,0:T(8,128)S(1)} %collective-permute-done.low, f32[152,256]{1,0:T(8,128)S(1)} %collective-permute-done.1.high, ...), custom_call_target="tpu_custom_call" | custom-call | flops 400000000 | bytes 2000000 | tf_op jit(solution)/shard_map/pallas_call | solution.py:654
  22.1 1.5 %collective-permute-done.3.right = f32[88,256]{1,0:T(8,128)S(1)} collective-permute-done((f32[88,256]{1,0:T(8,128)S(1)}, f32[88,256]{1,0:T(8,128)S(1)}, u32[]{:S(2)}, u32[]{:S(2)}) %collective-permute-start.3) | collective-permute-done | bytes 90144 | tf_op jit(solution)/shard_map/ppermute | solution.py:653
  23.7 1.3 %shard_map.91 = (f32[3,2048]{1,0:T(4,128)}, f32[16,3,128]{2,1,0:T(4,128)S(1)}) custom-call(f32[128,256]{1,0:T(8,128)S(1)} %get-tuple-element.19.rho, f32[88,256]{1,0:T(8,128)S(1)} %get-tuple-element.22.sent_left, f32[88,256]{1,0:T(8,128)S(1)} %get-tuple-element.21.sent_right, f32[152,256]{1,0:T(8,128)S(1)} %collective-permute-done.low, ...), custom_call_target="tpu_custom_call" | custom-call | flops 300000000 | bytes 2000000 | tf_op jit(solution)/shard_map/pallas_call | solution.py:667
  24.9 10.7 %all_to_all.10 = f32[16,3,128]{2,1,0:T(4,128)S(1)} all-to-all(f32[16,3,128]{2,1,0:T(4,128)S(1)} %get-tuple-element.28), channel_id=1, replica_groups=mesh['gx'=16,'gz'=16] {'gz'}, dimensions={0} | all-to-all | bytes 49152 | tf_op jit(solution)/shard_map/all_to_all | solution.py:691
  35.7 0.6 %broadcast_in_dim.2 = f32[16,3,128]{2,1,0:T(4,128)} broadcast(f32[3,128]{1,0:T(4,128)S(1)} %reduce_sum.18), dimensions={1,2} | broadcast | bytes 26112 | tf_op jit(solution)/shard_map/broadcast_in_dim | solution.py:692
  36.3 7.6 %all-to-all-start.1 = ((f32[16,3,128]{2,1,0:T(4,128)}), f32[16,3,128]{2,1,0:T(4,128)S(1)}, u32[]{:S(2)}, u32[]{:S(2)}) async-start(f32[16,3,128]{2,1,0:T(4,128)} %broadcast_in_dim.2), calls=%async_computation.1 | async-start | bytes 65536 | tf_op jit(solution)/shard_map/all_to_all | solution.py:693
  44.0 0.0 copy-start.2
  44.0 1.3 %copy-done.2 = bf16[19,16,8,256]{3,2,1,0:T(8,128)(2,1)S(1)} copy-done((bf16[19,16,8,256]{3,2,1,0:T(8,128)(2,1)S(1)}, bf16[19,16,8,256]{3,2,1,0:T(8,128)(2,1)}, u32[]{:S(2)}) %copy-start.2) | copy-done | bytes 1245208
  45.3 3.2 %shard_map.88.out_in = f32[19,16,8,256]{3,2,1,0:T(8,128)} custom-call(bf16[19,16,8,256]{3,2,1,0:T(8,128)(2,1)S(1)} %copy-done.2, f32[19,16,8,256]{3,2,1,0:T(8,128)S(1)} %copy-done, f32[152,256]{1,0:T(8,128)S(1)} %collective-permute-done.low, f32[152,256]{1,0:T(8,128)S(1)} %collective-permute-done.1.high), custom_call_target="tpu_custom_call" | custom-call | flops 10000000 | bytes 7000000 | tf_op jit(solution)/shard_map/pallas_call | solution.py:661
  48.4 0.9 %shard_map.89 = f32[19,16,8,256]{3,2,1,0:T(8,128)} custom-call(bf16[19,16,8,256]{3,2,1,0:T(8,128)(2,1)S(1)} %copy-done.2, bf16[19,16,8,256]{3,2,1,0:T(8,128)(2,1)S(1)} %copy-done.2, f32[19,16,8,256]{3,2,1,0:T(8,128)S(1)} %copy-done, f32[19,16,8,256]{3,2,1,0:T(8,128)S(1)} %copy-done, ...), custom_call_target="tpu_custom_call", output_to_operand_aliasing={{}: (8, {})} | custom-call | flops 1000000 | bytes 2000000 | tf_op jit(solution)/shard_map/pallas_call | solution.py:677
  49.3 3.5 %all-to-all-done.1 = f32[16,3,128]{2,1,0:T(4,128)S(1)} async-done(((f32[16,3,128]{2,1,0:T(4,128)}), f32[16,3,128]{2,1,0:T(4,128)S(1)}, u32[]{:S(2)}, u32[]{:S(2)}) %all-to-all-start.1) | async-done | bytes 24608 | tf_op jit(solution)/shard_map/all_to_all | solution.py:693
  52.8 0.6 %reduce_sum.19 = f32[3,128]{1,0:T(4,128)} reduce(f32[16,3,128]{2,1,0:T(4,128)S(1)} %all-to-all-done.1, f32[]{:T(128)} %constant.0.clone.1), dimensions={0}, to_apply=%region_1.0 | reduce | flops 5760 | bytes 26116 | tf_op jit(solution)/shard_map/reduce_sum | solution.py:693
  (9 shorter events, 0.0 us)
Async XLA Ops:
  0.6 10.9 %copy-start = (f32[19,16,8,256]{3,2,1,0:T(8,128)S(1)}, f32[19,16,8,256]{3,2,1,0:T(8,128)}, u32[]{:S(2)}) copy-start(f32[19,16,8,256]{3,2,1,0:T(8,128)} %adj_b.3) | copy-start | bytes 7471108
  0.6 10.9 %copy-start.1 = (bf16[19,16,8,256]{3,2,1,0:T(8,128)(2,1)S(1)}, bf16[19,16,8,256]{3,2,1,0:T(8,128)(2,1)}, u32[]{:S(2)}) copy-start(bf16[19,16,8,256]{3,2,1,0:T(8,128)(2,1)} %stored_b.3) | copy-start | bytes 3735556
  0.7 6.5 %copy-start.3 = (s32[2048]{0:T(1024)S(1)}, s32[2048]{0:T(1024)}, u32[]{:S(2)}) copy-start(s32[2048]{0:T(1024)} %param.8) | copy-start | bytes 24580
  3.1 7.3 %collective-permute-start = (f32[152,256]{1,0:T(8,128)S(1)}, f32[152,256]{1,0:T(8,128)S(1)}, u32[]{:S(2)}, u32[]{:S(2)}) collective-permute-start(f32[152,256]{1,0:T(8,128)S(1)} %get-tuple-element.16.sent_high), channel_id=1, source_target_pairs={{0,1},{1,2},{2,3},{3,4},{4,5},{5,6},{6,7},{7,8},{8,9},{9,10},{10,1... | collective-permute-start | bytes 466952 | tf_op jit(solution)/shard_map/ppermute | solution.py:630
  6.2 5.3 %collective-permute-start.1 = (f32[152,256]{1,0:T(8,128)S(1)}, f32[152,256]{1,0:T(8,128)S(1)}, u32[]{:S(2)}, u32[]{:S(2)}) collective-permute-start(f32[152,256]{1,0:T(8,128)S(1)} %get-tuple-element.17.sent_low), channel_id=1, source_target_pairs={{0,15},{1,0},{2,1},{3,2},{4,3},{5,4},{6,5},{7,6},{8,7},{9,8},{10,9... | collective-permute-start | bytes 466952 | tf_op jit(solution)/shard_map/ppermute | solution.py:631
  7.2 0.9 %copy-start.5 = (f32[9,2048]{1,0:T(8,128)S(1)}, f32[9,2048]{1,0:T(8,128)}, u32[]{:S(2)}) copy-start(f32[9,2048]{1,0:T(8,128)} %weight.1) | copy-start | bytes 221188
  11.6 8.5 %copy-start.4 = (s32[2048]{0:T(1024)S(1)}, s32[2048]{0:T(1024)}, u32[]{:S(2)}) copy-start(s32[2048]{0:T(1024)} %param.10) | copy-start | bytes 24580
  11.7 10.4 %collective-permute-start.2 = (f32[88,256]{1,0:T(8,128)S(1)}, f32[88,256]{1,0:T(8,128)S(1)}, u32[]{:S(2)}, u32[]{:S(2)}) collective-permute-start(f32[88,256]{1,0:T(8,128)S(1)} %get-tuple-element.21.sent_right), channel_id=1, source_target_pairs={{0,16},{16,32},{32,48},{48,64},{64,80},{80,96},{96,112},{112,128},... | collective-permute-start | bytes 270344 | tf_op jit(solution)/shard_map/ppermute | solution.py:652
  14.5 9.2 %collective-permute-start.3 = (f32[88,256]{1,0:T(8,128)S(1)}, f32[88,256]{1,0:T(8,128)S(1)}, u32[]{:S(2)}, u32[]{:S(2)}) collective-permute-start(f32[88,256]{1,0:T(8,128)S(1)} %get-tuple-element.22.sent_left), channel_id=1, source_target_pairs={{0,240},{16,0},{32,16},{48,32},{64,48},{80,64},{96,80},{112,96},{1... | collective-permute-start | bytes 270344 | tf_op jit(solution)/shard_map/ppermute | solution.py:653
  36.3 16.5 %all-to-all-start.1 = ((f32[16,3,128]{2,1,0:T(4,128)}), f32[16,3,128]{2,1,0:T(4,128)S(1)}, u32[]{:S(2)}, u32[]{:S(2)}) async-start(f32[16,3,128]{2,1,0:T(4,128)} %broadcast_in_dim.2), calls=%async_computation.1 | async-start | bytes 65536 | tf_op jit(solution)/shard_map/all_to_all | solution.py:693
  44.0 1.3 %copy-start.2 = (bf16[19,16,8,256]{3,2,1,0:T(8,128)(2,1)S(1)}, bf16[19,16,8,256]{3,2,1,0:T(8,128)(2,1)}, u32[]{:S(2)}) copy-start(bf16[19,16,8,256]{3,2,1,0:T(8,128)(2,1)} %stored_b.3) | copy-start | bytes 3735556

commit v3 on v2

--- a/solution.py
+++ b/solution.py
@@ -42,10 +42,16 @@
 ZROWS, Z_RHO, Z_MOM, Z_SPILL = 152, 80, 96, 144
 XROWS, X_MOM, X_RHO, X_EDGE, X_FAR = 88, 40, 64, 72, 80
 
+GX = ("y", "zh")
+GZ = ("x", "zl", "core")
+FIRST = ("core", "zh", "zl")
+SECOND = ("y", "x")
+
 CHUNK = 256
 UNROLL_C = 8
 GROUPS = 4
 STEP = X // GROUPS
+NEAR = (0, 1, X - 2, X - 1)
 
 
 def roll_y(tile, q):
@@ -112,30 +118,35 @@
 
 
 def ends():
-    gz = lax.axis_index("gz")
-    gx = lax.axis_index("gx")
-    gz_n, gx_n = lax.axis_size("gz"), lax.axis_size("gx")
+    gz, gx = lax.axis_index(GZ), lax.axis_index(GX)
+    gz_n, gx_n = lax.axis_size(GZ), lax.axis_size(GX)
     flag = lambda c: jnp.where(c, 1.0, 0.0).astype(jnp.float32)
     return flag(gz > 0), flag(gz < gz_n - 1), flag(gx > 0), flag(gx < gx_n - 1)
 
 
-def pack_z(stored_in, adj_in, to_low, to_high, mom_out, rho_out, stored, adj, sems):
+def column(adj, x):
+    g = [None] * 19
+    for q in range(1, 19):
+        at = x + STENCIL[q][0]
+        if 0 <= at < X:
+            g[q] = pulled_own(adj, q, at)
+    return first_moments(g)
+
+
+def pack_z(stored_in, adj_in, to_low, to_high, rho_out, stored, adj, sems):
     copies = []
     for n in range(GROUPS):
         part = pl.ds(n * STEP, STEP)
-        for k, (src, dst) in enumerate(((adj_in, adj), (stored_in, stored))):
-            copy = pltpu.make_async_copy(src.at[:, part], dst.at[:, part], sems.at[k, n])
+        group = []
+        for k, first in enumerate((0, Z - 2)):
+            at = (pl.ds(1, 18), part, pl.ds(first, 2))
+            group.append(pltpu.make_async_copy(adj_in.at[at], adj.at[at], sems.at[k, n]))
+        group.append(
+            pltpu.make_async_copy(stored_in.at[:, part], stored.at[:, part], sems.at[2, n])
+        )
+        for copy in group:
             copy.start()
-            copies.append(copy)
-
-    def column(x):
-        g = [None] * 19
-        for q in range(1, 19):
-            at = x + STENCIL[q][0]
-            if isinstance(at, int) and not 0 <= at < X:
-                continue
-            g[q] = pulled_own(adj, q, at)
-        return first_moments(g)
+        copies.append(group)
 
     def density(x):
         rho = stored[0, x].astype(jnp.float32)
@@ -149,20 +160,19 @@
             to_high[pl.ds(n * X + x, 1), :] = adj[Z_DOWN[n], x, Z - 1 : Z, :]
 
     def moments(x):
-        for d, mom in enumerate(column(x)):
-            mom_out[d, pl.ds(x * Z, Z), :] = mom
+        for d, mom in enumerate(column(adj, x)):
             to_low[pl.ds(Z_MOM + d * X + x, 1), :] = mom[0:1]
             to_high[pl.ds(Z_MOM + d * X + x, 1), :] = mom[Z - 1 : Z]
 
     for n in range(GROUPS):
-        copies[2 * n].wait()
-        copies[2 * n + 1].wait()
+        for copy in copies[n]:
+            copy.wait()
         first, last = n * STEP, (n + 1) * STEP
         for x in range(first, last):
             density(x)
         for x in range(max(first - 1, 0), last if n == GROUPS - 1 else last - 1):
             moments(x)
-    spill = [column(-1), column(X)]
+    spill = [column(adj, -1), column(adj, X)]
     zero = jnp.zeros((1, Y), jnp.float32)
     low_rows, high_rows = [], []
     for d in range(3):
@@ -199,41 +209,26 @@
     return a if b is None else a + b
 
 
-def pack_x(
-    stored_a,
-    stored_b,
-    adj_a,
-    adj_b,
-    sent_low,
-    sent_high,
-    low,
-    high,
-    after,
-    to_left,
-    to_right,
-):
+def pack_x(near, rho, sent_low, sent_high, low, high, after, to_left, to_right):
     del after
     low_on, high_on, _, _ = ends()
     edge_low, edge_high = edge_moments(sent_low, Z_UP), edge_moments(sent_high, Z_DOWN)
 
-    def side(out, adj, stored, x, plane, inner, away, skip):
+    def side(out, x, plane, inner, away, skip):
         for n, q in enumerate(away):
             out[n * Z : (n + 1) * Z, :] = pulled_z(
-                adj, q, x, low, high, plane, low_on, high_on
+                near, q, x, low, high, plane, low_on, high_on
             )
         g = [None] * 19
         for q in range(1, 19):
             step = STENCIL[q][0]
             if step == 0:
-                g[q] = pulled_z(adj, q, x, low, high, plane, low_on, high_on)
+                g[q] = pulled_z(near, q, x, low, high, plane, low_on, high_on)
             elif step != skip:
-                g[q] = pulled_z(adj, q, x + step, low, high, inner, low_on, high_on)
+                g[q] = pulled_z(near, q, x + step, low, high, inner, low_on, high_on)
         for d, mom in enumerate(first_moments(g)):
             out[X_MOM + d * Z : X_MOM + (d + 1) * Z, :] = mom
-        rho = stored[0, plane].astype(jnp.float32)
-        for q in range(1, 19):
-            rho = rho + stored[q, plane].astype(jnp.float32)
-        out[X_RHO : X_RHO + Z, :] = rho
+        out[X_RHO : X_RHO + Z, :] = rho[x * Z : (x + 1) * Z, :]
         beyond = 1 if x > 0 else 0
         edge, far = [], []
         for ref, own, on in ((low, edge_low, low_on), (high, edge_high, high_on)):
@@ -248,8 +243,8 @@
         far = far + [jnp.zeros((1, Y), jnp.float32)] * 2
         out[X_FAR : X_FAR + 8, :] = jnp.concatenate(far)
 
-    side(to_left, adj_a, stored_a, 0, 0, 1, X_UP, -1)
-    side(to_right, adj_b, stored_b, X - 1, 1, 0, X_DOWN, 1)
+    side(to_left, 0, 0, 1, X_UP, -1)
+    side(to_right, X - 1, 3, 2, X_DOWN, 1)
 
 
 def collide_transpose(f, g, emit):
@@ -316,56 +311,71 @@
         emit(q, along[STENCIL[q]] + (1.0 - OMEGA) * g[q])
 
 
-def interior(stored, adj, low, high, out):
-    low_on, high_on, _, _ = ends()
-
-    def body(x, carry):
+def output(
+    stored_in,
+    adj_in,
+    low,
+    high,
+    left,
+    right,
+    grad,
+    out_hbm,
+    grad_hbm,
+    stored,
+    adj,
+    out,
+    in_sems,
+    out_sems,
+):
+    low_on, high_on, left_on, right_on = ends()
+    reads, writes = [], []
+    for n in range(GROUPS):
+        part = pl.ds(n * STEP, STEP)
+        for k, (src, dst) in enumerate(((adj_in, adj), (stored_in, stored))):
+            copy = pltpu.make_async_copy(src.at[:, part], dst.at[:, part], in_sems.at[k, n])
+            copy.start()
+            reads.append(copy)
+    copy = pltpu.make_async_copy(grad, grad_hbm, out_sems.at[GROUPS])
+    copy.start()
+    writes.append(copy)
+
+    def plane(x, taken=(), ref=None, on=None):
         f = [stored[q, x].astype(jnp.float32) for q in range(19)]
         g = []
         for q in range(19):
             at = x + STENCIL[q][0]
-            g.append(pulled_z(adj, q, at, low, high, at, low_on, high_on))
-
-        def emit(q, value):
-            out[q, x] = value
-
-        collide_transpose(f, g, emit)
-        return carry
-
-    lax.fori_loop(1, X - 1, body, 0)
-    zero = jnp.zeros((Z, Y), jnp.float32)
-    for q in range(19):
-        out[q, 0] = zero
-        out[q, X - 1] = zero
-
-
-def borders(stored_a, stored_b, adj_a, adj_b, low, high, left, right, out_in, out, planes, sems):
-    del out_in
-    low_on, high_on, left_on, right_on = ends()
-    copies = []
-    for x, adj, stored, plane, inner, taken, ref, on in (
-        (0, adj_a, stored_a, 0, 1, X_DOWN, left, left_on),
-        (X - 1, adj_b, stored_b, 1, 0, X_UP, right, right_on),
-    ):
-        f = [stored[q, plane].astype(jnp.float32) for q in range(19)]
-        g = []
-        for q in range(19):
-            step = STENCIL[q][0]
             if q in taken:
                 n = taken.index(q)
                 g.append(ref[n * Z : (n + 1) * Z, :] * on)
             else:
-                at = plane if step == 0 else inner
-                g.append(pulled_z(adj, q, x + step, low, high, at, low_on, high_on))
-
-        def emit(q, value, plane=plane):
-            planes[plane, q] = value
+                g.append(pulled_z(adj, q, at, low, high, at, low_on, high_on))
+
+        def emit(q, value):
+            out[q, x] = value
 
         collide_transpose(f, g, emit)
-        copy = pltpu.make_async_copy(planes.at[plane], out.at[:, x], sems.at[plane])
+
+    def body(x, carry):
+        plane(x)
+        return carry
+
+    done = 0
+    for n in range(GROUPS):
+        reads[2 * n].wait()
+        reads[2 * n + 1].wait()
+        ready = (n + 1) * STEP - 1
+        if n == 0:
+            plane(0, X_DOWN, left, left_on)
+        lax.fori_loop(max(done, 1), ready, body, 0)
+        if n == GROUPS - 1:
+            plane(X - 1, X_UP, right, right_on)
+            ready = X
+        part = pl.ds(done, ready - done)
+        copy = pltpu.make_async_copy(out.at[:, part], out_hbm.at[:, part], out_sems.at[n])
         copy.start()
-        copies.append(copy)
-    for copy in copies:
+        writes.append(copy)
+        done = ready
+    for copy in writes:
         copy.wait()
 
 
@@ -415,12 +425,15 @@
     return [jnp.broadcast_to(weight[s : s + 1, where], (8, CHUNK)) for s in range(9)]
 
 
-def stage_a(count, mom, rho, cell, weight, live_weight, hot, acc, split):
+def stage_a(count, adj, rho, cell, weight, live_weight, hot, acc, near, split):
     rows = X * Z
+    for k, x in enumerate(NEAR):
+        near[:, k] = adj[:, x]
     for x in range(0, X, 2):
         scale = 3.0 * rho[x * Z : (x + 2) * Z, :]
+        first, second = column(adj, x), column(adj, x + 1)
         for d in range(3):
-            put(split, d * rows + x * Z, scale * mom[d, x * Z : (x + 2) * Z, :])
+            put(split, d * rows + x * Z, scale * jnp.concatenate([first[d], second[d]]))
     lanes = lax.broadcasted_iota(jnp.int32, (9, CHUNK), 1)
 
     def chunk(c, carry):
@@ -440,7 +453,7 @@
             acc[d, :, where] = tile
         return carry
 
-    lax.fori_loop(0, cell.shape[1] // CHUNK, chunk, 0)
+    lax.fori_loop(0, cell.shape[1] // CHUNK, chunk, 0, unroll=4)
 
 
 def stage_b(
@@ -484,7 +497,7 @@
         which[:, where] = jnp.where(match, 1.0, 0.0).astype(jnp.bfloat16)
         return carry
 
-    lax.fori_loop(0, cell.shape[1] // CHUNK, chunk, 0)
+    lax.fori_loop(0, cell.shape[1] // CHUNK, chunk, 0, unroll=4)
 
 
 def stage_c(
@@ -588,6 +601,8 @@
 
 
 PARAMS = pltpu.CompilerParams(vmem_limit_bytes=48 * 1024 * 1024)
+FIRST_BIG = pltpu.CompilerParams(vmem_limit_bytes=53 * 1024 * 1024)
+BIG = pltpu.CompilerParams(vmem_limit_bytes=52 * 1024 * 1024)
 
 
 def cost(flops, moved):
@@ -598,9 +613,9 @@
     return jax.ShapeDtypeStruct(dims, jnp.float32)
 
 
-def pair(low):
-    index = 0 if low else X // 2 - 1
-    return pl.BlockSpec((19, 2, Z, Y), lambda i: (0, index, 0, 0))
+def summed(parts, count):
+    total = jnp.sum(parts, axis=0)
+    return jnp.broadcast_to(total[None], (count,) + total.shape)
 
 
 def local(stored, adj, marker_cell, marker_weight, marker_panel, marker_count):
@@ -609,48 +624,47 @@
     hbm = pl.BlockSpec(memory_space=pltpu.HBM)
     any_space = pl.BlockSpec(memory_space=pl.ANY)
     cell, panel = marker_cell.reshape(1, slots), marker_panel.reshape(1, slots)
-    to_low, to_high, mom, rho = pl.pallas_call(
+    to_low, to_high, rho = pl.pallas_call(
         pack_z,
         out_shape=(
             shape(ZROWS, Y),
             shape(ZROWS, Y),
-            shape(3, X * Z, Y),
             shape(X * Z, Y),
         ),
         in_specs=[hbm, hbm],
-        out_specs=(whole,) * 4,
+        out_specs=(whole,) * 3,
         scratch_shapes=[
             pltpu.VMEM(stored.shape, stored.dtype),
             pltpu.VMEM(adj.shape, adj.dtype),
-            pltpu.SemaphoreType.DMA((2, GROUPS)),
+            pltpu.SemaphoreType.DMA((3, GROUPS)),
         ],
-        compiler_params=pltpu.CompilerParams(vmem_limit_bytes=52 * 1024 * 1024),
+        compiler_params=FIRST_BIG,
         cost_estimate=cost(5_000_000, 4_000_000),
     )(stored, adj)
-    low = lax.ppermute(to_high, "gz", ring("gz", 1))
-    high = lax.ppermute(to_low, "gz", ring("gz", -1))
-    weight, hot, acc = pl.pallas_call(
+    low = lax.ppermute(to_high, GZ, ring(GZ, 1))
+    high = lax.ppermute(to_low, GZ, ring(GZ, -1))
+    weight, hot, acc, near = pl.pallas_call(
         stage_a,
         out_shape=(
             shape(9, slots),
             jax.ShapeDtypeStruct((Y, slots), jnp.bfloat16),
             shape(3, 8, slots),
+            shape(19, len(NEAR), Z, Y),
         ),
         in_specs=[pl.BlockSpec(memory_space=pltpu.SMEM)] + [whole] * 4,
         scratch_shapes=[pltpu.VMEM((6 * X * Z, Y), jnp.bfloat16)],
         compiler_params=PARAMS,
         cost_estimate=cost(800_000_000, 2_000_000),
-    )(marker_count, mom, rho, cell, marker_weight)
+    )(marker_count, adj, rho, cell, marker_weight)
     to_left, to_right = pl.pallas_call(
         pack_x,
-        grid=(1,),
         out_shape=(shape(XROWS, Y), shape(XROWS, Y)),
-        in_specs=[pair(True), pair(False), pair(True), pair(False)] + [whole] * 4 + [any_space],
+        in_specs=[whole] * 6 + [any_space],
         compiler_params=PARAMS,
         cost_estimate=cost(1_000_000, 2_000_000),
-    )(stored, stored, adj, adj, to_low, to_high, low, high, acc)
-    left = lax.ppermute(to_right, "gx", ring("gx", 1))
-    right = lax.ppermute(to_left, "gx", ring("gx", -1))
+    )(near, rho, to_low, to_high, low, high, acc)
+    left = lax.ppermute(to_right, GX, ring(GX, 1))
+    right = lax.ppermute(to_left, GX, ring(GX, -1))
     acc, which = pl.pallas_call(
         stage_b,
         out_shape=(shape(3, 8, slots), jax.ShapeDtypeStruct((PANELS, slots), jnp.bfloat16)),
@@ -658,15 +672,9 @@
         compiler_params=PARAMS,
         cost_estimate=cost(400_000_000, 2_000_000),
     )(to_low, to_high, low, high, cell, panel, weight, hot, acc)
-    out = pl.pallas_call(
-        interior,
-        out_shape=shape(19, X, Z, Y),
-        compiler_params=PARAMS,
-        cost_estimate=cost(10_000_000, 7_000_000),
-    )(stored, adj, low, high)
     grad, partial = pl.pallas_call(
         stage_c,
-        out_shape=(shape(3, slots), shape(lax.axis_size("gz"), 3, PANELS)),
+        out_shape=(shape(3, slots), shape(lax.axis_size(FIRST), 3, PANELS)),
         scratch_shapes=[
             pltpu.VMEM((6 * 48, Y), jnp.bfloat16),
             pltpu.VMEM((16, slots), jnp.bfloat16),
@@ -674,38 +682,41 @@
         compiler_params=PARAMS,
         cost_estimate=cost(300_000_000, 2_000_000),
     )(rho, to_left, to_right, low, high, left, right, cell, weight, hot, which, acc)
-    out = pl.pallas_call(
-        borders,
-        grid=(1,),
-        out_shape=shape(19, X, Z, Y),
-        in_specs=[pair(True), pair(False), pair(True), pair(False)] + [whole] * 4 + [any_space],
-        out_specs=any_space,
+    out, grad = pl.pallas_call(
+        output,
+        out_shape=(shape(19, X, Z, Y), shape(3, slots)),
+        in_specs=[hbm, hbm] + [whole] * 5,
+        out_specs=(hbm, hbm),
         scratch_shapes=[
-            pltpu.VMEM((2, 19, Z, Y), jnp.float32),
-            pltpu.SemaphoreType.DMA((2,)),
+            pltpu.VMEM(stored.shape, stored.dtype),
+            pltpu.VMEM(adj.shape, adj.dtype),
+            pltpu.VMEM(adj.shape, adj.dtype),
+            pltpu.SemaphoreType.DMA((2, GROUPS)),
+            pltpu.SemaphoreType.DMA((GROUPS + 1,)),
         ],
-        input_output_aliases={8: 0},
-        compiler_params=PARAMS,
-        cost_estimate=cost(1_000_000, 2_000_000),
-    )(stored, stored, adj, adj, low, high, left, right, out)
-    total = jnp.sum(lax.all_to_all(partial, "gz", 0, 0), axis=0)
-    copies = jnp.broadcast_to(total[None], (lax.axis_size("gx"),) + total.shape)
-    total = jnp.sum(lax.all_to_all(copies, "gx", 0, 0), axis=0)
+        compiler_params=BIG,
+        cost_estimate=cost(10_000_000, 7_000_000),
+    )(stored, adj, low, high, left, right, grad)
+    partial = summed(lax.all_to_all(partial, FIRST, 0, 0), lax.axis_size(SECOND))
+    total = jnp.sum(lax.all_to_all(partial, SECOND, 0, 0), axis=0)
     return (out, grad, total)
 
 
 def solution(mesh):
+    split = jax.sharding.Mesh(
+        mesh.devices.reshape(4, 4, 4, 2, 2), ("y", "zh", "x", "zl", "core")
+    )
     return jax.shard_map(
         local,
-        mesh=mesh,
+        mesh=split,
         in_specs=(
-            P(None, "gx", "gz", None),
-            P(None, "gx", "gz", None),
-            P(("gx", "gz")),
-            P(None, ("gx", "gz")),
-            P(("gx", "gz")),
-            P(("gx", "gz")),
+            P(None, GX, GZ, None),
+            P(None, GX, GZ, None),
+            P(GX + GZ),
+            P(None, GX + GZ),
+            P(GX + GZ),
+            P(GX + GZ),
         ),
-        out_specs=(P(None, "gx", "gz", None), P(None, ("gx", "gz")), P()),
+        out_specs=(P(None, GX, GZ, None), P(None, GX + GZ), P()),
         check_vma=False,
     )

time: 53.7 us -> 51.2 us (0.953)
  Pallas kernels: 12.2 us -> 9.91 us
  local copies, waits for them, and re-layouts: 2.81 us -> 0.64 us
  blocking collectives: 10.7 us -> 12.4 us
  waiting for transfers between devices: 6.21 us -> 7.51 us
  starting transfers between devices: 19.4 us -> 18.5 us
    ppermute x4, waiting for transfers between devices: 2.7 us -> 5.13 us  [the longest x1 2.61 us: local(): high = lax.ppermute(to_low, GZ, ring(GZ, -1))]
    unnamed x12 -> x10, local copies, waits for them, and re-layouts: 2.21 us -> 0.03 us
    all_to_all x1, blocking collectives: 10.7 us -> 12.4 us  [local(): lax.all_to_all(partial, FIRST, 0, 0)]
    all_to_all x1, waiting for transfers between devices: 3.51 us -> 2.38 us  [local(): total = jnp.sum(lax.all_to_all(partial, SECOND, 0, 0), axis=0)]
    pallas_call x1, Pallas kernels: 2.04 us -> 1.05 us  [local(): pl.pallas_call(stage_b, out_shape=(shape(3, 8, slots), jax.ShapeDtypeStru...]
    all_to_all x1, starting transfers between devices: 7.65 us -> 6.72 us  [local(): total = jnp.sum(lax.all_to_all(partial, SECOND, 0, 0), axis=0)]
    pallas_call x4 -> x3, Pallas kernels: 5.44 us -> 4.95 us  [the longest x1 4.05 us: local(): pl.pallas_call(output, out_shape=(shape(19, X, Z, Y), shape(3, slots)), i...]
  transfers between devices with their start and end apart: 5 -> 5, of which waited for: 3 -> 4; matrix products, arithmetic and copies ran while one was open for 0% -> 0% of each run, Pallas kernels for 16% -> 13%
where the time goes in v3:
time: 51.2 us; the launch traced here: 51 us
  starting transfers between devices  18.5 us (36%)
  blocking collectives  12.4 us (24%)
  Pallas kernels  9.91 us (19%)
  waiting for transfers between devices  7.51 us (15%)
  between operations  1.41 us (3%)
  local copies, waits for them, and re-layouts  0.64 us (1%)
  other arithmetic  0.63 us (1%)
    all_to_all x1, blocking collectives, local(): lax.all_to_all(partial, FIRST, 0, 0)  12.4 us
    all_to_all x1, starting transfers between devices, local(): total = jnp.sum(lax.all_to_all(partial, SECOND, 0, 0), axis=0)  6.72 us
    ppermute x1, starting transfers between devices, local(): right = lax.ppermute(to_left, GX, ring(GX, -1))  5.59 us
    pallas_call x1, Pallas kernels, local(): pl.pallas_call(output, out_shape=(shape(19, X, Z, Y), shape(3, slots)), i...  4.05 us
    ppermute x1, starting transfers between devices, local(): low = lax.ppermute(to_high, GZ, ring(GZ, 1))  3.1 us
    ppermute x1, starting transfers between devices, local(): left = lax.ppermute(to_right, GX, ring(GX, 1))  2.77 us
    ppermute x1, waiting for transfers between devices, local(): high = lax.ppermute(to_low, GZ, ring(GZ, -1))  2.61 us
    all_to_all x1, waiting for transfers between devices, local(): total = jnp.sum(lax.all_to_all(partial, SECOND, 0, 0), axis=0)  2.38 us
  transfers between devices with their start and end apart: 5, of which 4 were waited for; matrix products, arithmetic and copies ran while one was open for 0% of the time, Pallas kernels for 13%

profile of v3, /device:TPU:1, one launch (start us, length us, event | category | flops | bytes accessed | tf_op | source)
XLA Modules:
  0.0 51.0 jit_solution(17208202757286981524)
XLA Ops:
  0.6 0.0 copy-start
  0.6 0.0 copy-start.4
  0.7 2.2 %shard_map.85 = (f32[152,256]{1,0:T(8,128)S(1)}, f32[152,256]{1,0:T(8,128)S(1)}, f32[128,256]{1,0:T(8,128)S(1)}) custom-call(bf16[19,16,8,256]{3,2,1,0:T(8,128)(2,1)} %stored_in.3, f32[19,16,8,256]{3,2,1,0:T(8,128)} %adj_in.3), custom_call_target="tpu_custom_call" | custom-call | flops 5000000 | bytes 4000000 | tf_op jit(solution)/shard_map/pallas_call | solution.py:627
  2.9 0.0 copy-start.3
  2.9 3.1 %collective-permute-start = (f32[152,256]{1,0:T(8,128)S(1)}, f32[152,256]{1,0:T(8,128)S(1)}, u32[]{:S(2)}, u32[]{:S(2)}) collective-permute-start(f32[152,256]{1,0:T(8,128)S(1)} %get-tuple-element.18.sent_high), channel_id=1, source_target_pairs={{0,1},{1,2},{2,3},{3,4},{4,5},{5,6},{6,7},{7,8},{8,9},{9,10},{10,1... | collective-permute-start | bytes 466952 | tf_op jit(solution)/shard_map/ppermute | solution.py:644
  6.0 0.3 collective-permute-start.1
  7.0 1.7 %shard_map.86 = (f32[9,2048]{1,0:T(8,128)S(1)}, bf16[256,2048]{1,0:T(8,128)(2,1)S(1)}, f32[3,8,2048]{2,1,0:T(8,128)S(1)}, f32[19,4,8,256]{3,2,1,0:T(8,128)S(1)}) custom-call(s32[1]{0:T(128)S(6)} %copy.11.count, f32[19,16,8,256]{3,2,1,0:T(8,128)S(1)} %copy-done, f32[128,256]{1,0:T(8,128)S(1)} %get-tuple-element.20.rho, s32[1,2048]{1,0:T(1,128)S(1)} %bitcast.2, ...), custom_call_target="tpu_custom_call" | custom-call | flops 800000000 | bytes 2000000 | tf_op jit(solution)/shard_map/pallas_call | solution.py:646
  8.7 0.0 collective-permute-done.low
  8.7 2.6 %collective-permute-done.1.high = f32[152,256]{1,0:T(8,128)S(1)} collective-permute-done((f32[152,256]{1,0:T(8,128)S(1)}, f32[152,256]{1,0:T(8,128)S(1)}, u32[]{:S(2)}, u32[]{:S(2)}) %collective-permute-start.1) | collective-permute-done | bytes 155680 | tf_op jit(solution)/shard_map/ppermute | solution.py:645
  11.3 0.1 shard_map.87
  11.4 0.0 copy-start.1
  11.5 2.8 %collective-permute-start.2 = (f32[88,256]{1,0:T(8,128)S(1)}, f32[88,256]{1,0:T(8,128)S(1)}, u32[]{:S(2)}, u32[]{:S(2)}) collective-permute-start(f32[88,256]{1,0:T(8,128)S(1)} %get-tuple-element.23.sent_right), channel_id=1, source_target_pairs={{0,16},{16,32},{32,48},{48,64},{64,80},{80,96},{96,112},{112,128},... | collective-permute-start | bytes 270344 | tf_op jit(solution)/shard_map/ppermute | solution.py:666
  14.2 5.6 %collective-permute-start.3 = (f32[88,256]{1,0:T(8,128)S(1)}, f32[88,256]{1,0:T(8,128)S(1)}, u32[]{:S(2)}, u32[]{:S(2)}) collective-permute-start(f32[88,256]{1,0:T(8,128)S(1)} %get-tuple-element.24.sent_left), channel_id=1, source_target_pairs={{0,240},{16,0},{32,16},{48,32},{64,48},{80,64},{96,80},{112,96},{1... | collective-permute-start | bytes 270344 | tf_op jit(solution)/shard_map/ppermute | solution.py:667
  19.8 0.0 copy-done.3
  19.8 1.0 %shard_map.88 = (f32[3,8,2048]{2,1,0:T(8,128)S(1)}, bf16[128,2048]{1,0:T(8,128)(2,1)S(1)}) custom-call(f32[152,256]{1,0:T(8,128)S(1)} %get-tuple-element.19.sent_low, f32[152,256]{1,0:T(8,128)S(1)} %get-tuple-element.18.sent_high, f32[152,256]{1,0:T(8,128)S(1)} %collective-permute-done.low, f32[152,256]{1,0:T(8,128)S(1)} %collective-permute-done.1.high, ...), custom_call_target="tpu_custom_call" | custom-call | flops 400000000 | bytes 2000000 | tf_op jit(solution)/shard_map/pallas_call | solution.py:668
  20.9 1.3 %collective-permute-done.2.left = f32[88,256]{1,0:T(8,128)S(1)} collective-permute-done((f32[88,256]{1,0:T(8,128)S(1)}, f32[88,256]{1,0:T(8,128)S(1)}, u32[]{:S(2)}, u32[]{:S(2)}) %collective-permute-start.2) | collective-permute-done | bytes 90144 | tf_op jit(solution)/shard_map/ppermute | solution.py:666
  22.2 1.2 %collective-permute-done.3.right = f32[88,256]{1,0:T(8,128)S(1)} collective-permute-done((f32[88,256]{1,0:T(8,128)S(1)}, f32[88,256]{1,0:T(8,128)S(1)}, u32[]{:S(2)}, u32[]{:S(2)}) %collective-permute-start.3) | collective-permute-done | bytes 90144 | tf_op jit(solution)/shard_map/ppermute | solution.py:667
  23.4 0.8 %shard_map.89 = (f32[3,2048]{1,0:T(4,128)S(1)}, f32[16,3,128]{2,1,0:T(4,128)S(1)}) custom-call(f32[128,256]{1,0:T(8,128)S(1)} %get-tuple-element.20.rho, f32[88,256]{1,0:T(8,128)S(1)} %get-tuple-element.24.sent_left, f32[88,256]{1,0:T(8,128)S(1)} %get-tuple-element.23.sent_right, f32[152,256]{1,0:T(8,128)S(1)} %collective-permute-done.low, ...), custom_call_target="tpu_custom_call" | custom-call | flops 300000000 | bytes 2000000 | tf_op jit(solution)/shard_map/pallas_call | solution.py:675
  24.2 12.4 %all_to_all.10 = f32[16,3,128]{2,1,0:T(4,128)S(1)} all-to-all(f32[16,3,128]{2,1,0:T(4,128)S(1)} %get-tuple-element.32), channel_id=1, replica_groups=mesh['y'=4,'zh'=4,'x'=4,'zl'=2,'core'=2] {'core','zh','zl'}, dimensions={0} | all-to-all | bytes 49152 | tf_op jit(solution)/shard_map/all_to_all | solution.py:700
  36.6 0.6 %broadcast_in_dim.2 = f32[16,3,128]{2,1,0:T(4,128)} broadcast(f32[3,128]{1,0:T(4,128)S(1)} %reduce_sum.18), dimensions={1,2} | broadcast | bytes 26112 | tf_op jit(solution)/shard_map/broadcast_in_dim | solution.py:618
  37.2 6.7 %all-to-all-start.1 = ((f32[16,3,128]{2,1,0:T(4,128)}), f32[16,3,128]{2,1,0:T(4,128)S(1)}, u32[]{:S(2)}, u32[]{:S(2)}) async-start(f32[16,3,128]{2,1,0:T(4,128)} %broadcast_in_dim.2), calls=%async_computation.1 | async-start | bytes 65536 | tf_op jit(solution)/shard_map/all_to_all | solution.py:701
  43.9 4.0 %shard_map.90 = (f32[19,16,8,256]{3,2,1,0:T(8,128)}, f32[3,2048]{1,0:T(4,128)}) custom-call(bf16[19,16,8,256]{3,2,1,0:T(8,128)(2,1)S(1)} %copy-done.1, f32[19,16,8,256]{3,2,1,0:T(8,128)} %adj_in.3, f32[152,256]{1,0:T(8,128)S(1)} %collective-permute-done.low, f32[152,256]{1,0:T(8,128)S(1)} %collective-permute-done.1.high, ...), custom_call_target="tpu_custom_call" | custom-call | flops 10000000 | bytes 7000000 | tf_op jit(solution)/shard_map/pallas_call | solution.py:685
  48.0 2.4 %all-to-all-done.1 = f32[16,3,128]{2,1,0:T(4,128)S(1)} async-done(((f32[16,3,128]{2,1,0:T(4,128)}), f32[16,3,128]{2,1,0:T(4,128)S(1)}, u32[]{:S(2)}, u32[]{:S(2)}) %all-to-all-start.1) | async-done | bytes 24608 | tf_op jit(solution)/shard_map/all_to_all | solution.py:701
  50.4 0.6 %reduce_sum.19 = f32[3,128]{1,0:T(4,128)} reduce(f32[16,3,128]{2,1,0:T(4,128)S(1)} %all-to-all-done.1, f32[]{:T(128)} %constant.0.clone.1), dimensions={0}, to_apply=%region_1.0 | reduce | flops 5760 | bytes 26116 | tf_op jit(solution)/shard_map/reduce_sum | solution.py:701
  (6 shorter events, 0.0 us)
Async XLA Ops:
  0.6 6.3 %copy-start = (f32[19,16,8,256]{3,2,1,0:T(8,128)S(1)}, f32[19,16,8,256]{3,2,1,0:T(8,128)}, u32[]{:S(2)}) copy-start(f32[19,16,8,256]{3,2,1,0:T(8,128)} %adj_in.3) | copy-start | bytes 7471108
  0.6 6.3 %copy-start.4 = (f32[9,2048]{1,0:T(8,128)S(1)}, f32[9,2048]{1,0:T(8,128)}, u32[]{:S(2)}) copy-start(f32[9,2048]{1,0:T(8,128)} %weight.1) | copy-start | bytes 221188
  0.7 6.3 %copy-start.2 = (s32[2048]{0:T(1024)S(1)}, s32[2048]{0:T(1024)}, u32[]{:S(2)}) copy-start(s32[2048]{0:T(1024)} %param.8) | copy-start | bytes 24580
  2.9 17.0 %copy-start.3 = (s32[2048]{0:T(1024)S(1)}, s32[2048]{0:T(1024)}, u32[]{:S(2)}) copy-start(s32[2048]{0:T(1024)} %param.10) | copy-start | bytes 24580
  2.9 5.8 %collective-permute-start = (f32[152,256]{1,0:T(8,128)S(1)}, f32[152,256]{1,0:T(8,128)S(1)}, u32[]{:S(2)}, u32[]{:S(2)}) collective-permute-start(f32[152,256]{1,0:T(8,128)S(1)} %get-tuple-element.18.sent_high), channel_id=1, source_target_pairs={{0,1},{1,2},{2,3},{3,4},{4,5},{5,6},{6,7},{7,8},{8,9},{9,10},{10,1... | collective-permute-start | bytes 466952 | tf_op jit(solution)/shard_map/ppermute | solution.py:644
  6.0 5.3 %collective-permute-start.1 = (f32[152,256]{1,0:T(8,128)S(1)}, f32[152,256]{1,0:T(8,128)S(1)}, u32[]{:S(2)}, u32[]{:S(2)}) collective-permute-start(f32[152,256]{1,0:T(8,128)S(1)} %get-tuple-element.19.sent_low), channel_id=1, source_target_pairs={{0,15},{1,0},{2,1},{3,2},{4,3},{5,4},{6,5},{7,6},{8,7},{9,8},{10,9... | collective-permute-start | bytes 466952 | tf_op jit(solution)/shard_map/ppermute | solution.py:645
  11.4 32.5 %copy-start.1 = (bf16[19,16,8,256]{3,2,1,0:T(8,128)(2,1)S(1)}, bf16[19,16,8,256]{3,2,1,0:T(8,128)(2,1)}, u32[]{:S(2)}) copy-start(bf16[19,16,8,256]{3,2,1,0:T(8,128)(2,1)} %stored_in.3) | copy-start | bytes 3735556
  11.5 10.7 %collective-permute-start.2 = (f32[88,256]{1,0:T(8,128)S(1)}, f32[88,256]{1,0:T(8,128)S(1)}, u32[]{:S(2)}, u32[]{:S(2)}) collective-permute-start(f32[88,256]{1,0:T(8,128)S(1)} %get-tuple-element.23.sent_right), channel_id=1, source_target_pairs={{0,16},{16,32},{32,48},{48,64},{64,80},{80,96},{96,112},{112,128},... | collective-permute-start | bytes 270344 | tf_op jit(solution)/shard_map/ppermute | solution.py:666
  14.2 9.2 %collective-permute-start.3 = (f32[88,256]{1,0:T(8,128)S(1)}, f32[88,256]{1,0:T(8,128)S(1)}, u32[]{:S(2)}, u32[]{:S(2)}) collective-permute-start(f32[88,256]{1,0:T(8,128)S(1)} %get-tuple-element.24.sent_left), channel_id=1, source_target_pairs={{0,240},{16,0},{32,16},{48,32},{64,48},{80,64},{96,80},{112,96},{1... | collective-permute-start | bytes 270344 | tf_op jit(solution)/shard_map/ppermute | solution.py:667
  37.2 13.2 %all-to-all-start.1 = ((f32[16,3,128]{2,1,0:T(4,128)}), f32[16,3,128]{2,1,0:T(4,128)S(1)}, u32[]{:S(2)}, u32[]{:S(2)}) async-start(f32[16,3,128]{2,1,0:T(4,128)} %broadcast_in_dim.2), calls=%async_computation.1 | async-start | bytes 65536 | tf_op jit(solution)/shard_map/all_to_all | solution.py:701

commit v4 on v3

--- a/solution.py
+++ b/solution.py
@@ -133,7 +133,14 @@
     return first_moments(g)
 
 
-def pack_z(stored_in, adj_in, to_low, to_high, rho_out, stored, adj, sems):
+def by_parity(index, first, second, even_first, even_second):
+    even = lax.rem(index, 2) == 0
+    a, b = even_first[...], even_second[...]
+    first[...] = jnp.where(even, a, b)
+    second[...] = jnp.where(even, b, a)
+
+
+def pack_z(stored_in, adj_in, to_low, to_high, across, along, rho_out, stored, adj, sems):
     copies = []
     for n in range(GROUPS):
         part = pl.ds(n * STEP, STEP)
@@ -182,6 +189,7 @@
             high_rows.append(zero if mom is None else mom[Z - 1 : Z])
     to_low[Z_SPILL:, :] = jnp.concatenate(low_rows + [zero, zero])
     to_high[Z_SPILL:, :] = jnp.concatenate(high_rows + [zero, zero])
+    by_parity(lax.axis_index(GZ), across, along, to_high, to_low)
 
 
 def shift_rows(tile, step):
@@ -209,8 +217,23 @@
     return a if b is None else a + b
 
 
-def pack_x(near, rho, sent_low, sent_high, low, high, after, to_left, to_right):
+def pack_x(
+    near,
+    rho,
+    sent_low,
+    sent_high,
+    along_in,
+    across_in,
+    after,
+    to_left,
+    to_right,
+    across,
+    along,
+    low,
+    high,
+):
     del after
+    by_parity(lax.axis_index(GZ), high, low, across_in, along_in)
     low_on, high_on, _, _ = ends()
     edge_low, edge_high = edge_moments(sent_low, Z_UP), edge_moments(sent_high, Z_DOWN)
 
@@ -245,6 +268,7 @@
 
     side(to_left, 0, 0, 1, X_UP, -1)
     side(to_right, X - 1, 3, 2, X_DOWN, 1)
+    by_parity(lax.axis_index(GX), across, along, to_right, to_left)
 
 
 def collide_transpose(f, g, emit):
@@ -506,8 +530,8 @@
     sent_right,
     low,
     high,
-    left,
-    right,
+    along,
+    across,
     cell,
     weight,
     hot,
@@ -515,10 +539,13 @@
     acc_in,
     grad,
     partial,
+    left,
+    right,
     split,
     totals,
 ):
     low_on, high_on, left_on, right_on = ends()
+    by_parity(lax.axis_index(GX), right, left, across, along)
     rows = 48
     zero = jnp.zeros((8, Y), jnp.float32)
     beyond, added = [], []
@@ -591,13 +618,31 @@
         totals[...], which[...], (((1,), (1,)), ((), ())), preferred_element_type=jnp.float32
     )
     result = total[0:3] + total[8:11]
+    result = jnp.concatenate([result[0:1], result[1:2], result[2:3]], axis=1)
     for n in range(partial.shape[0]):
         partial[n] = result
 
 
-def ring(axis, step):
-    count = lax.axis_size(axis)
-    return [(i, (i + step) % count) for i in range(count)]
+def exchange_z(across, along):
+    count = lax.axis_size(GZ)
+    along = lax.ppermute(
+        along, GZ, [(i, (i + 1 if i % 2 else i - 1) % count) for i in range(count)]
+    )
+    return lax.ppermute(across, GZ, [(i, i ^ 1) for i in range(count)]), along
+
+
+def exchange_x(across, along):
+    count, width = lax.axis_size(GX), lax.axis_size(GZ)
+    pairs = []
+    for i in range(count):
+        for j in range(width):
+            if i in (0, count - 1):
+                to = i * width + (j ^ 1)
+            else:
+                to = (i + 1 if i % 2 else i - 1) * width + j
+            pairs.append((i * width + j, to))
+    along = lax.ppermute(along, GX + GZ, pairs)
+    return lax.ppermute(across, GX, [(i, i ^ 1) for i in range(count)]), along
 
 
 PARAMS = pltpu.CompilerParams(vmem_limit_bytes=48 * 1024 * 1024)
@@ -624,15 +669,17 @@
     hbm = pl.BlockSpec(memory_space=pltpu.HBM)
     any_space = pl.BlockSpec(memory_space=pl.ANY)
     cell, panel = marker_cell.reshape(1, slots), marker_panel.reshape(1, slots)
-    to_low, to_high, rho = pl.pallas_call(
+    to_low, to_high, across, along, rho = pl.pallas_call(
         pack_z,
         out_shape=(
+            shape(ZROWS, Y),
+            shape(ZROWS, Y),
             shape(ZROWS, Y),
             shape(ZROWS, Y),
             shape(X * Z, Y),
         ),
         in_specs=[hbm, hbm],
-        out_specs=(whole,) * 3,
+        out_specs=(whole,) * 5,
         scratch_shapes=[
             pltpu.VMEM(stored.shape, stored.dtype),
             pltpu.VMEM(adj.shape, adj.dtype),
@@ -641,8 +688,7 @@
         compiler_params=FIRST_BIG,
         cost_estimate=cost(5_000_000, 4_000_000),
     )(stored, adj)
-    low = lax.ppermute(to_high, GZ, ring(GZ, 1))
-    high = lax.ppermute(to_low, GZ, ring(GZ, -1))
+    across, along = exchange_z(across, along)
     weight, hot, acc, near = pl.pallas_call(
         stage_a,
         out_shape=(
@@ -656,15 +702,14 @@
         compiler_params=PARAMS,
         cost_estimate=cost(800_000_000, 2_000_000),
     )(marker_count, adj, rho, cell, marker_weight)
-    to_left, to_right = pl.pallas_call(
+    to_left, to_right, across, along, low, high = pl.pallas_call(
         pack_x,
-        out_shape=(shape(XROWS, Y), shape(XROWS, Y)),
+        out_shape=(shape(XROWS, Y),) * 4 + (shape(ZROWS, Y),) * 2,
         in_specs=[whole] * 6 + [any_space],
         compiler_params=PARAMS,
         cost_estimate=cost(1_000_000, 2_000_000),
-    )(near, rho, to_low, to_high, low, high, acc)
-    left = lax.ppermute(to_right, GX, ring(GX, 1))
-    right = lax.ppermute(to_left, GX, ring(GX, -1))
+    )(near, rho, to_low, to_high, along, across, acc)
+    across, along = exchange_x(across, along)
     acc, which = pl.pallas_call(
         stage_b,
         out_shape=(shape(3, 8, slots), jax.ShapeDtypeStruct((PANELS, slots), jnp.bfloat16)),
@@ -672,16 +717,21 @@
         compiler_params=PARAMS,
         cost_estimate=cost(400_000_000, 2_000_000),
     )(to_low, to_high, low, high, cell, panel, weight, hot, acc)
-    grad, partial = pl.pallas_call(
+    grad, partial, left, right = pl.pallas_call(
         stage_c,
-        out_shape=(shape(3, slots), shape(lax.axis_size(FIRST), 3, PANELS)),
+        out_shape=(
+            shape(3, slots),
+            shape(lax.axis_size(FIRST), 1, 3 * PANELS),
+            shape(XROWS, Y),
+            shape(XROWS, Y),
+        ),
         scratch_shapes=[
             pltpu.VMEM((6 * 48, Y), jnp.bfloat16),
             pltpu.VMEM((16, slots), jnp.bfloat16),
         ],
         compiler_params=PARAMS,
         cost_estimate=cost(300_000_000, 2_000_000),
-    )(rho, to_left, to_right, low, high, left, right, cell, weight, hot, which, acc)
+    )(rho, to_left, to_right, low, high, along, across, cell, weight, hot, which, acc)
     out, grad = pl.pallas_call(
         output,
         out_shape=(shape(19, X, Z, Y), shape(3, slots)),
@@ -698,7 +748,7 @@
         cost_estimate=cost(10_000_000, 7_000_000),
     )(stored, adj, low, high, left, right, grad)
     partial = summed(lax.all_to_all(partial, FIRST, 0, 0), lax.axis_size(SECOND))
-    total = jnp.sum(lax.all_to_all(partial, SECOND, 0, 0), axis=0)
+    total = jnp.sum(lax.all_to_all(partial, SECOND, 0, 0), axis=0).reshape(3, PANELS)
     return (out, grad, total)
 
 

time: 51.2 us -> 50.1 us (0.979)
  blocking collectives: 12.4 us -> 15.7 us
  waiting for transfers between devices: 7.51 us -> 4.51 us
  starting transfers between devices: 18.5 us -> 17 us
    all_to_all x1, blocking collectives: 12.4 us -> 15.7 us  [local(): lax.all_to_all(partial, FIRST, 0, 0)]
    ppermute x4, waiting for transfers between devices: 5.13 us -> 2.13 us  [the longest x1 2.12 us: exchange_x(): return (lax.ppermute(across, GX, [(i, i ^ 1) for i in range(count)]), along)]
    all_to_all x1, starting transfers between devices: 6.72 us -> 5.46 us  [local(): lax.all_to_all(partial, SECOND, 0, 0)]
  transfers between devices with their start and end apart: 5 -> 5, of which waited for: 4 -> 2; matrix products, arithmetic and copies ran while one was open for 0% -> 0% of each run, Pallas kernels for 13% -> 14%
where the time goes in v4:
time: 50.1 us; the launch traced here: 49.9 us
  starting transfers between devices  17 us (34%)
  blocking collectives  15.7 us (31%)
  Pallas kernels  9.94 us (20%)
  waiting for transfers between devices  4.51 us (9%)
  between operations  1.43 us (3%)
  other arithmetic  0.65 us (1%)
  local copies, waits for them, and re-layouts  0.64 us (1%)
    all_to_all x1, blocking collectives, local(): lax.all_to_all(partial, FIRST, 0, 0)  15.7 us
    all_to_all x1, starting transfers between devices, local(): lax.all_to_all(partial, SECOND, 0, 0)  5.46 us
    pallas_call x1, Pallas kernels, local(): pl.pallas_call(output, out_shape=(shape(19, X, Z, Y), shape(3, slots)), i...  4.05 us
    ppermute x1, starting transfers between devices, exchange_x(): return (lax.ppermute(across, GX, [(i, i ^ 1) for i in range(count)]), along)  3.29 us
    ppermute x1, starting transfers between devices, exchange_z(): lax.ppermute(along, GZ, [(i, (i + 1 if i % 2 else i - 1) % count) for i i...  3.11 us
    ppermute x1, starting transfers between devices, exchange_x(): along = lax.ppermute(along, GX + GZ, pairs)  3.1 us
    all_to_all x1, waiting for transfers between devices, local(): lax.all_to_all(partial, SECOND, 0, 0)  2.38 us
    pallas_call x1, Pallas kernels, local(): pl.pallas_call(pack_z, out_shape=(shape(ZROWS, Y), shape(ZROWS, Y), shape...  2.2 us
  transfers between devices with their start and end apart: 5, of which 2 were waited for; matrix products, arithmetic and copies ran while one was open for 0% of the time, Pallas kernels for 14%

profile of v4, /device:TPU:1, one launch (start us, length us, event | category | flops | bytes accessed | tf_op | source)
XLA Modules:
  0.0 49.9 jit_solution(86336979954991612)
XLA Ops:
  0.6 0.0 copy-start
  0.6 0.0 copy-start.4
  0.7 0.0 copy-start.2
  0.7 2.2 %shard_map.85 = (f32[152,256]{1,0:T(8,128)S(1)}, f32[152,256]{1,0:T(8,128)S(1)}, f32[152,256]{1,0:T(8,128)S(1)}, f32[152,256]{1,0:T(8,128)S(1)}, f32[128,256]{1,0:T(8,128)S(1)}) custom-call(bf16[19,16,8,256]{3,2,1,0:T(8,128)(2,1)} %stored_in.3, f32[19,16,8,256]{3,2,1,0:T(8,128)} %adj_in.3), custom_call_target="tpu_custom_call" | custom-call | flops 5000000 | bytes 4000000 | tf_op jit(solution)/shard_map/pallas_call | solution.py:672
  2.9 0.0 copy-start.3
  2.9 3.1 %collective-permute-start = (f32[152,256]{1,0:T(8,128)S(1)}, f32[152,256]{1,0:T(8,128)S(1)}, u32[]{:S(2)}, u32[]{:S(2)}) collective-permute-start(f32[152,256]{1,0:T(8,128)S(1)} %get-tuple-element.30), channel_id=1, source_target_pairs={{0,15},{1,2},{2,1},{3,4},{4,3},{5,6},{6,5},{7,8},{8,7},{9,10},{10,... | collective-permute-start | bytes 466952 | tf_op jit(solution)/shard_map/ppermute | solution.py:628
  6.0 2.0 %collective-permute-start.1 = (f32[152,256]{1,0:T(8,128)S(1)}, f32[152,256]{1,0:T(8,128)S(1)}, u32[]{:S(2)}, u32[]{:S(2)}) collective-permute-start(f32[152,256]{1,0:T(8,128)S(1)} %get-tuple-element.31), channel_id=1, source_target_pairs={{0,1},{1,0},{2,3},{3,2},{4,5},{5,4},{6,7},{7,6},{8,9},{9,8},{10,11... | collective-permute-start | bytes 466952 | tf_op jit(solution)/shard_map/ppermute | solution.py:631
  8.7 1.7 %shard_map.86 = (f32[9,2048]{1,0:T(8,128)S(1)}, bf16[256,2048]{1,0:T(8,128)(2,1)S(1)}, f32[3,8,2048]{2,1,0:T(8,128)S(1)}, f32[19,4,8,256]{3,2,1,0:T(8,128)S(1)}) custom-call(s32[1]{0:T(128)S(6)} %copy.11.count, f32[19,16,8,256]{3,2,1,0:T(8,128)S(1)} %copy-done, f32[128,256]{1,0:T(8,128)S(1)} %get-tuple-element.26.rho, s32[1,2048]{1,0:T(1,128)S(1)} %bitcast.3, ...), custom_call_target="tpu_custom_call" | custom-call | flops 800000000 | bytes 2000000 | tf_op jit(solution)/shard_map/pallas_call | solution.py:692
  10.4 0.0 collective-permute-done.along_in
  10.5 0.0 collective-permute-done.1.across_in
  10.5 0.2 shard_map.87
  10.6 0.0 copy-start.1
  10.6 3.1 %collective-permute-start.2 = (f32[88,256]{1,0:T(8,128)S(1)}, f32[88,256]{1,0:T(8,128)S(1)}, u32[]{:S(2)}, u32[]{:S(2)}) collective-permute-start(f32[88,256]{1,0:T(8,128)S(1)} %get-tuple-element.37), channel_id=1, source_target_pairs={{0,1},{1,0},{2,3},{3,2},{4,5},{5,4},{6,7},{7,6},{8,9},{9,8},{10,11... | collective-permute-start | bytes 270344 | tf_op jit(solution)/shard_map/ppermute | solution.py:644
  13.7 3.3 %collective-permute-start.3 = (f32[88,256]{1,0:T(8,128)S(1)}, f32[88,256]{1,0:T(8,128)S(1)}, u32[]{:S(2)}, u32[]{:S(2)}) collective-permute-start(f32[88,256]{1,0:T(8,128)S(1)} %get-tuple-element.38), channel_id=1, source_target_pairs={{0,16},{16,0},{32,48},{48,32},{64,80},{80,64},{96,112},{112,96},{1... | collective-permute-start | bytes 270344 | tf_op jit(solution)/shard_map/ppermute | solution.py:645
  17.0 1.0 %shard_map.88 = (f32[3,8,2048]{2,1,0:T(8,128)S(1)}, bf16[128,2048]{1,0:T(8,128)(2,1)S(1)}) custom-call(f32[152,256]{1,0:T(8,128)S(1)} %get-tuple-element.28.sent_low, f32[152,256]{1,0:T(8,128)S(1)} %get-tuple-element.29.sent_high, f32[152,256]{1,0:T(8,128)S(1)} %get-tuple-element.33.low, f32[152,256]{1,0:T(8,128)S(1)} %get-tuple-element.34.high, ...), custom_call_target="tpu_custom_call" | custom-call | flops 400000000 | bytes 2000000 | tf_op jit(solution)/shard_map/pallas_call | solution.py:713
  18.1 0.0 collective-permute-done.2.along
  18.1 2.1 %collective-permute-done.3.across = f32[88,256]{1,0:T(8,128)S(1)} collective-permute-done((f32[88,256]{1,0:T(8,128)S(1)}, f32[88,256]{1,0:T(8,128)S(1)}, u32[]{:S(2)}, u32[]{:S(2)}) %collective-permute-start.3) | collective-permute-done | bytes 90144 | tf_op jit(solution)/shard_map/ppermute | solution.py:645
  20.2 0.8 %shard_map.89 = (f32[3,2048]{1,0:T(4,128)S(1)}, f32[16,1,384]{2,1,0:T(1,128)S(1)}, f32[88,256]{1,0:T(8,128)S(1)}, f32[88,256]{1,0:T(8,128)S(1)}) custom-call(f32[128,256]{1,0:T(8,128)S(1)} %get-tuple-element.26.rho, f32[88,256]{1,0:T(8,128)S(1)} %get-tuple-element.35.sent_left, f32[88,256]{1,0:T(8,128)S(1)} %get-tuple-element.36.sent_right, ...), custom_call_target="tpu_custom_call" | custom-call | flops 300000000 | bytes 2000000 | tf_op jit(solution)/shard_map/pallas_call | solution.py:720
  21.0 15.7 %all_to_all.10 = f32[16,1,384]{2,1,0:T(1,128)S(1)} all-to-all(f32[16,1,384]{2,1,0:T(1,128)S(1)} %get-tuple-element.48), channel_id=1, replica_groups=mesh['y'=4,'zh'=4,'x'=4,'zl'=2,'core'=2] {'core','zh','zl'}, dimensions={0} | all-to-all | bytes 49152 | tf_op jit(solution)/shard_map/all_to_all | solution.py:750
  36.8 0.6 %broadcast_in_dim.2 = f32[16,1,384]{2,1,0:T(1,128)} broadcast(f32[384]{0:T(512)S(1)} %reduce_sum.18), dimensions={2} | broadcast | bytes 26112 | tf_op jit(solution)/shard_map/broadcast_in_dim | solution.py:663
  37.4 5.5 %all-to-all-start.1 = ((f32[16,1,384]{2,1,0:T(1,128)}), f32[16,1,384]{2,1,0:T(1,128)S(1)}, u32[]{:S(2)}, u32[]{:S(2)}) async-start(f32[16,1,384]{2,1,0:T(1,128)} %broadcast_in_dim.2), calls=%async_computation.1 | async-start | bytes 49152 | tf_op jit(solution)/shard_map/all_to_all | solution.py:751
  42.9 4.0 %shard_map.90 = (f32[19,16,8,256]{3,2,1,0:T(8,128)}, f32[3,2048]{1,0:T(4,128)}) custom-call(bf16[19,16,8,256]{3,2,1,0:T(8,128)(2,1)S(1)} %copy-done.1, f32[19,16,8,256]{3,2,1,0:T(8,128)} %adj_in.3, f32[152,256]{1,0:T(8,128)S(1)} %get-tuple-element.33.low, f32[152,256]{1,0:T(8,128)S(1)} %get-tuple-element.34.high, f32[88,256]{1,0:T(8,128)S(1)} %get-tuple-element.43.left, ...), custom_call_target="tpu_custom_call" | custom-call | flops 10000000 | bytes 7000000 | tf_op jit(solution)/shard_map/pallas_call | solution.py:735
  46.9 2.4 %all-to-all-done.1 = f32[16,1,384]{2,1,0:T(1,128)S(1)} async-done(((f32[16,1,384]{2,1,0:T(1,128)}), f32[16,1,384]{2,1,0:T(1,128)S(1)}, u32[]{:S(2)}, u32[]{:S(2)}) %all-to-all-start.1) | async-done | bytes 24608 | tf_op jit(solution)/shard_map/all_to_all | solution.py:751
  49.3 0.6 %reduce_sum.19 = f32[384]{0:T(512)} reduce(f32[16,1,384]{2,1,0:T(1,128)S(1)} %all-to-all-done.1, f32[]{:T(128)} %constant.0.clone.1), dimensions={0,1}, to_apply=%region_1.0 | reduce | flops 5760 | bytes 26116 | tf_op jit(solution)/shard_map/reduce_sum | solution.py:751
  (6 shorter events, 0.0 us)
Async XLA Ops:
  0.6 8.1 %copy-start = (f32[19,16,8,256]{3,2,1,0:T(8,128)S(1)}, f32[19,16,8,256]{3,2,1,0:T(8,128)}, u32[]{:S(2)}) copy-start(f32[19,16,8,256]{3,2,1,0:T(8,128)} %adj_in.3) | copy-start | bytes 7471108
  0.6 8.1 %copy-start.4 = (f32[9,2048]{1,0:T(8,128)S(1)}, f32[9,2048]{1,0:T(8,128)}, u32[]{:S(2)}) copy-start(f32[9,2048]{1,0:T(8,128)} %weight.1) | copy-start | bytes 221188
  0.7 8.1 %copy-start.2 = (s32[2048]{0:T(1024)S(1)}, s32[2048]{0:T(1024)}, u32[]{:S(2)}) copy-start(s32[2048]{0:T(1024)} %param.8) | copy-start | bytes 24580
  2.9 14.1 %copy-start.3 = (s32[2048]{0:T(1024)S(1)}, s32[2048]{0:T(1024)}, u32[]{:S(2)}) copy-start(s32[2048]{0:T(1024)} %param.10) | copy-start | bytes 24580
  2.9 7.6 %collective-permute-start = (f32[152,256]{1,0:T(8,128)S(1)}, f32[152,256]{1,0:T(8,128)S(1)}, u32[]{:S(2)}, u32[]{:S(2)}) collective-permute-start(f32[152,256]{1,0:T(8,128)S(1)} %get-tuple-element.30), channel_id=1, source_target_pairs={{0,15},{1,2},{2,1},{3,4},{4,3},{5,6},{6,5},{7,8},{8,7},{9,10},{10,... | collective-permute-start | bytes 466952 | tf_op jit(solution)/shard_map/ppermute | solution.py:628
  6.0 4.5 %collective-permute-start.1 = (f32[152,256]{1,0:T(8,128)S(1)}, f32[152,256]{1,0:T(8,128)S(1)}, u32[]{:S(2)}, u32[]{:S(2)}) collective-permute-start(f32[152,256]{1,0:T(8,128)S(1)} %get-tuple-element.31), channel_id=1, source_target_pairs={{0,1},{1,0},{2,3},{3,2},{4,5},{5,4},{6,7},{7,6},{8,9},{9,8},{10,11... | collective-permute-start | bytes 466952 | tf_op jit(solution)/shard_map/ppermute | solution.py:631
  10.6 32.2 %copy-start.1 = (bf16[19,16,8,256]{3,2,1,0:T(8,128)(2,1)S(1)}, bf16[19,16,8,256]{3,2,1,0:T(8,128)(2,1)}, u32[]{:S(2)}) copy-start(bf16[19,16,8,256]{3,2,1,0:T(8,128)(2,1)} %stored_in.3) | copy-start | bytes 3735556
  10.6 7.4 %collective-permute-start.2 = (f32[88,256]{1,0:T(8,128)S(1)}, f32[88,256]{1,0:T(8,128)S(1)}, u32[]{:S(2)}, u32[]{:S(2)}) collective-permute-start(f32[88,256]{1,0:T(8,128)S(1)} %get-tuple-element.37), channel_id=1, source_target_pairs={{0,1},{1,0},{2,3},{3,2},{4,5},{5,4},{6,7},{7,6},{8,9},{9,8},{10,11... | collective-permute-start | bytes 270344 | tf_op jit(solution)/shard_map/ppermute | solution.py:644
  13.7 6.5 %collective-permute-start.3 = (f32[88,256]{1,0:T(8,128)S(1)}, f32[88,256]{1,0:T(8,128)S(1)}, u32[]{:S(2)}, u32[]{:S(2)}) collective-permute-start(f32[88,256]{1,0:T(8,128)S(1)} %get-tuple-element.38), channel_id=1, source_target_pairs={{0,16},{16,0},{32,48},{48,32},{64,80},{80,64},{96,112},{112,96},{1... | collective-permute-start | bytes 270344 | tf_op jit(solution)/shard_map/ppermute | solution.py:645
  37.4 11.9 %all-to-all-start.1 = ((f32[16,1,384]{2,1,0:T(1,128)}), f32[16,1,384]{2,1,0:T(1,128)S(1)}, u32[]{:S(2)}, u32[]{:S(2)}) async-start(f32[16,1,384]{2,1,0:T(1,128)} %broadcast_in_dim.2), calls=%async_computation.1 | async-start | bytes 49152 | tf_op jit(solution)/shard_map/all_to_all | solution.py:751

commit v5 on v4

--- a/solution.py
+++ b/solution.py
@@ -335,70 +335,91 @@
         emit(q, along[STENCIL[q]] + (1.0 - OMEGA) * g[q])
 
 
-def output(
-    stored_in,
-    adj_in,
+def interior(stored, adj, low, high, after, out_hbm, token, ends_stored, out, sems):
+    del after
+    low_on, high_on, _, _ = ends()
+
+    def body(x, carry):
+        f = [stored[q, x].astype(jnp.float32) for q in range(19)]
+        g = []
+        for q in range(19):
+            at = x + STENCIL[q][0]
+            g.append(pulled_z(adj, q, at, low, high, at, low_on, high_on))
+
+        def emit(q, value):
+            out[q, x] = value
+
+        collide_transpose(f, g, emit)
+        return carry
+
+    writes = []
+    for n, (first, last) in enumerate(((1, 5), (5, 9), (9, 13), (13, X - 1))):
+        lax.fori_loop(first, last, body, 0)
+        part = pl.ds(first, last - first)
+        copy = pltpu.make_async_copy(out.at[:, part], out_hbm.at[:, part], sems.at[n])
+        copy.start()
+        writes.append(copy)
+    for k, x in enumerate((0, X - 1)):
+        ends_stored[k] = stored[:, x].astype(jnp.float32)
+    token[...] = jnp.zeros_like(token)
+    for copy in writes:
+        copy.wait()
+
+
+def finish(
+    parts,
+    grad,
+    near,
+    ends_stored,
     low,
     high,
     left,
     right,
-    grad,
-    out_hbm,
+    out_in,
+    out,
     grad_hbm,
-    stored,
-    adj,
-    out,
-    in_sems,
-    out_sems,
+    panel_hbm,
+    planes,
+    panel,
+    sems,
 ):
+    del out_in
     low_on, high_on, left_on, right_on = ends()
-    reads, writes = [], []
-    for n in range(GROUPS):
-        part = pl.ds(n * STEP, STEP)
-        for k, (src, dst) in enumerate(((adj_in, adj), (stored_in, stored))):
-            copy = pltpu.make_async_copy(src.at[:, part], dst.at[:, part], in_sems.at[k, n])
-            copy.start()
-            reads.append(copy)
-    copy = pltpu.make_async_copy(grad, grad_hbm, out_sems.at[GROUPS])
-    copy.start()
-    writes.append(copy)
-
-    def plane(x, taken=(), ref=None, on=None):
-        f = [stored[q, x].astype(jnp.float32) for q in range(19)]
+    total = parts[0]
+    for n in range(1, parts.shape[0]):
+        total = total + parts[n]
+    for d in range(3):
+        panel[d : d + 1, :] = total[:, d * PANELS : (d + 1) * PANELS]
+    writes = [
+        pltpu.make_async_copy(panel, panel_hbm, sems.at[0]),
+        pltpu.make_async_copy(grad, grad_hbm, sems.at[1]),
+    ]
+    for copy in writes:
+        copy.start()
+    for k, (x, plane, inner, taken, ref, on) in enumerate(
+        (
+            (0, 0, 1, X_DOWN, left, left_on),
+            (X - 1, 3, 2, X_UP, right, right_on),
+        )
+    ):
+        f = [ends_stored[k, q] for q in range(19)]
         g = []
         for q in range(19):
-            at = x + STENCIL[q][0]
+            step = STENCIL[q][0]
             if q in taken:
                 n = taken.index(q)
                 g.append(ref[n * Z : (n + 1) * Z, :] * on)
             else:
-                g.append(pulled_z(adj, q, at, low, high, at, low_on, high_on))
-
-        def emit(q, value):
-            out[q, x] = value
+                at = plane if step == 0 else inner
+                g.append(pulled_z(near, q, x + step, low, high, at, low_on, high_on))
+
+        def emit(q, value, k=k):
+            planes[k, q] = value
 
         collide_transpose(f, g, emit)
-
-    def body(x, carry):
-        plane(x)
-        return carry
-
-    done = 0
-    for n in range(GROUPS):
-        reads[2 * n].wait()
-        reads[2 * n + 1].wait()
-        ready = (n + 1) * STEP - 1
-        if n == 0:
-            plane(0, X_DOWN, left, left_on)
-        lax.fori_loop(max(done, 1), ready, body, 0)
-        if n == GROUPS - 1:
-            plane(X - 1, X_UP, right, right_on)
-            ready = X
-        part = pl.ds(done, ready - done)
-        copy = pltpu.make_async_copy(out.at[:, part], out_hbm.at[:, part], out_sems.at[n])
+        copy = pltpu.make_async_copy(planes.at[k], out.at[:, x], sems.at[2 + k])
         copy.start()
         writes.append(copy)
-        done = ready
     for copy in writes:
         copy.wait()
 
@@ -537,6 +558,7 @@
     hot,
     which,
     acc_in,
+    token,
     grad,
     partial,
     left,
@@ -544,6 +566,7 @@
     split,
     totals,
 ):
+    del token
     low_on, high_on, left_on, right_on = ends()
     by_parity(lax.axis_index(GX), right, left, across, along)
     rows = 48
@@ -717,6 +740,17 @@
         compiler_params=PARAMS,
         cost_estimate=cost(400_000_000, 2_000_000),
     )(to_low, to_high, low, high, cell, panel, weight, hot, acc)
+    out, token, ends_stored = pl.pallas_call(
+        interior,
+        out_shape=(shape(19, X, Z, Y), shape(8, PANELS), shape(2, 19, Z, Y)),
+        out_specs=(hbm, whole, whole),
+        scratch_shapes=[
+            pltpu.VMEM(adj.shape, adj.dtype),
+            pltpu.SemaphoreType.DMA((GROUPS,)),
+        ],
+        compiler_params=PARAMS,
+        cost_estimate=cost(10_000_000, 7_000_000),
+    )(stored, adj, low, high, acc)
     grad, partial, left, right = pl.pallas_call(
         stage_c,
         out_shape=(
@@ -731,25 +765,23 @@
         ],
         compiler_params=PARAMS,
         cost_estimate=cost(300_000_000, 2_000_000),
-    )(rho, to_left, to_right, low, high, along, across, cell, weight, hot, which, acc)
-    out, grad = pl.pallas_call(
-        output,
-        out_shape=(shape(19, X, Z, Y), shape(3, slots)),
-        in_specs=[hbm, hbm] + [whole] * 5,
-        out_specs=(hbm, hbm),
+    )(rho, to_left, to_right, low, high, along, across, cell, weight, hot, which, acc, token)
+    partial = summed(lax.all_to_all(partial, FIRST, 0, 0), lax.axis_size(SECOND))
+    partial = lax.all_to_all(partial, SECOND, 0, 0)
+    return pl.pallas_call(
+        finish,
+        out_shape=(shape(19, X, Z, Y), shape(3, slots), shape(3, PANELS)),
+        in_specs=[whole] * 8 + [any_space],
+        out_specs=(any_space, hbm, hbm),
         scratch_shapes=[
-            pltpu.VMEM(stored.shape, stored.dtype),
-            pltpu.VMEM(adj.shape, adj.dtype),
-            pltpu.VMEM(adj.shape, adj.dtype),
-            pltpu.SemaphoreType.DMA((2, GROUPS)),
-            pltpu.SemaphoreType.DMA((GROUPS + 1,)),
+            pltpu.VMEM((2, 19, Z, Y), jnp.float32),
+            pltpu.VMEM((3, PANELS), jnp.float32),
+            pltpu.SemaphoreType.DMA((4,)),
         ],
-        compiler_params=BIG,
-        cost_estimate=cost(10_000_000, 7_000_000),
-    )(stored, adj, low, high, left, right, grad)
-    partial = summed(lax.all_to_all(partial, FIRST, 0, 0), lax.axis_size(SECOND))
-    total = jnp.sum(lax.all_to_all(partial, SECOND, 0, 0), axis=0).reshape(3, PANELS)
-    return (out, grad, total)
+        input_output_aliases={8: 0},
+        compiler_params=PARAMS,
+        cost_estimate=cost(1_000_000, 2_000_000),
+    )(partial, grad, near, ends_stored, low, high, left, right, out)
 
 
 def solution(mesh):

time: 50.1 us -> 49.6 us (0.990)
  blocking collectives: 15.7 us -> 27 us
  starting transfers between devices: 17 us -> 11.5 us
  waiting for transfers between devices: 4.51 us -> 0.01 us
  other arithmetic: 0.65 us -> 0.04 us
  Pallas kernels: 9.94 us -> 9.33 us
  local copies, waits for them, and re-layouts: 0.64 us -> 0.04 us
    all_to_all x0 -> x1, blocking collectives: none -> 11.7 us  [local(): partial = lax.all_to_all(partial, SECOND, 0, 0)]
    all_to_all x1 -> x0, starting transfers between devices: 5.46 us -> none  [local(): lax.all_to_all(partial, SECOND, 0, 0)]
    all_to_all x1 -> x0, waiting for transfers between devices: 2.38 us -> none  [local(): lax.all_to_all(partial, SECOND, 0, 0)]
    ppermute x1, waiting for transfers between devices: 2.12 us -> 0.01 us  [exchange_x(): return (lax.ppermute(across, GX, [(i, i ^ 1) for i in range(count)]), along)]
    pallas_call x1 -> x2, Pallas kernels: 4.05 us -> 3.42 us  [the longest x1 2.48 us: local(): pl.pallas_call(interior, out_shape=(shape(19, X, Z, Y), shape(8, PANELS),...]
    reduce_sum x1 -> x0, other arithmetic: 0.61 us -> none  [local(): jnp.sum(lax.all_to_all(partial, SECOND, 0, 0), axis=0).reshape(3, PANELS)]
    broadcast_in_dim x1, local copies, waits for them, and re-layouts: 0.62 us -> 0.02 us  [summed(): return jnp.broadcast_to(total[None], (count,) + total.shape)]
  transfers between devices with their start and end apart: 5 -> 4, of which waited for: 2 -> 0; matrix products, arithmetic and copies ran while one was open for 0% -> 0% of each run, Pallas kernels for 14% -> 11%
where the time goes in v5:
time: 49.6 us; the launch traced here: 49.4 us
  blocking collectives  27 us (54%)
  starting transfers between devices  11.5 us (23%)
  Pallas kernels  9.33 us (19%)
  between operations  1.43 us (3%)
    all_to_all x1, blocking collectives, local(): lax.all_to_all(partial, FIRST, 0, 0)  15.3 us
    all_to_all x1, blocking collectives, local(): partial = lax.all_to_all(partial, SECOND, 0, 0)  11.7 us
    ppermute x1, starting transfers between devices, exchange_x(): return (lax.ppermute(across, GX, [(i, i ^ 1) for i in range(count)]), along)  3.3 us
    ppermute x1, starting transfers between devices, exchange_z(): lax.ppermute(along, GZ, [(i, (i + 1 if i % 2 else i - 1) % count) for i i...  3.11 us
    ppermute x1, starting transfers between devices, exchange_x(): along = lax.ppermute(along, GX + GZ, pairs)  3.08 us
    pallas_call x1, Pallas kernels, local(): pl.pallas_call(interior, out_shape=(shape(19, X, Z, Y), shape(8, PANELS),...  2.48 us
    pallas_call x1, Pallas kernels, local(): pl.pallas_call(pack_z, out_shape=(shape(ZROWS, Y), shape(ZROWS, Y), shape...  2.2 us
    ppermute x1, starting transfers between devices, exchange_z(): return (lax.ppermute(across, GZ, [(i, i ^ 1) for i in range(count)]), along)  2.03 us
  transfers between devices with their start and end apart: 4, of which 0 were waited for; matrix products, arithmetic and copies ran while one was open for 0% of the time, Pallas kernels for 11%

profile of v5, /device:TPU:1, one launch (start us, length us, event | category | flops | bytes accessed | tf_op | source)
XLA Modules:
  0.0 49.4 jit_solution(3223322426508679575)
XLA Ops:
  0.6 0.0 copy-start
  0.6 0.0 copy-start.4
  0.7 0.0 copy-start.2
  0.7 2.2 %shard_map.85 = (f32[152,256]{1,0:T(8,128)S(1)}, f32[152,256]{1,0:T(8,128)S(1)}, f32[152,256]{1,0:T(8,128)S(1)}, f32[152,256]{1,0:T(8,128)S(1)}, f32[128,256]{1,0:T(8,128)S(1)}) custom-call(bf16[19,16,8,256]{3,2,1,0:T(8,128)(2,1)} %stored.1, f32[19,16,8,256]{3,2,1,0:T(8,128)} %adj.3), custom_call_target="tpu_custom_call" | custom-call | flops 5000000 | bytes 4000000 | tf_op jit(solution)/shard_map/pallas_call | solution.py:695
  2.9 0.0 copy-start.3
  2.9 3.1 %collective-permute-start = (f32[152,256]{1,0:T(8,128)S(1)}, f32[152,256]{1,0:T(8,128)S(1)}, u32[]{:S(2)}, u32[]{:S(2)}) collective-permute-start(f32[152,256]{1,0:T(8,128)S(1)} %get-tuple-element.31), channel_id=1, source_target_pairs={{0,15},{1,2},{2,1},{3,4},{4,3},{5,6},{6,5},{7,8},{8,7},{9,10},{10,... | collective-permute-start | bytes 466952 | tf_op jit(solution)/shard_map/ppermute | solution.py:651
  6.0 2.0 %collective-permute-start.1 = (f32[152,256]{1,0:T(8,128)S(1)}, f32[152,256]{1,0:T(8,128)S(1)}, u32[]{:S(2)}, u32[]{:S(2)}) collective-permute-start(f32[152,256]{1,0:T(8,128)S(1)} %get-tuple-element.32), channel_id=1, source_target_pairs={{0,1},{1,0},{2,3},{3,2},{4,5},{5,4},{6,7},{7,6},{8,9},{9,8},{10,11... | collective-permute-start | bytes 466952 | tf_op jit(solution)/shard_map/ppermute | solution.py:654
  8.7 0.0 copy-done
  8.7 1.7 %shard_map.86 = (f32[9,2048]{1,0:T(8,128)S(1)}, bf16[256,2048]{1,0:T(8,128)(2,1)S(1)}, f32[3,8,2048]{2,1,0:T(8,128)S(1)}, f32[19,4,8,256]{3,2,1,0:T(8,128)S(1)}) custom-call(s32[1]{0:T(128)S(6)} %copy.11.count, f32[19,16,8,256]{3,2,1,0:T(8,128)S(1)} %copy-done, f32[128,256]{1,0:T(8,128)S(1)} %get-tuple-element.27.rho, s32[1,2048]{1,0:T(1,128)S(1)} %bitcast.2, ...), custom_call_target="tpu_custom_call" | custom-call | flops 800000000 | bytes 2000000 | tf_op jit(solution)/shard_map/pallas_call | solution.py:715
  10.4 0.0 copy-start.1
  10.5 0.0 collective-permute-done.along_in
  10.5 0.0 collective-permute-done.1.across_in
  10.5 0.2 shard_map.87
  10.6 3.1 %collective-permute-start.2 = (f32[88,256]{1,0:T(8,128)S(1)}, f32[88,256]{1,0:T(8,128)S(1)}, u32[]{:S(2)}, u32[]{:S(2)}) collective-permute-start(f32[88,256]{1,0:T(8,128)S(1)} %get-tuple-element.38), channel_id=1, source_target_pairs={{0,1},{1,0},{2,3},{3,2},{4,5},{5,4},{6,7},{7,6},{8,9},{9,8},{10,11... | collective-permute-start | bytes 270344 | tf_op jit(solution)/shard_map/ppermute | solution.py:667
  13.7 3.3 %collective-permute-start.3 = (f32[88,256]{1,0:T(8,128)S(1)}, f32[88,256]{1,0:T(8,128)S(1)}, u32[]{:S(2)}, u32[]{:S(2)}) collective-permute-start(f32[88,256]{1,0:T(8,128)S(1)} %get-tuple-element.39), channel_id=1, source_target_pairs={{0,16},{16,0},{32,48},{48,32},{64,80},{80,64},{96,112},{112,96},{1... | collective-permute-start | bytes 270344 | tf_op jit(solution)/shard_map/ppermute | solution.py:668
  17.0 0.0 copy-done.3
  17.0 1.0 %shard_map.88 = (f32[3,8,2048]{2,1,0:T(8,128)S(1)}, bf16[128,2048]{1,0:T(8,128)(2,1)S(1)}) custom-call(f32[152,256]{1,0:T(8,128)S(1)} %get-tuple-element.29.sent_low, f32[152,256]{1,0:T(8,128)S(1)} %get-tuple-element.30.sent_high, f32[152,256]{1,0:T(8,128)S(1)} %get-tuple-element.36.low, f32[152,256]{1,0:T(8,128)S(1)} %get-tuple-element.37.high, ...), custom_call_target="tpu_custom_call" | custom-call | flops 400000000 | bytes 2000000 | tf_op jit(solution)/shard_map/pallas_call | solution.py:736
  18.1 2.5 %shard_map.89 = (f32[19,16,8,256]{3,2,1,0:T(8,128)}, f32[8,128]{1,0:T(8,128)S(1)}, f32[2,19,8,256]{3,2,1,0:T(8,128)S(1)}) custom-call(bf16[19,16,8,256]{3,2,1,0:T(8,128)(2,1)S(1)} %copy-done.1, f32[19,16,8,256]{3,2,1,0:T(8,128)S(1)} %copy-done, f32[152,256]{1,0:T(8,128)S(1)} %get-tuple-element.36.low, f32[152,256]{1,0:T(8,128)S(1)} %get-tuple-element.37.high, ...), custom_call_target="tpu_custom_call" | custom-call | flops 10000000 | bytes 7000000 | tf_op jit(solution)/shard_map/pallas_call | solution.py:743
  20.6 0.0 collective-permute-done.2.along
  20.6 0.0 collective-permute-done.3.across
  20.6 0.8 %shard_map.90 = (f32[3,2048]{1,0:T(4,128)S(1)}, f32[16,1,384]{2,1,0:T(1,128)S(1)}, f32[88,256]{1,0:T(8,128)S(1)}, f32[88,256]{1,0:T(8,128)S(1)}) custom-call(f32[128,256]{1,0:T(8,128)S(1)} %get-tuple-element.27.rho, f32[88,256]{1,0:T(8,128)S(1)} %get-tuple-element.34.sent_left, f32[88,256]{1,0:T(8,128)S(1)} %get-tuple-element.35.sent_right, ...), custom_call_target="tpu_custom_call" | custom-call | flops 300000000 | bytes 2000000 | tf_op jit(solution)/shard_map/pallas_call | solution.py:754
  21.4 15.3 %all_to_all.10 = f32[16,1,384]{2,1,0:T(1,128)S(1)} all-to-all(f32[16,1,384]{2,1,0:T(1,128)S(1)} %get-tuple-element.45), channel_id=1, replica_groups=mesh['y'=4,'zh'=4,'x'=4,'zl'=2,'core'=2] {'core','zh','zl'}, dimensions={0} | all-to-all | bytes 49152 | tf_op jit(solution)/shard_map/all_to_all | solution.py:769
  36.8 11.7 %all_to_all.11.parts = f32[16,1,384]{2,1,0:T(1,128)S(1)} all-to-all(f32[16,1,384]{2,1,0:T(1,128)S(1)} %broadcast_in_dim.2), channel_id=1, replica_groups=mesh['y'=4,'zh'=4,'x'=4,'zl'=2,'core'=2] {'y','x'}, dimensions={0} | all-to-all | bytes 49152 | tf_op jit(solution)/shard_map/all_to_all | solution.py:770
  48.5 0.9 %shard_map.91 = (f32[19,16,8,256]{3,2,1,0:T(8,128)}, f32[3,2048]{1,0:T(4,128)}, f32[3,128]{1,0:T(4,128)}) custom-call(f32[16,1,384]{2,1,0:T(1,128)S(1)} %all_to_all.11.parts, f32[3,2048]{1,0:T(4,128)S(1)} %get-tuple-element.46.grad, f32[19,4,8,256]{3,2,1,0:T(8,128)S(1)} %get-tuple-element.28.near, ...), custom_call_target="tpu_custom_call", output_to_operand_aliasing={{0}: (8, {})} | custom-call | flops 1000000 | bytes 2000000 | tf_op jit(solution)/shard_map/pallas_call | solution.py:771
  (5 shorter events, 0.1 us)
Async XLA Ops:
  0.6 8.1 %copy-start = (f32[19,16,8,256]{3,2,1,0:T(8,128)S(1)}, f32[19,16,8,256]{3,2,1,0:T(8,128)}, u32[]{:S(2)}) copy-start(f32[19,16,8,256]{3,2,1,0:T(8,128)} %adj.3) | copy-start | bytes 7471108
  0.6 8.1 %copy-start.4 = (f32[9,2048]{1,0:T(8,128)S(1)}, f32[9,2048]{1,0:T(8,128)}, u32[]{:S(2)}) copy-start(f32[9,2048]{1,0:T(8,128)} %weight.1) | copy-start | bytes 221188
  0.7 8.1 %copy-start.2 = (s32[2048]{0:T(1024)S(1)}, s32[2048]{0:T(1024)}, u32[]{:S(2)}) copy-start(s32[2048]{0:T(1024)} %param.8) | copy-start | bytes 24580
  2.9 14.2 %copy-start.3 = (s32[2048]{0:T(1024)S(1)}, s32[2048]{0:T(1024)}, u32[]{:S(2)}) copy-start(s32[2048]{0:T(1024)} %param.10) | copy-start | bytes 24580
  2.9 7.6 %collective-permute-start = (f32[152,256]{1,0:T(8,128)S(1)}, f32[152,256]{1,0:T(8,128)S(1)}, u32[]{:S(2)}, u32[]{:S(2)}) collective-permute-start(f32[152,256]{1,0:T(8,128)S(1)} %get-tuple-element.31), channel_id=1, source_target_pairs={{0,15},{1,2},{2,1},{3,4},{4,3},{5,6},{6,5},{7,8},{8,7},{9,10},{10,... | collective-permute-start | bytes 466952 | tf_op jit(solution)/shard_map/ppermute | solution.py:651
  6.0 4.5 %collective-permute-start.1 = (f32[152,256]{1,0:T(8,128)S(1)}, f32[152,256]{1,0:T(8,128)S(1)}, u32[]{:S(2)}, u32[]{:S(2)}) collective-permute-start(f32[152,256]{1,0:T(8,128)S(1)} %get-tuple-element.32), channel_id=1, source_target_pairs={{0,1},{1,0},{2,3},{3,2},{4,5},{5,4},{6,7},{7,6},{8,9},{9,8},{10,11... | collective-permute-start | bytes 466952 | tf_op jit(solution)/shard_map/ppermute | solution.py:654
  10.4 7.6 %copy-start.1 = (bf16[19,16,8,256]{3,2,1,0:T(8,128)(2,1)S(1)}, bf16[19,16,8,256]{3,2,1,0:T(8,128)(2,1)}, u32[]{:S(2)}) copy-start(bf16[19,16,8,256]{3,2,1,0:T(8,128)(2,1)} %stored.1) | copy-start | bytes 3735556
  10.6 9.9 %collective-permute-start.2 = (f32[88,256]{1,0:T(8,128)S(1)}, f32[88,256]{1,0:T(8,128)S(1)}, u32[]{:S(2)}, u32[]{:S(2)}) collective-permute-start(f32[88,256]{1,0:T(8,128)S(1)} %get-tuple-element.38), channel_id=1, source_target_pairs={{0,1},{1,0},{2,3},{3,2},{4,5},{5,4},{6,7},{7,6},{8,9},{9,8},{10,11... | collective-permute-start | bytes 270344 | tf_op jit(solution)/shard_map/ppermute | solution.py:667
  13.7 6.9 %collective-permute-start.3 = (f32[88,256]{1,0:T(8,128)S(1)}, f32[88,256]{1,0:T(8,128)S(1)}, u32[]{:S(2)}, u32[]{:S(2)}) collective-permute-start(f32[88,256]{1,0:T(8,128)S(1)} %get-tuple-element.39), channel_id=1, source_target_pairs={{0,16},{16,0},{32,48},{48,32},{64,80},{80,64},{96,112},{112,96},{1... | collective-permute-start | bytes 270344 | tf_op jit(solution)/shard_map/ppermute | solution.py:668

commit v6 on v5

--- a/solution.py
+++ b/solution.py
@@ -50,6 +50,7 @@
 CHUNK = 256
 UNROLL_C = 8
 GROUPS = 4
+PARTS = 2
 STEP = X // GROUPS
 NEAR = (0, 1, X - 2, X - 1)
 
@@ -142,8 +143,8 @@
 
 def pack_z(stored_in, adj_in, to_low, to_high, across, along, rho_out, stored, adj, sems):
     copies = []
-    for n in range(GROUPS):
-        part = pl.ds(n * STEP, STEP)
+    for n in range(PARTS):
+        part = pl.ds(n * (X // PARTS), (X // PARTS))
         group = []
         for k, first in enumerate((0, Z - 2)):
             at = (pl.ds(1, 18), part, pl.ds(first, 2))
@@ -171,13 +172,13 @@
             to_low[pl.ds(Z_MOM + d * X + x, 1), :] = mom[0:1]
             to_high[pl.ds(Z_MOM + d * X + x, 1), :] = mom[Z - 1 : Z]
 
-    for n in range(GROUPS):
+    for n in range(PARTS):
         for copy in copies[n]:
             copy.wait()
-        first, last = n * STEP, (n + 1) * STEP
+        first, last = n * (X // PARTS), (n + 1) * (X // PARTS)
         for x in range(first, last):
             density(x)
-        for x in range(max(first - 1, 0), last if n == GROUPS - 1 else last - 1):
+        for x in range(max(first - 1, 0), last if n == PARTS - 1 else last - 1):
             moments(x)
     spill = [column(adj, -1), column(adj, X)]
     zero = jnp.zeros((1, Y), jnp.float32)
@@ -470,39 +471,74 @@
     return [jnp.broadcast_to(weight[s : s + 1, where], (8, CHUNK)) for s in range(9)]
 
 
-def stage_a(count, adj, rho, cell, weight, live_weight, hot, acc, near, split):
+def stage_a(count, adj_in, rho, cell, weight, live_weight, hot, acc, near, adj, split, sems):
     rows = X * Z
-    for k, x in enumerate(NEAR):
-        near[:, k] = adj[:, x]
-    for x in range(0, X, 2):
-        scale = 3.0 * rho[x * Z : (x + 2) * Z, :]
-        first, second = column(adj, x), column(adj, x + 1)
-        for d in range(3):
-            put(split, d * rows + x * Z, scale * jnp.concatenate([first[d], second[d]]))
+    copies = []
+    for n in range(GROUPS):
+        part = pl.ds(n * STEP, STEP)
+        copy = pltpu.make_async_copy(adj_in.at[:, part], adj.at[:, part], sems.at[n])
+        copy.start()
+        copies.append(copy)
     lanes = lax.broadcasted_iota(jnp.int32, (9, CHUNK), 1)
 
-    def chunk(c, carry):
+    def prepare(c, carry):
         where = chunk_of(c)
         live = (lanes + c * CHUNK) < count[0]
         live_weight[:, where] = jnp.where(live, weight[:, where], 0.0)
-        w = weights_of(live_weight, where)
         y_of = jnp.broadcast_to(cell[:, where] & (Y - 1), (Y, CHUNK))
         one = jnp.where(lax.broadcasted_iota(jnp.int32, (Y, CHUNK), 0) == y_of, 1.0, 0.0)
-        one = one.astype(jnp.bfloat16)
-        hot[:, where] = one
+        hot[:, where] = one.astype(jnp.bfloat16)
+        return carry
+
+    lax.fori_loop(0, cell.shape[1] // CHUNK, prepare, 0, unroll=2)
+    done = 0
+    for n in range(GROUPS):
+        copies[n].wait()
+        ready = X if n == GROUPS - 1 else (n + 1) * STEP - 2
+        for x in range(done, ready, 2):
+            scale = 3.0 * rho[x * Z : (x + 2) * Z, :]
+            first, second = column(adj, x), column(adj, x + 1)
+            for d in range(3):
+                put(split, d * rows + x * Z, scale * jnp.concatenate([first[d], second[d]]))
+        done = ready
+    for k, x in enumerate(NEAR):
+        near[:, k] = adj[:, x]
+
+    def chunk(c, carry):
+        where = chunk_of(c)
+        w = weights_of(live_weight, where)
         bx, bz = bases(cell, where)
         dz = sublanes() - bz
         three = [pick(dz, w[3 * a : 3 * a + 3]) for a in range(3)]
         factors = [pick(x - bx, three) for x in range(X)]
-        for d, tile in enumerate(gathered(split, rows, one, factors)):
+        for d, tile in enumerate(gathered(split, rows, hot[:, where], factors)):
             acc[d, :, where] = tile
         return carry
 
     lax.fori_loop(0, cell.shape[1] // CHUNK, chunk, 0, unroll=4)
 
 
+def shares(sub, bx, bz, w):
+    kind = sub & 3
+    corner_x = jnp.where(kind == 0, -1, jnp.where(kind == 1, X, jnp.where(kind == 2, 0, X - 1)))
+    dz = sub - bz
+    at_low, at_high = (sub < 4) & (bz == 0), (sub >= 4) & (bz == Z - 1)
+    inner, corner = [], []
+    for a in range(3):
+        wa = w[3 * a : 3 * a + 3]
+        inner.append(pick(dz, wa))
+        corner.append(jnp.where(at_low, wa[0], jnp.where(at_high, wa[2], 0.0)))
+    return [
+        jnp.where(bx == 0, inner[0], 0.0),
+        jnp.where(bx == X - 1, inner[2], 0.0),
+        jnp.where(bx == 0, inner[1], jnp.where(bx == 1, inner[0], 0.0)),
+        jnp.where(bx == X - 1, inner[1], jnp.where(bx == X - 2, inner[2], 0.0)),
+        pick(corner_x - bx, corner),
+    ]
+
+
 def stage_b(
-    sent_low, sent_high, low, high, cell, panel, weight, hot, acc_in, acc, which, split
+    sent_low, sent_high, low, high, cell, panel, weight, hot, acc_in, acc, which, share, split
 ):
     low_on, high_on, _, _ = ends()
     rows = 4 * X
@@ -526,6 +562,8 @@
         w = weights_of(weight, where)
         bx, bz = bases(cell, where)
         sub = sublanes()
+        for t, tile in enumerate(shares(sub, bx, bz, w)):
+            share[8 * t : 8 * t + 8, where] = tile
         dx = [sub - bx, sub + 8 - bx]
         first, last, under, over = [], [], [], []
         for a in range(3):
@@ -539,7 +577,8 @@
             acc[d, :, where] = acc_in[d, :, where] + tile
         panels = jnp.broadcast_to(panel[:, where], (PANELS, CHUNK))
         match = lax.broadcasted_iota(jnp.int32, (PANELS, CHUNK), 0) == panels
-        which[:, where] = jnp.where(match, 1.0, 0.0).astype(jnp.bfloat16)
+        rows_at = pl.ds(pl.multiple_of(c * CHUNK, CHUNK), CHUNK)
+        which[rows_at, :] = jnp.where(match, 1.0, 0.0).T.astype(jnp.bfloat16)
         return carry
 
     lax.fori_loop(0, cell.shape[1] // CHUNK, chunk, 0, unroll=4)
@@ -553,8 +592,7 @@
     high,
     along,
     across,
-    cell,
-    weight,
+    share,
     hot,
     which,
     acc_in,
@@ -603,29 +641,9 @@
         for t in range(0, 6, 2):
             put(split, d * rows + t * 8, jnp.concatenate(tiles[t : t + 2]))
 
-    sub = sublanes()
-    kind = sub & 3
-    corner_x = jnp.where(kind == 0, -1, jnp.where(kind == 1, X, jnp.where(kind == 2, 0, X - 1)))
-    bottom = sub < 4
-
     def chunk(c, carry):
         where = chunk_of(c)
-        w = weights_of(weight, where)
-        bx, bz = bases(cell, where)
-        dz = sub - bz
-        at_low, at_high = bottom & (bz == 0), (sub >= 4) & (bz == Z - 1)
-        inner, corner = [], []
-        for a in range(3):
-            wa = w[3 * a : 3 * a + 3]
-            inner.append(pick(dz, wa))
-            corner.append(jnp.where(at_low, wa[0], jnp.where(at_high, wa[2], 0.0)))
-        factors = [
-            jnp.where(bx == 0, inner[0], 0.0),
-            jnp.where(bx == X - 1, inner[2], 0.0),
-            jnp.where(bx == 0, inner[1], jnp.where(bx == 1, inner[0], 0.0)),
-            jnp.where(bx == X - 1, inner[1], jnp.where(bx == X - 2, inner[2], 0.0)),
-            pick(corner_x - bx, corner),
-        ]
+        factors = [share[8 * t : 8 * t + 8, where] for t in range(5)]
         sums = []
         for d, tile in enumerate(gathered(split, rows, hot[:, where], factors)):
             sums.append(jnp.sum(acc_in[d, :, where] + tile, axis=0, keepdims=True))
@@ -636,10 +654,8 @@
         totals[:, where] = jnp.concatenate([top, rest])
         return carry
 
-    lax.fori_loop(0, cell.shape[1] // CHUNK, chunk, 0, unroll=UNROLL_C)
-    total = lax.dot_general(
-        totals[...], which[...], (((1,), (1,)), ((), ())), preferred_element_type=jnp.float32
-    )
+    lax.fori_loop(0, hot.shape[1] // CHUNK, chunk, 0, unroll=UNROLL_C)
+    total = jnp.dot(totals[...], which[...], preferred_element_type=jnp.float32)
     result = total[0:3] + total[8:11]
     result = jnp.concatenate([result[0:1], result[1:2], result[2:3]], axis=1)
     for n in range(partial.shape[0]):
@@ -669,6 +685,7 @@
 
 
 PARAMS = pltpu.CompilerParams(vmem_limit_bytes=48 * 1024 * 1024)
+MID = pltpu.CompilerParams(vmem_limit_bytes=50 * 1024 * 1024)
 FIRST_BIG = pltpu.CompilerParams(vmem_limit_bytes=53 * 1024 * 1024)
 BIG = pltpu.CompilerParams(vmem_limit_bytes=52 * 1024 * 1024)
 
@@ -706,7 +723,7 @@
         scratch_shapes=[
             pltpu.VMEM(stored.shape, stored.dtype),
             pltpu.VMEM(adj.shape, adj.dtype),
-            pltpu.SemaphoreType.DMA((3, GROUPS)),
+            pltpu.SemaphoreType.DMA((3, PARTS)),
         ],
         compiler_params=FIRST_BIG,
         cost_estimate=cost(5_000_000, 4_000_000),
@@ -720,9 +737,13 @@
             shape(3, 8, slots),
             shape(19, len(NEAR), Z, Y),
         ),
-        in_specs=[pl.BlockSpec(memory_space=pltpu.SMEM)] + [whole] * 4,
-        scratch_shapes=[pltpu.VMEM((6 * X * Z, Y), jnp.bfloat16)],
-        compiler_params=PARAMS,
+        in_specs=[pl.BlockSpec(memory_space=pltpu.SMEM)] + [hbm] + [whole] * 3,
+        scratch_shapes=[
+            pltpu.VMEM(adj.shape, adj.dtype),
+            pltpu.VMEM((6 * X * Z, Y), jnp.bfloat16),
+            pltpu.SemaphoreType.DMA((GROUPS,)),
+        ],
+        compiler_params=MID,
         cost_estimate=cost(800_000_000, 2_000_000),
     )(marker_count, adj, rho, cell, marker_weight)
     to_left, to_right, across, along, low, high = pl.pallas_call(
@@ -733,9 +754,13 @@
         cost_estimate=cost(1_000_000, 2_000_000),
     )(near, rho, to_low, to_high, along, across, acc)
     across, along = exchange_x(across, along)
-    acc, which = pl.pallas_call(
+    acc, which, share = pl.pallas_call(
         stage_b,
-        out_shape=(shape(3, 8, slots), jax.ShapeDtypeStruct((PANELS, slots), jnp.bfloat16)),
+        out_shape=(
+            shape(3, 8, slots),
+            jax.ShapeDtypeStruct((slots, PANELS), jnp.bfloat16),
+            shape(40, slots),
+        ),
         scratch_shapes=[pltpu.VMEM((24 * X, Y), jnp.bfloat16)],
         compiler_params=PARAMS,
         cost_estimate=cost(400_000_000, 2_000_000),
@@ -765,7 +790,7 @@
         ],
         compiler_params=PARAMS,
         cost_estimate=cost(300_000_000, 2_000_000),
-    )(rho, to_left, to_right, low, high, along, across, cell, weight, hot, which, acc, token)
+    )(rho, to_left, to_right, low, high, along, across, share, hot, which, acc, token)
     partial = summed(lax.all_to_all(partial, FIRST, 0, 0), lax.axis_size(SECOND))
     partial = lax.all_to_all(partial, SECOND, 0, 0)
     return pl.pallas_call(

time: 49.6 us -> 49.4 us (level)
  blocking collectives: 27 us -> 25.2 us
  Pallas kernels: 9.33 us -> 10.5 us
    all_to_all x1, blocking collectives: 15.3 us -> 13.3 us  [local(): lax.all_to_all(partial, FIRST, 0, 0)]
    ppermute x1, starting transfers between devices: 3.3 us -> 4.8 us  [exchange_x(): return (lax.ppermute(across, GX, [(i, i ^ 1) for i in range(count)]), along)]
    ppermute x1, starting transfers between devices: 3.08 us -> 1.58 us  [exchange_x(): along = lax.ppermute(along, GX + GZ, pairs)]
    pallas_call x1, Pallas kernels: 1.73 us -> 3.22 us  [local(): pl.pallas_call(stage_a, out_shape=(shape(9, slots), jax.ShapeDtypeStruct(...]
  transfers between devices with their start and end apart: 4 -> 4, of which waited for: 0 -> 1; matrix products, arithmetic and copies ran while one was open for 0% -> 0% of each run, Pallas kernels for 11% -> 14%
where the time goes in v6:
time: 49.4 us; the launch traced here: 49.2 us
  blocking collectives  25.2 us (51%)
  starting transfers between devices  11.5 us (23%)
  Pallas kernels  10.5 us (21%)
  between operations  1.43 us (3%)
    all_to_all x1, blocking collectives, local(): lax.all_to_all(partial, FIRST, 0, 0)  13.3 us
    all_to_all x1, blocking collectives, local(): partial = lax.all_to_all(partial, SECOND, 0, 0)  11.9 us
    ppermute x1, starting transfers between devices, exchange_x(): return (lax.ppermute(across, GX, [(i, i ^ 1) for i in range(count)]), along)  4.8 us
    pallas_call x1, Pallas kernels, local(): pl.pallas_call(stage_a, out_shape=(shape(9, slots), jax.ShapeDtypeStruct(...  3.22 us
    ppermute x1, starting transfers between devices, exchange_z(): lax.ppermute(along, GZ, [(i, (i + 1 if i % 2 else i - 1) % count) for i i...  3.11 us
    pallas_call x1, Pallas kernels, local(): pl.pallas_call(interior, out_shape=(shape(19, X, Z, Y), shape(8, PANELS),...  2.48 us
    pallas_call x1, Pallas kernels, local(): pl.pallas_call(pack_z, out_shape=(shape(ZROWS, Y), shape(ZROWS, Y), shape...  2.08 us
    ppermute x1, starting transfers between devices, exchange_z(): return (lax.ppermute(across, GZ, [(i, i ^ 1) for i in range(count)]), along)  2.03 us
  transfers between devices with their start and end apart: 4, of which 1 were waited for; matrix products, arithmetic and copies ran while one was open for 0% of the time, Pallas kernels for 14%

profile of v6, /device:TPU:1, one launch (start us, length us, event | category | flops | bytes accessed | tf_op | source)
XLA Modules:
  0.0 49.2 jit_solution(5235361331573848130)
XLA Ops:
  0.6 0.0 copy-start.4
  0.6 0.0 copy-start.2
  0.7 2.1 %shard_map.85 = (f32[152,256]{1,0:T(8,128)S(1)}, f32[152,256]{1,0:T(8,128)S(1)}, f32[152,256]{1,0:T(8,128)S(1)}, f32[152,256]{1,0:T(8,128)S(1)}, f32[128,256]{1,0:T(8,128)S(1)}) custom-call(bf16[19,16,8,256]{3,2,1,0:T(8,128)(2,1)} %stored.1, f32[19,16,8,256]{3,2,1,0:T(8,128)} %adj.1), custom_call_target="tpu_custom_call" | custom-call | flops 5000000 | bytes 4000000 | tf_op jit(solution)/shard_map/pallas_call | solution.py:712
  2.7 0.0 copy-start.3
  2.8 3.1 %collective-permute-start = (f32[152,256]{1,0:T(8,128)S(1)}, f32[152,256]{1,0:T(8,128)S(1)}, u32[]{:S(2)}, u32[]{:S(2)}) collective-permute-start(f32[152,256]{1,0:T(8,128)S(1)} %get-tuple-element.32), channel_id=1, source_target_pairs={{0,15},{1,2},{2,1},{3,4},{4,3},{5,6},{6,5},{7,8},{8,7},{9,10},{10,... | collective-permute-start | bytes 466952 | tf_op jit(solution)/shard_map/ppermute | solution.py:667
  5.9 2.0 %collective-permute-start.1 = (f32[152,256]{1,0:T(8,128)S(1)}, f32[152,256]{1,0:T(8,128)S(1)}, u32[]{:S(2)}, u32[]{:S(2)}) collective-permute-start(f32[152,256]{1,0:T(8,128)S(1)} %get-tuple-element.33), channel_id=1, source_target_pairs={{0,1},{1,0},{2,3},{3,2},{4,5},{5,4},{6,7},{7,6},{8,9},{9,8},{10,11... | collective-permute-start | bytes 466952 | tf_op jit(solution)/shard_map/ppermute | solution.py:670
  8.5 0.0 copy-done.4
  8.6 0.0 copy-start.1
  8.6 3.2 %shard_map.86 = (f32[9,2048]{1,0:T(8,128)S(1)}, bf16[256,2048]{1,0:T(8,128)(2,1)S(1)}, f32[3,8,2048]{2,1,0:T(8,128)S(1)}, f32[19,4,8,256]{3,2,1,0:T(8,128)S(1)}) custom-call(s32[1]{0:T(128)S(6)} %copy.11.count, f32[19,16,8,256]{3,2,1,0:T(8,128)} %adj.1, f32[128,256]{1,0:T(8,128)S(1)} %get-tuple-element.28.rho, s32[1,2048]{1,0:T(1,128)S(1)} %bitcast.2, ...), custom_call_target="tpu_custom_call" | custom-call | flops 800000000 | bytes 2000000 | tf_op jit(solution)/shard_map/pallas_call | solution.py:732
  11.8 0.0 copy-start
  11.8 0.0 collective-permute-done.along_in
  11.8 0.0 collective-permute-done.1.across_in
  11.8 0.2 shard_map.87
  12.0 1.6 %collective-permute-start.2 = (f32[88,256]{1,0:T(8,128)S(1)}, f32[88,256]{1,0:T(8,128)S(1)}, u32[]{:S(2)}, u32[]{:S(2)}) collective-permute-start(f32[88,256]{1,0:T(8,128)S(1)} %get-tuple-element.39), channel_id=1, source_target_pairs={{0,1},{1,0},{2,3},{3,2},{4,5},{5,4},{6,7},{7,6},{8,9},{9,8},{10,11... | collective-permute-start | bytes 270344 | tf_op jit(solution)/shard_map/ppermute | solution.py:683
  13.6 4.8 %collective-permute-start.3 = (f32[88,256]{1,0:T(8,128)S(1)}, f32[88,256]{1,0:T(8,128)S(1)}, u32[]{:S(2)}, u32[]{:S(2)}) collective-permute-start(f32[88,256]{1,0:T(8,128)S(1)} %get-tuple-element.40), channel_id=1, source_target_pairs={{0,16},{16,0},{32,48},{48,32},{64,80},{80,64},{96,112},{112,96},{1... | collective-permute-start | bytes 270344 | tf_op jit(solution)/shard_map/ppermute | solution.py:684
  18.4 0.0 copy-done.3
  18.4 1.0 %shard_map.88 = (f32[3,8,2048]{2,1,0:T(8,128)S(1)}, bf16[2048,128]{1,0:T(8,128)(2,1)S(1)}, f32[40,2048]{1,0:T(8,128)S(1)}) custom-call(f32[152,256]{1,0:T(8,128)S(1)} %get-tuple-element.30.sent_low, f32[152,256]{1,0:T(8,128)S(1)} %get-tuple-element.31.sent_high, f32[152,256]{1,0:T(8,128)S(1)} %get-tuple-element.37.low, ...), custom_call_target="tpu_custom_call" | custom-call | flops 400000000 | bytes 2000000 | tf_op jit(solution)/shard_map/pallas_call | solution.py:757
  19.4 2.5 %shard_map.89 = (f32[19,16,8,256]{3,2,1,0:T(8,128)}, f32[8,128]{1,0:T(8,128)S(1)}, f32[2,19,8,256]{3,2,1,0:T(8,128)S(1)}) custom-call(bf16[19,16,8,256]{3,2,1,0:T(8,128)(2,1)S(1)} %copy-done.1, f32[19,16,8,256]{3,2,1,0:T(8,128)S(1)} %copy-done, f32[152,256]{1,0:T(8,128)S(1)} %get-tuple-element.37.low, f32[152,256]{1,0:T(8,128)S(1)} %get-tuple-element.38.high, ...), custom_call_target="tpu_custom_call" | custom-call | flops 10000000 | bytes 7000000 | tf_op jit(solution)/shard_map/pallas_call | solution.py:768
  21.9 0.0 collective-permute-done.2.along
  21.9 0.4 collective-permute-done.3.across
  22.3 0.7 %shard_map.90 = (f32[3,2048]{1,0:T(4,128)S(1)}, f32[16,1,384]{2,1,0:T(1,128)S(1)}, f32[88,256]{1,0:T(8,128)S(1)}, f32[88,256]{1,0:T(8,128)S(1)}) custom-call(f32[128,256]{1,0:T(8,128)S(1)} %get-tuple-element.28.rho, f32[88,256]{1,0:T(8,128)S(1)} %get-tuple-element.35.sent_left, f32[88,256]{1,0:T(8,128)S(1)} %get-tuple-element.36.sent_right, ...), custom_call_target="tpu_custom_call" | custom-call | flops 300000000 | bytes 2000000 | tf_op jit(solution)/shard_map/pallas_call | solution.py:779
  23.0 13.3 %all_to_all.10 = f32[16,1,384]{2,1,0:T(1,128)S(1)} all-to-all(f32[16,1,384]{2,1,0:T(1,128)S(1)} %get-tuple-element.47), channel_id=1, replica_groups=mesh['y'=4,'zh'=4,'x'=4,'zl'=2,'core'=2] {'core','zh','zl'}, dimensions={0} | all-to-all | bytes 49152 | tf_op jit(solution)/shard_map/all_to_all | solution.py:794
  36.3 11.9 %all_to_all.11.parts = f32[16,1,384]{2,1,0:T(1,128)S(1)} all-to-all(f32[16,1,384]{2,1,0:T(1,128)S(1)} %broadcast_in_dim.2), channel_id=1, replica_groups=mesh['y'=4,'zh'=4,'x'=4,'zl'=2,'core'=2] {'y','x'}, dimensions={0} | all-to-all | bytes 49152 | tf_op jit(solution)/shard_map/all_to_all | solution.py:795
  48.2 0.9 %shard_map.91 = (f32[19,16,8,256]{3,2,1,0:T(8,128)}, f32[3,2048]{1,0:T(4,128)}, f32[3,128]{1,0:T(4,128)}) custom-call(f32[16,1,384]{2,1,0:T(1,128)S(1)} %all_to_all.11.parts, f32[3,2048]{1,0:T(4,128)S(1)} %get-tuple-element.48.grad, f32[19,4,8,256]{3,2,1,0:T(8,128)S(1)} %get-tuple-element.29.near, ...), custom_call_target="tpu_custom_call", output_to_operand_aliasing={{0}: (8, {})} | custom-call | flops 1000000 | bytes 2000000 | tf_op jit(solution)/shard_map/pallas_call | solution.py:796
  (5 shorter events, 0.1 us)
Async XLA Ops:
  0.6 7.9 %copy-start.4 = (f32[9,2048]{1,0:T(8,128)S(1)}, f32[9,2048]{1,0:T(8,128)}, u32[]{:S(2)}) copy-start(f32[9,2048]{1,0:T(8,128)} %weight.1) | copy-start | bytes 221188
  0.6 7.9 %copy-start.2 = (s32[2048]{0:T(1024)S(1)}, s32[2048]{0:T(1024)}, u32[]{:S(2)}) copy-start(s32[2048]{0:T(1024)} %param.8) | copy-start | bytes 24580
  2.7 15.6 %copy-start.3 = (s32[2048]{0:T(1024)S(1)}, s32[2048]{0:T(1024)}, u32[]{:S(2)}) copy-start(s32[2048]{0:T(1024)} %param.10) | copy-start | bytes 24580
  2.8 9.1 %collective-permute-start = (f32[152,256]{1,0:T(8,128)S(1)}, f32[152,256]{1,0:T(8,128)S(1)}, u32[]{:S(2)}, u32[]{:S(2)}) collective-permute-start(f32[152,256]{1,0:T(8,128)S(1)} %get-tuple-element.32), channel_id=1, source_target_pairs={{0,15},{1,2},{2,1},{3,4},{4,3},{5,6},{6,5},{7,8},{8,7},{9,10},{10,... | collective-permute-start | bytes 466952 | tf_op jit(solution)/shard_map/ppermute | solution.py:667
  5.9 6.0 %collective-permute-start.1 = (f32[152,256]{1,0:T(8,128)S(1)}, f32[152,256]{1,0:T(8,128)S(1)}, u32[]{:S(2)}, u32[]{:S(2)}) collective-permute-start(f32[152,256]{1,0:T(8,128)S(1)} %get-tuple-element.33), channel_id=1, source_target_pairs={{0,1},{1,0},{2,3},{3,2},{4,5},{5,4},{6,7},{7,6},{8,9},{9,8},{10,11... | collective-permute-start | bytes 466952 | tf_op jit(solution)/shard_map/ppermute | solution.py:670
  8.6 10.8 %copy-start.1 = (bf16[19,16,8,256]{3,2,1,0:T(8,128)(2,1)S(1)}, bf16[19,16,8,256]{3,2,1,0:T(8,128)(2,1)}, u32[]{:S(2)}) copy-start(bf16[19,16,8,256]{3,2,1,0:T(8,128)(2,1)} %stored.1) | copy-start | bytes 3735556
  11.8 7.6 %copy-start = (f32[19,16,8,256]{3,2,1,0:T(8,128)S(1)}, f32[19,16,8,256]{3,2,1,0:T(8,128)}, u32[]{:S(2)}) copy-start(f32[19,16,8,256]{3,2,1,0:T(8,128)} %adj.1) | copy-start | bytes 7471108
  12.0 9.9 %collective-permute-start.2 = (f32[88,256]{1,0:T(8,128)S(1)}, f32[88,256]{1,0:T(8,128)S(1)}, u32[]{:S(2)}, u32[]{:S(2)}) collective-permute-start(f32[88,256]{1,0:T(8,128)S(1)} %get-tuple-element.39), channel_id=1, source_target_pairs={{0,1},{1,0},{2,3},{3,2},{4,5},{5,4},{6,7},{7,6},{8,9},{9,8},{10,11... | collective-permute-start | bytes 270344 | tf_op jit(solution)/shard_map/ppermute | solution.py:683
  13.6 8.7 %collective-permute-start.3 = (f32[88,256]{1,0:T(8,128)S(1)}, f32[88,256]{1,0:T(8,128)S(1)}, u32[]{:S(2)}, u32[]{:S(2)}) collective-permute-start(f32[88,256]{1,0:T(8,128)S(1)} %get-tuple-element.40), channel_id=1, source_target_pairs={{0,16},{16,0},{32,48},{48,32},{64,80},{80,64},{96,112},{112,96},{1... | collective-permute-start | bytes 270344 | tf_op jit(solution)/shard_map/ppermute | solution.py:684
